TPU v7x, 32 devices: a whole 2x2x4 slice. The times are simulated.
32 devices in a mesh: seq: 4 (over y, x), dp: 8 (over z, core).
Axes of the slice: x: 2, y: 2, z: 4, core: 2. Of those that a mesh axis runs over, the one named last changes fastest.
Arguments:
- latents: bfloat16 [16, 2048, 64], P('dp', 'seq'), may hold values from -6 to 6
- noise_draw: bfloat16 [16, 2048, 64], P('dp', 'seq'), may hold values from -6 to 6
- audio_len: int32 [16], P('dp'), may hold values from 512 to 2048
- bucket: int32 [16], P('dp'), may hold values from 0 to 999
- timing: int32 [16, 2], P('dp'), may hold values from 0 to 63
- prompt: bfloat16 [16, 128, 768], P('dp'), may hold values from -6 to 6
- prompt_len: int32 [16], P('dp'), may hold values from 4 to 128, as said below
- step_count: int32 [1], replicated, may hold values from 2 to 20
- edge_weight: float32 [896, 1536], P(None, ('seq', 'dp'))
- edge_first: float32 [896, 1536], P(None, ('seq', 'dp')), may hold values from -4.7683716e-07 to 4.7683716e-07
- edge_second: float32 [896, 1536], P(None, ('seq', 'dp')), may hold values from 4.1179106e-17 to 6.588657e-16
- attend_weight: float32 [1536, 4608], P(('seq', 'dp')), may hold values from -0.15625 to 0.15625
- attend_first: float32 [1536, 4608], P(('seq', 'dp')), may hold values from -4.7683716e-07 to 4.7683716e-07
- attend_second: float32 [1536, 4608], P(('seq', 'dp')), may hold values from 4.1179106e-17 to 6.588657e-16
- square_weight: float32 [4, 1536, 1536], P(None, ('seq', 'dp'))
- square_first: float32 [4, 1536, 1536], P(None, ('seq', 'dp')), may hold values from -1.1920929e-07 to 1.1920929e-07
- square_second: float32 [4, 1536, 1536], P(None, ('seq', 'dp')), may hold values from 3.2943285e-18 to 5.2709256e-17
- cross_weight: float32 [768, 3072], P(('seq', 'dp')), may hold values from -0.21875 to 0.21875
- cross_first: float32 [768, 3072], P(('seq', 'dp')), may hold values from -4.7683716e-07 to 4.7683716e-07
- cross_second: float32 [768, 3072], P(('seq', 'dp')), may hold values from 4.1179106e-17 to 6.588657e-16
- upward_weight: float32 [1536, 12288], P(('seq', 'dp')), may hold values from -0.15625 to 0.15625
- upward_first: float32 [1536, 12288], P(('seq', 'dp')), may hold values from -4.4703484e-08 to 4.4703484e-08
- upward_second: float32 [1536, 12288], P(('seq', 'dp')), may hold values from 3.2943285e-19 to 5.2709256e-18
- down_weight: float32 [6144, 1536], P(('seq', 'dp')), may hold values from -0.078125 to 0.078125
- down_first: float32 [6144, 1536], P(('seq', 'dp')), may hold values from -1.0430813e-07 to 1.0430813e-07
- down_second: float32 [6144, 1536], P(('seq', 'dp')), may hold values from 2.0589553e-18 to 3.2943285e-17
- gain_weight: float32 [4, 1536], P(None, ('seq', 'dp')), may hold values from 0.5 to 1.5
- gain_first: float32 [4, 1536], P(None, ('seq', 'dp')), may hold values from -1.9073486e-06 to 1.9073486e-06
- gain_second: float32 [4, 1536], P(None, ('seq', 'dp')), may hold values from 6.588657e-16 to 1.0541851e-14
Outputs:
- loss_value: float32 [], replicated
- grad_norm: float32 [], replicated
- new_edge: float32 [896, 1536], P(None, ('seq', 'dp'))
- first_edge: float32 [896, 1536], P(None, ('seq', 'dp'))
- second_edge: float32 [896, 1536], P(None, ('seq', 'dp'))
- new_attend: float32 [1536, 4608], P(('seq', 'dp'))
- first_attend: float32 [1536, 4608], P(('seq', 'dp'))
- second_attend: float32 [1536, 4608], P(('seq', 'dp'))
- new_square: float32 [4, 1536, 1536], P(None, ('seq', 'dp'))
- first_square: float32 [4, 1536, 1536], P(None, ('seq', 'dp'))
- second_square: float32 [4, 1536, 1536], P(None, ('seq', 'dp'))
- new_cross: float32 [768, 3072], P(('seq', 'dp'))
- first_cross: float32 [768, 3072], P(('seq', 'dp'))
- second_cross: float32 [768, 3072], P(('seq', 'dp'))
- new_upward: float32 [1536, 12288], P(('seq', 'dp'))
- first_upward: float32 [1536, 12288], P(('seq', 'dp'))
- second_upward: float32 [1536, 12288], P(('seq', 'dp'))
- new_down: float32 [6144, 1536], P(('seq', 'dp'))
- first_down: float32 [6144, 1536], P(('seq', 'dp'))
- second_down: float32 [6144, 1536], P(('seq', 'dp'))
- clip_gain: float32 [4, 1536], P(None, ('seq', 'dp'))
- first_gain: float32 [4, 1536], P(None, ('seq', 'dp'))
- second_gain: float32 [4, 1536], P(None, ('seq', 'dp'))
Inputs may be any that keep to these rules, and one draw needn't show every extreme that they name: `prompt_len`: valid prompt tokens of each clip, mostly short with a long tail; the first clip's prompt fills all 128 slots.
All inputs are finite; a program needn't handle non-finite values.
Results may differ from a plain program's by a relative error of at most 0.011.
Values may be sent and summed in bfloat16 or wider, within the bound.
A program may use at most 1 GiB of HBM per device.

v0:
```python
import math

import jax
import jax.numpy as jnp
from jax import lax
from jax.sharding import PartitionSpec as P

D = 1536
H = 24
HD = 64
FF = 6144
C = 64
TF = 256
PT = 128
NB = 1000


highest = lax.Precision.HIGHEST
clip_norm = 0.002
learn_rate = 0.1
weight_decay = 0.1
rot_width = 32


def layer_normalize(h, norm_gain):
    centered_input = h - jnp.mean(h, -1, keepdims=True)
    inverse_deviation = lax.rsqrt(
        jnp.mean(centered_input * centered_input, -1, keepdims=True) + 1e-05
    )
    standardized = centered_input * inverse_deviation
    return (standardized * norm_gain, standardized, inverse_deviation)


def norm_backward(incoming_gradient, standardized, inverse_deviation, norm_gain):
    scaled_gradient = incoming_gradient * norm_gain
    gain_gradient = jnp.sum(incoming_gradient * standardized, 0)
    d_in = inverse_deviation * (
        scaled_gradient
        - jnp.mean(scaled_gradient, -1, keepdims=True)
        - standardized * jnp.mean(scaled_gradient * standardized, -1, keepdims=True)
    )
    return (d_in, gain_gradient)


def plan(bucket):
    t = (bucket.astype(jnp.float32) + 0.5) / NB
    keep_rate = jnp.cos(t * (math.pi / 2))
    noise_rate = jnp.sin(t * (math.pi / 2))
    snr_ratio = keep_rate * keep_rate / (noise_rate * noise_rate)
    return (t, keep_rate, noise_rate, jnp.minimum(snr_ratio, 5.0) / (snr_ratio + 1.0))


def time_features(t):
    freqs = jnp.exp(-math.log(10000.0) * jnp.arange(TF // 2, dtype=jnp.float32) / (TF // 2))
    angle = t[:, None] * 1000.0 * freqs[None, :]
    return jnp.concatenate([jnp.cos(angle), jnp.sin(angle)], -1)


def timing_features(timing):
    seconds = timing.astype(jnp.float32) / 64.0
    return jnp.concatenate([time_features(seconds[:, 0]), time_features(seconds[:, 1])], -1)


def rope_tables(positions):
    inverse = 10000.0 ** (-2.0 * jnp.arange(rot_width // 2, dtype=jnp.float32) / rot_width)
    angle = positions[:, None].astype(jnp.float32) * inverse[None, :]
    angle = jnp.concatenate([angle, angle], -1)
    return (jnp.cos(angle), jnp.sin(angle))


def rotate(x):
    half = rot_width // 2
    return jnp.concatenate([-x[..., half:], x[..., :half]], -1)


def apply_rope(x, cosine, sine_part):
    turned = x[..., :rot_width]
    turned = turned * cosine[None, :, None, :] + rotate(turned) * sine_part[None, :, None, :]
    return jnp.concatenate([turned, x[..., rot_width:]], -1)


def rope_back(incoming_gradient, cosine, sine_part):
    turned = incoming_gradient[..., :rot_width]
    turned = turned * cosine[None, :, None, :] - rotate(turned * sine_part[None, :, None, :])
    return jnp.concatenate([turned, incoming_gradient[..., rot_width:]], -1)


def split_blocks(x, count, block):
    return x.reshape((x.shape[0], count, block) + x.shape[2:]).swapaxes(0, 1)


def join_blocks(x):
    x = x.swapaxes(0, 1)
    return x.reshape((x.shape[0], x.shape[1] * x.shape[2]) + x.shape[3:])


def attend(q, keys, values):
    rows_q = q.shape[1]
    block = min(512, rows_q)
    count = rows_q // block
    score_scale = HD ** (-0.5)

    def one_block(q_block):
        s = (
            jnp.einsum("ibd,ikd->ibk", q_block, keys, preferred_element_type=jnp.float32)
            * score_scale
        )
        top = jnp.max(s, -1, keepdims=True)
        lse = top + jnp.log(jnp.sum(jnp.exp(s - top), -1, keepdims=True))
        p = jnp.exp(s - lse)
        o = jnp.einsum(
            "ibk,ikd->ibd", p.astype(jnp.bfloat16), values, preferred_element_type=jnp.float32
        )
        return (o, lse[..., 0])

    outs, lses = lax.map(one_block, split_blocks(q, count, block))
    return (join_blocks(outs), join_blocks(lses))


def attend_back(q, keys, values, lse, grad_o):
    rows_q = q.shape[1]
    block = min(512, rows_q)
    count = rows_q // block
    score_scale = HD ** (-0.5)

    def one_block(carry, parts):
        d_key, d_value = carry
        q_block, g_block, l_block = parts
        s = (
            jnp.einsum("ibd,ikd->ibk", q_block, keys, preferred_element_type=jnp.float32)
            * score_scale
        )
        p = jnp.exp(s - l_block[..., None])
        d_prob = jnp.einsum("ibd,ikd->ibk", g_block, values, preferred_element_type=jnp.float32)
        d_value = d_value + jnp.einsum(
            "ibk,ibd->ikd", p.astype(jnp.bfloat16), g_block, preferred_element_type=jnp.float32
        )
        d_score = (p * (d_prob - jnp.sum(d_prob * p, -1, keepdims=True)) * score_scale).astype(
            jnp.bfloat16
        )
        d_query = jnp.einsum("ibk,ikd->ibd", d_score, keys, preferred_element_type=jnp.float32)
        d_key = d_key + jnp.einsum(
            "ibk,ibd->ikd", d_score, q_block, preferred_element_type=jnp.float32
        )
        return ((d_key, d_value), d_query)

    zeros = jnp.zeros(keys.shape, jnp.float32)
    parts = (
        split_blocks(q, count, block),
        split_blocks(grad_o, count, block),
        split_blocks(lse, count, block),
    )
    (d_key, d_value), d_queries = lax.scan(one_block, (zeros, zeros), parts)
    return (join_blocks(d_queries), d_key, d_value)


def adam(w, m, v, g, first_fix, second_fix):
    first = 0.9 * m + 0.1 * g
    second = 0.999 * v + 0.001 * g * g
    new = w - learn_rate * (
        first / first_fix / (jnp.sqrt(second / second_fix) + 1e-08) + weight_decay * w
    )
    return (new, first, second)


def exact(form, a, b):
    return jnp.einsum(form, a, b, precision=highest, preferred_element_type=jnp.float32)


def body(
    latents,
    noise_draw,
    audio_len,
    bucket,
    timing,
    prompt,
    prompt_len,
    step_count,
    edge_weight,
    edge_first,
    edge_second,
    attend_weight,
    attend_first,
    attend_second,
    square_weight,
    square_first,
    square_second,
    cross_weight,
    cross_first,
    cross_second,
    upward_weight,
    upward_first,
    upward_second,
    down_weight,
    down_first,
    down_second,
    gain_weight,
    gain_first,
    gain_second,
):
    low_type = jnp.bfloat16
    wide = jnp.float32
    groups, frames = (latents.shape[0], latents.shape[1])
    total_rows = groups * frames
    items = groups * H
    edge16, attend16, square16, cross16, upward16, down16, gain16 = (
        lax.all_gather(edge_weight.astype(low_type), ("seq", "dp"), axis=1, tiled=True),
        lax.all_gather(attend_weight.astype(low_type), ("seq", "dp"), axis=0, tiled=True),
        lax.all_gather(square_weight.astype(low_type), ("seq", "dp"), axis=1, tiled=True),
        lax.all_gather(cross_weight.astype(low_type), ("seq", "dp"), axis=0, tiled=True),
        lax.all_gather(upward_weight.astype(low_type), ("seq", "dp"), axis=0, tiled=True),
        lax.all_gather(down_weight.astype(low_type), ("seq", "dp"), axis=0, tiled=True),
        lax.all_gather(gain_weight.astype(low_type), ("seq", "dp"), axis=1, tiled=True),
    )
    norm_gains = gain16.astype(wide)
    positions = lax.axis_index("seq") * frames + jnp.arange(frames, dtype=jnp.int32)
    t, keep_rate, noise_rate, clip_weight = plan(bucket)
    frame_mask = (positions[None, :] < audio_len[:, None]).astype(wide)
    row_weight = (clip_weight[:, None] * frame_mask).reshape(total_rows)
    weight_sum = lax.psum(jnp.sum(row_weight), ("seq", "dp"))
    clean = latents.astype(wide)
    noisy_part = noise_draw.astype(wide)
    x_in = (
        (keep_rate[:, None, None] * clean + noise_rate[:, None, None] * noisy_part)
        .astype(low_type)
        .reshape(total_rows, C)
    )
    t_feat = time_features(t).astype(low_type)
    z_feat = timing_features(timing).astype(low_type)
    t_pre = jnp.dot(t_feat, edge16[2 * C : 2 * C + TF], preferred_element_type=wide)
    t_hidden = jax.nn.silu(t_pre).astype(low_type)
    leading_token = jnp.dot(t_hidden, square16[3], preferred_element_type=wide) + jnp.dot(
        z_feat, edge16[2 * C + TF :], preferred_element_type=wide
    )
    prefix_normed, prefix_standardized, prefix_inverse_deviation = layer_normalize(
        leading_token, norm_gains[0]
    )
    n_prefix_low = prefix_normed.astype(low_type)
    kv_prefix = jnp.dot(n_prefix_low, attend16[:, D:], preferred_element_type=wide).astype(low_type)
    k_prefix = kv_prefix[:, :D].reshape(items, 1, HD)
    v_prefix = kv_prefix[:, D:].reshape(items, 1, HD)
    hidden_start = jnp.dot(x_in, edge16[:C], preferred_element_type=wide)
    first_normed, first_standardized, first_inverse_deviation = layer_normalize(
        hidden_start, norm_gains[0]
    )
    n1_low = first_normed.astype(low_type)
    projected = jnp.dot(n1_low, attend16, preferred_element_type=wide).reshape(
        groups, frames, 3, H, HD
    )
    cosine, sine_part = rope_tables(positions + 1)
    rotated = jnp.stack(
        [
            apply_rope(projected[:, :, 0], cosine, sine_part),
            apply_rope(projected[:, :, 1], cosine, sine_part),
            projected[:, :, 2],
        ]
    ).astype(low_type)
    as_items = rotated.transpose(0, 1, 3, 2, 4).reshape(3, items, frames, HD)
    q_use = as_items[0]
    key_value = lax.all_gather(as_items[1:], "seq", axis=2, tiled=True)
    keys = jnp.concatenate([k_prefix, key_value[0]], 1)
    values = jnp.concatenate([v_prefix, key_value[1]], 1)
    o_items, lse = attend(q_use, keys, values)
    o_local = o_items.astype(low_type)
    o_low = o_local.reshape(groups, H, frames, HD).transpose(0, 2, 1, 3).reshape(total_rows, D)
    hidden_after_self = hidden_start + jnp.dot(o_low, square16[0], preferred_element_type=wide)
    second_normed, second_standardized, second_inverse_deviation = layer_normalize(
        hidden_after_self, norm_gains[1]
    )
    n2_low = second_normed.astype(low_type)
    cross_q = (
        jnp.dot(n2_low, square16[1], preferred_element_type=wide)
        .astype(low_type)
        .reshape(groups, frames, H, HD)
    )
    cross_kv = jnp.einsum("gpc,ce->gpe", prompt, cross16, preferred_element_type=wide).astype(
        low_type
    )
    cross_k = cross_kv[..., :D].reshape(groups, PT, H, HD)
    cross_v = cross_kv[..., D:].reshape(groups, PT, H, HD)
    key_mask = jnp.arange(PT)[None, :] < prompt_len[:, None]
    score_scale = HD ** (-0.5)
    scores = (
        jnp.einsum("gfhd,gphd->ghfp", cross_q, cross_k, preferred_element_type=wide) * score_scale
    )
    scores = jnp.where(key_mask[:, None, None, :], scores, -1000000000.0)
    probs = jax.nn.softmax(scores, -1)
    probs_low = probs.astype(low_type)
    co_low = (
        jnp.einsum("ghfp,gphd->gfhd", probs_low, cross_v, preferred_element_type=wide)
        .astype(low_type)
        .reshape(total_rows, D)
    )
    hidden_after_cross = hidden_after_self + jnp.dot(
        co_low, square16[2], preferred_element_type=wide
    )
    third_normed, third_standardized, third_inverse_deviation = layer_normalize(
        hidden_after_cross, norm_gains[2]
    )
    n3_low = third_normed.astype(low_type)
    gate_up = jnp.dot(n3_low, upward16, preferred_element_type=wide)
    gate, upper = (gate_up[:, :FF], gate_up[:, FF:])
    hidden = (jax.nn.silu(gate) * upper).astype(low_type)
    hidden_after_feed = hidden_after_cross + jnp.dot(hidden, down16, preferred_element_type=wide)
    fourth_normed, fourth_standardized, fourth_inverse_deviation = layer_normalize(
        hidden_after_feed, norm_gains[3]
    )
    n4_low = fourth_normed.astype(low_type)
    predicted = jnp.einsum("rd,cd->rc", n4_low, edge16[C : 2 * C], preferred_element_type=wide)
    target = (keep_rate[:, None, None] * noisy_part - noise_rate[:, None, None] * clean).reshape(
        total_rows, C
    )
    error = predicted - target
    loss_local = jnp.sum(row_weight[:, None] * error * error)
    d_pred = (2.0 / (C * weight_sum) * row_weight[:, None] * error).astype(low_type)
    g_out = jnp.einsum("rc,rd->cd", d_pred, n4_low, preferred_element_type=wide)
    fourth_norm_gradient = jnp.dot(d_pred, edge16[C : 2 * C], preferred_element_type=wide)
    hidden_gradient, fourth_gain_gradient = norm_backward(
        fourth_norm_gradient, fourth_standardized, fourth_inverse_deviation, norm_gains[3]
    )
    d_f = hidden_gradient.astype(low_type)
    g_down = jnp.einsum("rf,rd->fd", hidden, d_f, preferred_element_type=wide)
    d_hidden = jnp.einsum("rd,fd->rf", d_f, down16, preferred_element_type=wide)
    sig = jax.nn.sigmoid(gate)
    d_gate_up = jnp.concatenate(
        [d_hidden * upper * sig * (1.0 + gate * (1.0 - sig)), d_hidden * gate * sig], -1
    ).astype(low_type)
    g_up = jnp.einsum("rd,re->de", n3_low, d_gate_up, preferred_element_type=wide)
    third_norm_gradient = jnp.einsum("re,de->rd", d_gate_up, upward16, preferred_element_type=wide)
    partial_gradient, third_gain_gradient = norm_backward(
        third_norm_gradient, third_standardized, third_inverse_deviation, norm_gains[2]
    )
    hidden_gradient = hidden_gradient + partial_gradient
    d_c = hidden_gradient.astype(low_type)
    g_co = jnp.einsum("rd,re->de", co_low, d_c, preferred_element_type=wide)
    d_co = (
        jnp.einsum("re,de->rd", d_c, square16[2], preferred_element_type=wide)
        .astype(low_type)
        .reshape(groups, frames, H, HD)
    )
    d_prob = jnp.einsum("gfhd,gphd->ghfp", d_co, cross_v, preferred_element_type=wide)
    d_cv = jnp.einsum("ghfp,gfhd->gphd", probs_low, d_co, preferred_element_type=wide)
    d_score = (probs * (d_prob - jnp.sum(d_prob * probs, -1, keepdims=True)) * score_scale).astype(
        low_type
    )
    d_cq = (
        jnp.einsum("ghfp,gphd->gfhd", d_score, cross_k, preferred_element_type=wide)
        .astype(low_type)
        .reshape(total_rows, D)
    )
    d_ck = jnp.einsum("ghfp,gfhd->gphd", d_score, cross_q, preferred_element_type=wide)
    d_cross_kv = jnp.concatenate([d_ck.reshape(groups, PT, D), d_cv.reshape(groups, PT, D)], -1)
    g_cross = exact("gpc,gpe->ce", prompt.astype(wide), d_cross_kv)
    g_cq = jnp.einsum("rd,re->de", n2_low, d_cq, preferred_element_type=wide)
    second_norm_gradient = jnp.einsum("re,de->rd", d_cq, square16[1], preferred_element_type=wide)
    partial_gradient, second_gain_gradient = norm_backward(
        second_norm_gradient, second_standardized, second_inverse_deviation, norm_gains[1]
    )
    hidden_gradient = hidden_gradient + partial_gradient
    d_a = hidden_gradient.astype(low_type)
    g_o = jnp.einsum("rd,re->de", o_low, d_a, preferred_element_type=wide)
    d_o = jnp.einsum("re,de->rd", d_a, square16[0], preferred_element_type=wide).astype(low_type)
    d_o_items = d_o.reshape(groups, frames, H, HD).transpose(0, 2, 1, 3).reshape(items, frames, HD)
    d_query, d_key, d_value = attend_back(q_use, keys, values, lse, d_o_items)
    summed_key, summed_value = (
        lax.psum_scatter(
            d_key[:, 1:].astype(jnp.bfloat16), "seq", scatter_dimension=1, tiled=True
        ).astype(jnp.float32),
        lax.psum_scatter(
            d_value[:, 1:].astype(jnp.bfloat16), "seq", scatter_dimension=1, tiled=True
        ).astype(jnp.float32),
    )
    d_items = jnp.stack(
        [d_query.astype(low_type), summed_key.astype(low_type), summed_value.astype(low_type)]
    )
    d_key_prefix = d_key[:, :1]
    d_value_prefix = d_value[:, :1]
    d_rot = d_items.astype(wide).reshape(3, groups, H, frames, HD).transpose(1, 3, 0, 2, 4)
    d_projected = (
        jnp.stack(
            [
                rope_back(d_rot[:, :, 0], cosine, sine_part),
                rope_back(d_rot[:, :, 1], cosine, sine_part),
                d_rot[:, :, 2],
            ],
            2,
        )
        .reshape(total_rows, 3 * D)
        .astype(low_type)
    )
    g_attend = jnp.einsum("rd,re->de", n1_low, d_projected, preferred_element_type=wide)
    first_norm_gradient = jnp.einsum(
        "re,de->rd", d_projected, attend16, preferred_element_type=wide
    )
    partial_gradient, first_gain_gradient = norm_backward(
        first_norm_gradient, first_standardized, first_inverse_deviation, norm_gains[0]
    )
    hidden_gradient = hidden_gradient + partial_gradient
    g_in = jnp.einsum(
        "rc,rd->cd", x_in, hidden_gradient.astype(low_type), preferred_element_type=wide
    )
    d_kv_prefix = jnp.concatenate(
        [d_key_prefix.reshape(groups, D), d_value_prefix.reshape(groups, D)], -1
    )
    attend_kv = attend16[:, D:].astype(wide)
    g_attend = g_attend.at[:, D:].add(exact("gd,ge->de", n_prefix_low.astype(wide), d_kv_prefix))
    prefix_norm_gradient = exact("ge,de->gd", d_kv_prefix, attend_kv)
    leading_token_gradient, prefix_gain_gradient = norm_backward(
        prefix_norm_gradient, prefix_standardized, prefix_inverse_deviation, norm_gains[0]
    )
    g_timing = exact("gz,gd->zd", z_feat.astype(wide), leading_token_gradient)
    g_t2 = exact("ge,gd->ed", t_hidden.astype(wide), leading_token_gradient)
    d_t_hidden = exact("gd,ed->ge", leading_token_gradient, square16[3].astype(wide))
    t_sig = jax.nn.sigmoid(t_pre)
    d_t_pre = d_t_hidden * t_sig * (1.0 + t_pre * (1.0 - t_sig))
    g_t1 = exact("gz,gd->zd", t_feat.astype(wide), d_t_pre)
    g_edge = jnp.concatenate([g_in, g_out, g_t1, g_timing], 0)
    g_square = jnp.stack([g_o, g_cq, g_co, g_t2])
    g_gain = jnp.stack(
        [
            first_gain_gradient + prefix_gain_gradient,
            second_gain_gradient,
            third_gain_gradient,
            fourth_gain_gradient,
        ]
    )
    sharded = (
        lax.psum_scatter(g_edge, ("seq", "dp"), scatter_dimension=1, tiled=True),
        lax.psum_scatter(g_attend, ("seq", "dp"), scatter_dimension=0, tiled=True),
        lax.psum_scatter(g_square, ("seq", "dp"), scatter_dimension=1, tiled=True),
        lax.psum_scatter(g_cross, ("seq", "dp"), scatter_dimension=0, tiled=True),
        lax.psum_scatter(g_up, ("seq", "dp"), scatter_dimension=0, tiled=True),
        lax.psum_scatter(g_down, ("seq", "dp"), scatter_dimension=0, tiled=True),
        lax.psum_scatter(g_gain, ("seq", "dp"), scatter_dimension=1, tiled=True),
    )
    square_local = sum((jnp.sum(g * g) for g in sharded))
    square_total, loss_total = lax.psum((square_local, loss_local), ("seq", "dp"))
    grad_norm = jnp.sqrt(square_total)
    loss_value = loss_total / (C * weight_sum)
    factor = jnp.minimum(1.0, clip_norm / grad_norm)
    count = step_count[0].astype(wide)
    first_fix = 1.0 - 0.9**count
    second_fix = 1.0 - 0.999**count
    weights = (
        edge_weight,
        attend_weight,
        square_weight,
        cross_weight,
        upward_weight,
        down_weight,
        gain_weight,
    )
    firsts = (
        edge_first,
        attend_first,
        square_first,
        cross_first,
        upward_first,
        down_first,
        gain_first,
    )
    seconds = (
        edge_second,
        attend_second,
        square_second,
        cross_second,
        upward_second,
        down_second,
        gain_second,
    )
    out = [
        adam(w, m, v, g * factor, first_fix, second_fix)
        for w, m, v, g in zip(weights, firsts, seconds, sharded)
    ]
    return (
        loss_value,
        grad_norm,
        out[0][0],
        out[0][1],
        out[0][2],
        out[1][0],
        out[1][1],
        out[1][2],
        out[2][0],
        out[2][1],
        out[2][2],
        out[3][0],
        out[3][1],
        out[3][2],
        out[4][0],
        out[4][1],
        out[4][2],
        out[5][0],
        out[5][1],
        out[5][2],
        sharded[6] * factor,
        out[6][1],
        out[6][2],
    )


def solution(mesh):
    return jax.shard_map(
        body,
        mesh=mesh,
        in_specs=(
            P("dp", "seq", None),
            P("dp", "seq", None),
            P("dp"),
            P("dp"),
            P("dp", None),
            P("dp", None, None),
            P("dp"),
            P(),
            P(None, ("seq", "dp")),
            P(None, ("seq", "dp")),
            P(None, ("seq", "dp")),
            P(("seq", "dp"), None),
            P(("seq", "dp"), None),
            P(("seq", "dp"), None),
            P(None, ("seq", "dp"), None),
            P(None, ("seq", "dp"), None),
            P(None, ("seq", "dp"), None),
            P(("seq", "dp"), None),
            P(("seq", "dp"), None),
            P(("seq", "dp"), None),
            P(("seq", "dp"), None),
            P(("seq", "dp"), None),
            P(("seq", "dp"), None),
            P(("seq", "dp"), None),
            P(("seq", "dp"), None),
            P(("seq", "dp"), None),
            P(None, ("seq", "dp")),
            P(None, ("seq", "dp")),
            P(None, ("seq", "dp")),
        ),
        out_specs=(
            P(),
            P(),
            P(None, ("seq", "dp")),
            P(None, ("seq", "dp")),
            P(None, ("seq", "dp")),
            P(("seq", "dp"), None),
            P(("seq", "dp"), None),
            P(("seq", "dp"), None),
            P(None, ("seq", "dp"), None),
            P(None, ("seq", "dp"), None),
            P(None, ("seq", "dp"), None),
            P(("seq", "dp"), None),
            P(("seq", "dp"), None),
            P(("seq", "dp"), None),
            P(("seq", "dp"), None),
            P(("seq", "dp"), None),
            P(("seq", "dp"), None),
            P(("seq", "dp"), None),
            P(("seq", "dp"), None),
            P(("seq", "dp"), None),
            P(None, ("seq", "dp")),
            P(None, ("seq", "dp")),
            P(None, ("seq", "dp")),
        ),
        check_vma=False,
    )
```

profile of v0, /device:TPU:0, one launch (start us, length us, event | category | flops | bytes accessed | tf_op | source)
XLA Modules:
  0.0 4067.6 jit_solution(12668862339112010209)
XLA Ops:
  15.6 43.3 %all-gather = bf16[32,48,4]{1,2,0:T(4,128)(2,1)S(1)} all-gather(bf16[1,48,4]{1,2,0:T(4,128)(2,1)S(1)} %convert_bitcast_fusion.2), channel_id=1, replica_groups=mesh['seq'=4,'dp'=8] {'seq','dp'}, dimensions={0}, use_global_device_ids=true | all-gather | bytes 12672 | tf_op jit(solution)/shard_map/all_gather | solution.py:213
  61.8 10.9 all-gather.9.cloned.1.call-done
  78.3 100.0 %all-gather.11.cloned.1.call-done = bf16[1536,4608]{1,0:T(8,128)(2,1)} async-done(((bf16[48,4608]{1,0:T(8,128)(2,1)}), bf16[1536,4608]{1,0:T(8,128)(2,1)}) %all-gather.11.cloned.1.call-update) | async-done | bytes 14155792 | tf_op jit(solution)/shard_map/all_gather | solution.py:208
  178.3 23.0 fusion.157
  201.4 24.7 reshape.422
  259.3 33.8 maximum_bitcast_fusion
  311.8 41.1 %psum.22 = f32[]{:T(128)} all-reduce(f32[]{:T(128)} %get-tuple-element.272), channel_id=1, replica_groups=mesh['seq'=4,'dp'=8] {'seq','dp'}, use_global_device_ids=true, to_apply=%region_17.18 | all-reduce | flops 1 | bytes 8 | tf_op jit(solution)/shard_map/psum | solution.py:220
  391.2 208.2 %all-gather.15.cloned.1.call-done = bf16[2,48,2048,64]{2,3,1,0:T(8,128)(2,1)} async-done(((bf16[2,48,512,64]{2,3,1,0:T(8,128)(2,1)}), bf16[2,48,2048,64]{2,3,1,0:T(8,128)(2,1)}) %all-gather.15.cloned.1.call-update) | async-done | bytes 25165840 | tf_op jit(solution)/shard_map/all_gather | solution.py:260
  599.4 18.1 slice_bitcast_fusion.1
  617.6 90.5 %multiply_reduce_fusion.1 = (f32[48,512]{1,0:T(8,128)}, f32[48,512,2049]{1,2,0:T(8,128)}) fusion(bf16[48,512,64]{1,2,0:T(8,128)(2,1)S(1)} %bitcast.214, bf16[48,2048,64]{1,2,0:T(8,128)(2,1)} %get-tuple-element.244, bf16[48,1,64]{1,2,0:T(8,128)(2,1)} %reshape.443), kind=kOutput, calls=%fused_computation.8 | convolution fusion | flops 6571462656 | bytes 217257984 | tf_op jit(solution)/shard_map/while/body/eval_jaxpr/ibd,ikd->ibk/dot_general | solution.py:105
  708.0 65.6 %exponential_reduce_fusion = f32[48,512]{1,0:T(8,128)S(1)} fusion(f32[48,512,2049]{1,2,0:T(8,128)} %get-tuple-element.293, f32[48,512]{1,0:T(8,128)} %get-tuple-element.292), kind=kLoop, calls=%fused_computation.7 | loop fusion | flops 151044096 | bytes 201621504 | tf_op jit(solution)/shard_map/while/body/eval_jaxpr/reduce_sum | solution.py:109
  773.7 71.9 %fusion.80 = bf16[48,512,64]{1,2,0:T(8,128)(2,1)} fusion(bf16[48,2048,64]{1,2,0:T(8,128)(2,1)} %get-tuple-element.245, bf16[48,1,64]{1,2,0:T(8,128)(2,1)S(1)} %copy-done.28, f32[48,512,2049]{1,2,0:T(8,128)} %get-tuple-element.293, f32[48,512]{1,0:T(8,128)S(1)} %log_add_fusion), kind=kOutput, calls=%fused_computation.152 | convolution fusion | flops 6623416320 | bytes 217257984 | tf_op jit(solution)/shard_map/while/body/eval_jaxpr/ibk,ikd->ibd/dot_general | solution.py:111
  851.8 8.7 fusion.170
  885.2 13.1 fusion.171
  920.4 48.8 %fusion.158 = f32[1024,12288]{1,0:T(8,128)} fusion(bf16[1536,12288]{1,0:T(8,128)(2,1)} %all-gather.19.cloned.1.call-done, f32[1024,1536]{1,0:T(8,128)} %copy-done.11, f32[1536]{0:T(1024)S(1)} %copy-done.82, f32[1024]{0:T(1024)S(1)} %add_rsqrt_fusion.1, f32[1024]{0:T(1024)S(1)} %broadcast_multiply_fusion.11), kind=kOutput, calls=%fused_computation.321 | convolution fusion | flops 38660997120 | bytes 94386176 | tf_op jit(solution)/shard_map/dot_general | solution.py:301
  969.2 21.2 multiply_convert_fusion.3
  990.5 27.5 fusion.173
  1030.9 40.9 %multiply_convert_fusion.2 = (bf16[1024,6144]{1,0:T(8,128)(2,1)}, bf16[1024,6144]{1,0:T(8,128)(2,1)}) fusion(f32[1024,12288]{1,0:T(8,128)} %fusion.158, bf16[6144,1536]{1,0:T(8,128)(2,1)} %all-gather.21.cloned.1.call-done, f32[1024,1536]{1,0:T(8,128)} %subtract_multiply_fusion), kind=kOutput, calls=%fused_computation.21 | convolution fusion | flops 19410714624 | bytes 100663296 | tf_op jit(solution)/shard_map/rd,fd->rf/dot_general | solution.py:323
  1071.8 51.5 %multiply_reduce_fusion.4 = (f32[1536]{0:T(1024)}, f32[1024]{0:T(1024)S(1)}, f32[1024]{0:T(1024)S(1)}, f32[1024,1536]{1,0:T(8,128)}) fusion(f32[1024,1536]{1,0:T(8,128)} %copy-done.11, f32[1024]{0:T(1024)S(1)} %copy-done.95, f32[1024]{0:T(1024)S(1)} %copy-done.73, f32[1536]{0:T(1024)S(1)} %copy-done.83, ...), kind=kOutput, calls=%fused_computation.59 | convolution fusion | flops 38717620224 | bytes 75526144 | tf_op jit(solution)/shard_map/re,de->rd/dot_general | solution.py:329
  1160.0 19.8 convert_bitcast_fusion
  1186.0 13.6 multiply_reduce_fusion.5
  1205.1 8.8 fusion.60
  1223.6 72.1 %fusion.24 = f32[48,2049,64]{1,2,0:T(8,128)} fusion(bf16[48,512,64]{1,2,0:T(8,128)(2,1)S(1)} %bitcast.195, f32[48,512,2049]{1,2,0:T(8,128)} %get-tuple-element.293, f32[48,512]{1,0:T(8,128)} %copy-done.58), kind=kOutput, calls=%fused_computation.28 | convolution fusion | flops 6596665344 | bytes 229847040 | tf_op jit(solution)/shard_map/while/body/eval_jaxpr/ibk,ibd->ikd/dot_general | solution.py:135
  1295.7 15.9 slice.390
  1311.7 89.1 %fusion.30 = f32[48,512,2049]{1,2,0:T(8,128)} fusion(bf16[48,512,64]{1,2,0:T(8,128)(2,1)S(1)} %bitcast.196, bf16[48,2048,64]{1,2,0:T(8,128)(2,1)} %get-tuple-element.245, bf16[48,1,64]{1,2,0:T(8,128)(2,1)} %reshape.444), kind=kOutput, calls=%fused_computation.43 | convolution fusion | flops 6470774784 | bytes 217159680 | tf_op jit(solution)/shard_map/while/body/eval_jaxpr/ibd,ikd->ibk/dot_general | solution.py:134
  1400.8 248.6 %fusion.8 = f32[48,2049,64]{1,2,0:T(8,128)} fusion(bf16[48,512,64]{1,2,0:T(8,128)(2,1)} %bitcast.213, f32[48,512,2049]{1,2,0:T(8,128)} %fusion.30, f32[48,512,2049]{1,2,0:T(8,128)} %get-tuple-element.293, f32[48,512]{1,0:T(8,128)} %copy-done.58), kind=kOutput, calls=%fused_computation.10 | convolution fusion | flops 6898829312 | bytes 431271936 | tf_op jit(solution)/shard_map/while/body/eval_jaxpr/ibk,ibd->ikd/dot_general | solution.py:142
  1649.4 15.8 slice.391
  1667.2 21.7 fusion.42
  1703.0 9.9 copy.293
  1715.7 247.3 %fusion.83 = bf16[48,512,64]{1,2,0:T(8,128)(2,1)} fusion(bf16[48,2048,64]{1,2,0:T(8,128)(2,1)} %get-tuple-element.244, bf16[48,1,64]{1,2,0:T(8,128)(2,1)S(1)} %copy-done.27, f32[48,512,2049]{1,2,0:T(8,128)} %fusion.30, f32[48,512,2049]{1,2,0:T(8,128)} %get-tuple-element.293, f32[48,512]{1,0:T(8,128)S(1)} %copy-done.59), kind=kOutput, calls=%fused_computation.153 | convolution fusion | flops 6925580288 | bytes 418682880 | tf_op jit(solution)/shard_map/while/body/eval_jaxpr/ibk,ikd->ibd/dot_general | solution.py:141
  1971.9 10.0 multiply_reduce_fusion.25
  2009.0 20.8 fusion.165
  2070.8 34.4 pad_maximum_fusion.6
  2105.3 10.4 copy.307
  2115.7 24.7 multiply_reduce_fusion.6
  2158.7 29.2 fusion.97
  2192.8 10.8 convolution_bitcast_fusion.1
  2211.6 9.0 convolution_bitcast_fusion.2
  2220.6 23.8 pad_maximum_fusion
  2244.6 23.9 fusion.156
  2268.5 18.5 fusion.21
  2287.7 51.8 %fusion.22 = f32[1536,12288]{1,0:T(8,128)} fusion(bf16[1024,6144]{1,0:T(8,128)(2,1)} %get-tuple-element.243, bf16[1024,6144]{1,0:T(8,128)(2,1)} %get-tuple-element.242, f32[1024,1536]{1,0:T(8,128)} %copy-done.11, f32[1536]{0:T(1024)S(1)} %copy-done.84, f32[1024]{0:T(1024)S(1)} %copy-done.96, f32[1024]{0:T(1024)S(1)} %copy-done.74), kind=kOutput, calls=%fused_computation.26 | convolution fusion | flops 38711328768 | bytes 106969088 | tf_op jit(solution)/shard_map/rd,re->de/dot_general | solution.py:328
  2344.4 9.2 reduce-scatter.28.cloned.1.call-done
  2355.4 352.3 %reduce-scatter.26.cloned.1.call-done = f32[192,1536]{1,0:T(8,128)} async-done(((f32[6144,1536]{1,0:T(8,128)}), f32[192,1536]{1,0:T(8,128)}) %reduce-scatter.26.cloned.1.call-update) | async-done | bytes 1179664 | tf_op jit(solution)/shard_map/reduce_scatter | solution.py:433
  2709.8 351.5 %reduce-scatter.22.cloned.1.call-done = f32[4,48,1536]{2,1,0:T(8,128)} async-done(((f32[4,1536,1536]{2,1,0:T(8,128)}), f32[4,48,1536]{2,1,0:T(8,128)}) %reduce-scatter.22.cloned.1.call-update) | async-done | bytes 1179664 | tf_op jit(solution)/shard_map/reduce_scatter | solution.py:430
  3063.5 266.8 %reduce-scatter.20.cloned.1.call-done = f32[48,4608]{1,0:T(8,128)} async-done(((f32[1536,4608]{1,0:T(8,128)}), f32[48,4608]{1,0:T(8,128)}) %reduce-scatter.20.cloned.1.call-update) | async-done | bytes 884752 | tf_op jit(solution)/shard_map/reduce_scatter | solution.py:429
  3335.0 657.6 %reduce-scatter.24.cloned.1.call-done = f32[48,12288]{1,0:T(8,128)} async-done(((f32[1536,12288]{1,0:T(8,128)}), f32[48,12288]{1,0:T(8,128)}) %reduce-scatter.24.cloned.1.call-update) | async-done | bytes 2359312 | tf_op jit(solution)/shard_map/reduce_scatter | solution.py:432
  3997.4 39.9 all-reduce
  (475 shorter events, 391.4 us)
Async XLA Ops:
  7.2 350.5 %copy-start = (bf16[2,128,768]{2,1,0:T(8,128)(2,1)S(1)}, bf16[2,128,768]{2,1,0:T(8,128)(2,1)}, u32[]{:S(2)}) copy-start(bf16[2,128,768]{2,1,0:T(8,128)(2,1)} %param.36) | copy-start | bytes 1179652
  7.2 65.5 %all-gather.9.cloned.1.call-start = ((), (), s32[]{:S(2)}) async-start(), calls=%async_computation.9 | async-start | bytes 2838528 | tf_op jit(solution)/shard_map/all_gather | solution.py:207
  8.9 169.4 %all-gather.11.cloned.1.call-start = ((), (), s32[]{:S(2)}) async-start(), calls=%async_computation.10 | async-start | bytes 14598144 | tf_op jit(solution)/shard_map/all_gather | solution.py:208
  10.9 346.7 %all-gather.17.cloned.1.call-start = ((), (), s32[]{:S(2)}) async-start(), calls=%async_computation.13 | async-start | bytes 4866048 | tf_op jit(solution)/shard_map/all_gather | solution.py:210
  12.6 359.1 %all-gather.13.cloned.1.call-start = ((), (), s32[]{:S(2)}) async-start(), calls=%async_computation.11 | async-start | bytes 19464192 | tf_op jit(solution)/shard_map/all_gather | solution.py:209
  14.9 584.5 %all-gather.15.cloned.1.call-start = ((), (), s32[]{:S(2)}) async-start(), calls=%async_computation.12 | async-start | bytes 31457280 | tf_op jit(solution)/shard_map/all_gather | solution.py:260
  61.1 179.0 %copy-start.54 = (f32[512,32]{0,1:T(8,128)}, f32[512,32]{0,1:T(8,128)S(1)}, u32[]{:S(2)}) copy-start(f32[512,32]{0,1:T(8,128)S(1)} %get-tuple-element.268) | copy-start | bytes 196612
  61.1 179.0 %copy-start.56 = (f32[512,32]{0,1:T(8,128)}, f32[512,32]{0,1:T(8,128)S(1)}, u32[]{:S(2)}) copy-start(f32[512,32]{0,1:T(8,128)S(1)} %get-tuple-element.269) | copy-start | bytes 196612
  61.8 315.3 %copy-start.60 = (f32[1536]{0:T(1024)}, f32[1536]{0:T(1024)S(1)}, u32[]{:S(2)}) copy-start(f32[1536]{0:T(1024)S(1)} %get-tuple-element.212) | copy-start | bytes 18436
  74.9 126.5 %copy-start.70 = (f32[1024]{0:T(1024)}, f32[1024]{0:T(1024)S(1)}, u32[]{:S(2)}) copy-start(f32[1024]{0:T(1024)S(1)} %broadcast_multiply_fusion.13) | copy-start | bytes 12292
  78.3 123.1 %copy-start.92 = (f32[1024]{0:T(1024)}, f32[1024]{0:T(1024)S(1)}, u32[]{:S(2)}) copy-start(f32[1024]{0:T(1024)S(1)} %add_rsqrt_fusion.3) | copy-start | bytes 12292
  305.3 615.1 %all-gather.19.cloned.1.call-start = ((), (), s32[]{:S(2)}) async-start(), calls=%async_computation.14 | async-start | bytes 38928384 | tf_op jit(solution)/shard_map/all_gather | solution.py:211
  308.1 682.4 %all-gather.21.cloned.1.call-start = ((), (), s32[]{:S(2)}) async-start(), calls=%async_computation.15 | async-start | bytes 19464192 | tf_op jit(solution)/shard_map/all_gather | solution.py:212
  310.3 1684.8 %reduce-scatter.18.cloned.1.call-start = ((), (), s32[]{:S(2)}) async-start(), calls=%async_computation.17 | async-start | bytes 15728640 | tf_op jit(solution)/shard_map/reduce_scatter | solution.py:369
  355.5 19.3 copy-start.109
  355.5 19.3 copy-start.111
  391.2 226.4 %copy-start.17 = (bf16[1,2,24,512,64]{3,4,2,1,0:T(8,128)(2,1)S(1)}, bf16[1,2,24,512,64]{3,4,2,1,0:T(8,128)(2,1)}, u32[]{:S(2)}) copy-start(bf16[1,2,24,512,64]{3,4,2,1,0:T(8,128)(2,1)} %copy.259) | copy-start | bytes 9437188
  708.0 65.6 %copy-start.51 = (f32[48,512]{1,0:T(8,128)S(1)}, f32[48,512]{1,0:T(8,128)}, u32[]{:S(2)}) copy-start(f32[48,512]{1,0:T(8,128)} %get-tuple-element.292) | copy-start | bytes 294916
  708.0 65.7 %copy-start.28 = (bf16[48,1,64]{1,2,0:T(8,128)(2,1)S(1)}, bf16[48,1,64]{1,2,0:T(8,128)(2,1)}, u32[]{:S(2)}) copy-start(bf16[48,1,64]{1,2,0:T(8,128)(2,1)} %reshape.444) | copy-start | bytes 18436
  773.7 71.9 %copy-start.58 = (f32[48,512]{1,0:T(8,128)}, f32[48,512]{1,0:T(8,128)S(1)}, u32[]{:S(2)}) copy-start(f32[48,512]{1,0:T(8,128)S(1)} %log_add_fusion) | copy-start | bytes 294916
  917.0 52.2 %copy-start.72 = (f32[1024]{0:T(1024)}, f32[1024]{0:T(1024)S(1)}, u32[]{:S(2)}) copy-start(f32[1024]{0:T(1024)S(1)} %broadcast_multiply_fusion.11) | copy-start | bytes 12292
  920.3 48.9 %copy-start.94 = (f32[1024]{0:T(1024)}, f32[1024]{0:T(1024)S(1)}, u32[]{:S(2)}) copy-start(f32[1024]{0:T(1024)S(1)} %add_rsqrt_fusion.1) | copy-start | bytes 12292
  1030.9 40.9 %copy-start.73 = (f32[1024]{0:T(1024)S(1)}, f32[1024]{0:T(1024)}, u32[]{:S(2)}) copy-start(f32[1024]{0:T(1024)} %copy-done.72) | copy-start | bytes 12292
  1030.9 40.9 %copy-start.83 = (f32[1536]{0:T(1024)S(1)}, f32[1536]{0:T(1024)}, u32[]{:S(2)}) copy-start(f32[1536]{0:T(1024)} %get-tuple-element.210) | copy-start | bytes 18436
  1030.9 40.9 %copy-start.95 = (f32[1024]{0:T(1024)S(1)}, f32[1024]{0:T(1024)}, u32[]{:S(2)}) copy-start(f32[1024]{0:T(1024)} %copy-done.94) | copy-start | bytes 12292
  1071.8 51.5 %copy-start.9 = (f32[1024,1536]{1,0:T(8,128)S(1)}, f32[1024,1536]{1,0:T(8,128)}, u32[]{:S(2)}) copy-start(f32[1024,1536]{1,0:T(8,128)} %subtract_multiply_fusion) | copy-start | bytes 18874372
  1311.6 690.3 %reduce-scatter.16.cloned.1.call-start = ((), (), s32[]{:S(2)}) async-start(), calls=%async_computation.16 | async-start | bytes 15728640 | tf_op jit(solution)/shard_map/reduce_scatter | solution.py:366
  1665.3 675.1 %reduce-scatter.30.cloned.1.call-start = ((), (), s32[]{:S(2)}) async-start(), calls=%async_computation.23 | async-start | bytes 9732096 | tf_op jit(solution)/shard_map/reduce_scatter | solution.py:431
  1667.2 21.7 copy-start.16
  1994.9 348.1 %reduce-scatter.32.cloned.1.call-start = ((), (), s32[]{:S(2)}) async-start(), calls=%async_computation.24 | async-start | bytes 811008
  2115.7 24.8 copy-start.89
  2115.7 24.8 copy-start.90
  2115.7 24.8 copy-start.91
  2115.7 26.1 copy-start.43
  2141.7 211.8 %reduce-scatter.28.cloned.1.call-start = ((), (), s32[]{:S(2)}) async-start(), calls=%async_computation.22 | async-start | bytes 5677056
  2158.6 549.0 %reduce-scatter.26.cloned.1.call-start = ((), (), s32[]{:S(2)}) async-start(), calls=%async_computation.21 | async-start | bytes 38928384 | tf_op jit(solution)/shard_map/reduce_scatter | solution.py:433
  2187.9 873.4 %reduce-scatter.22.cloned.1.call-start = ((), (), s32[]{:S(2)}) async-start(), calls=%async_computation.19 | async-start | bytes 38928384 | tf_op jit(solution)/shard_map/reduce_scatter | solution.py:430
  2244.5 24.0 copy-start.64
  2244.5 24.0 copy-start.68
  2244.5 1085.8 %reduce-scatter.20.cloned.1.call-start = ((), (), s32[]{:S(2)}) async-start(), calls=%async_computation.18 | async-start | bytes 29196288 | tf_op jit(solution)/shard_map/reduce_scatter | solution.py:429
  2287.1 1705.5 %reduce-scatter.24.cloned.1.call-start = ((), (), s32[]{:S(2)}) async-start(), calls=%async_computation.20 | async-start | bytes 77856768 | tf_op jit(solution)/shard_map/reduce_scatter | solution.py:432
  2339.5 1699.2 %copy-start.115 = (f32[4,48]{1,0:T(4,128)S(1)}, f32[4,48]{1,0:T(4,128)}, u32[]{:S(2)}) copy-start(f32[4,48]{1,0:T(4,128)} %param.59) | copy-start | bytes 2308
  2339.6 1699.8 %copy-start.116 = (f32[4,48]{1,0:T(4,128)S(1)}, f32[4,48]{1,0:T(4,128)}, u32[]{:S(2)}) copy-start(f32[4,48]{1,0:T(4,128)} %param.58) | copy-start | bytes 2308
  2339.6 1700.4 %copy-start.53 = (f32[896,48]{0,1:T(8,128)S(1)}, f32[896,48]{0,1:T(8,128)}, u32[]{:S(2)}) copy-start(f32[896,48]{0,1:T(8,128)} %param.39) | copy-start | bytes 516100
  2339.6 1702.3 %copy-start.49 = (f32[24,3072]{1,0:T(8,128)S(1)}, f32[24,3072]{1,0:T(8,128)}, u32[]{:S(2)}) copy-start(f32[24,3072]{1,0:T(8,128)} %param.48) | copy-start | bytes 884740
  2340.4 1701.5 %copy-start.48 = (f32[24,3072]{1,0:T(8,128)S(1)}, f32[24,3072]{1,0:T(8,128)}, u32[]{:S(2)}) copy-start(f32[24,3072]{1,0:T(8,128)} %reduce-scatter.30.cloned.1.call-done) | copy-start | bytes 884740
  3063.5 984.5 %copy-start.23 = (f32[4,48,1536]{2,1,0:T(8,128)S(1)}, f32[4,48,1536]{2,1,0:T(8,128)}, u32[]{:S(2)}) copy-start(f32[4,48,1536]{2,1,0:T(8,128)} %param.45) | copy-start | bytes 3538948
  3063.5 984.5 %copy-start.26 = (f32[4,48,1536]{2,1,0:T(8,128)S(1)}, f32[4,48,1536]{2,1,0:T(8,128)}, u32[]{:S(2)}) copy-start(f32[4,48,1536]{2,1,0:T(8,128)} %reduce-scatter.22.cloned.1.call-done) | copy-start | bytes 3538948
  (105 other events, 836.8 us)
Sparse Core Ops, SparseCore 0:
  11.6 61.0 all-gather.8
  76.3 101.9 all-gather.10
  181.9 61.7 all-gather.16
  247.4 124.3 all-gather.12
  373.4 225.9 all-gather.14
  602.9 215.0 all-gather.18
  821.5 122.9 all-gather.20
  1311.8 120.4 reduce-scatter.17
  1665.4 120.8 reduce-scatter.15
  1995.0 135.7 reduce-scatter.29
  2141.9 95.7 reduce-scatter.31
  2244.0 109.4 reduce-scatter.27
  2360.0 347.6 reduce-scatter.25
  2715.1 346.2 reduce-scatter.21
  3067.6 262.6 reduce-scatter.19
  3336.7 655.9 reduce-scatter.23
where the time goes:
time: 4070 us
  waiting for transfers between devices  1960 us (48%)
  matrix products  1390 us (34%)
  other arithmetic  308 us (8%)
  local copies, waits for them, and re-layouts  261 us (6%)
  blocking collectives  124 us (3%)
    reduce_scatter x1, waiting for transfers between devices, body(): lax.psum_scatter(g_up, ('seq', 'dp'), scatter_dimension=0, tiled=True)  658 us
    reduce_scatter x1, waiting for transfers between devices, body(): lax.psum_scatter(g_down, ('seq', 'dp'), scatter_dimension=0, tiled=True)  352 us
    reduce_scatter x1, waiting for transfers between devices, body(): lax.psum_scatter(g_square, ('seq', 'dp'), scatter_dimension=1, tiled=True)  352 us
    reduce_scatter x1, waiting for transfers between devices, body(): lax.psum_scatter(g_attend, ('seq', 'dp'), scatter_dimension=0, tiled=True)  267 us
    dot_general x1, matrix products, one_block(): jnp.einsum('ibk,ibd->ikd', d_score, q_block, preferred_element_type=jnp.f...  249 us
    dot_general x1, matrix products, one_block(): jnp.einsum('ibk,ikd->ibd', d_score, keys, preferred_element_type=jnp.floa...  247 us
    all_gather x1, waiting for transfers between devices, body(): key_value = lax.all_gather(as_items[1:], 'seq', axis=2, tiled=True)  208 us
    all_gather x1, waiting for transfers between devices, body(): lax.all_gather(attend_weight.astype(low_type), ('seq', 'dp'), axis=0, til...  100 us
  transfers between devices with their start and end apart: 16, of which 9 were waited for; matrix products, arithmetic and copies ran while one was open for 39% of the time, Pallas kernels for 0%

commit v1 on v0

--- a/solution.py
+++ b/solution.py
@@ -1,8 +1,12 @@
+import functools
 import math
 
 import jax
 import jax.numpy as jnp
 from jax import lax
+from jax.experimental import pallas as pl
+from jax.experimental.pallas import tpu as pltpu
+from jax.sharding import Mesh
 from jax.sharding import PartitionSpec as P
 
 D = 1536
@@ -167,7 +171,7 @@
     return jnp.einsum(form, a, b, precision=highest, preferred_element_type=jnp.float32)
 
 
-def body(
+def general_body(
     latents,
     noise_draw,
     audio_len,
@@ -499,65 +503,737 @@
     )
 
 
+f32 = jnp.float32
+bf16 = jnp.bfloat16
+HALF = D // 2
+PAIRS = HALF // 128
+HIDE = FF // 2
+
+
+def dot_nt(a, b):
+    return lax.dot_general(a, b, (((1,), (1,)), ((), ())), preferred_element_type=f32)
+
+
+def dot_nn(a, b):
+    return lax.dot_general(a, b, (((1,), (0,)), ((), ())), preferred_element_type=f32)
+
+
+def dot_tn(a, b):
+    return lax.dot_general(a, b, (((0,), (0,)), ((), ())), preferred_element_type=f32)
+
+
+def call(kernel, grid, in_specs, out_specs, out_shape, scratch, cost, *operands):
+    return pl.pallas_call(
+        kernel,
+        grid=grid,
+        in_specs=in_specs,
+        out_specs=out_specs,
+        out_shape=out_shape,
+        scratch_shapes=scratch,
+        cost_estimate=pl.CostEstimate(flops=cost[0], bytes_accessed=cost[1], transcendentals=0),
+        compiler_params=pltpu.CompilerParams(vmem_limit_bytes=60 << 20),
+    )(*operands)
+
+
+def shape_of(shape, kind):
+    return jax.ShapeDtypeStruct(shape, kind)
+
+
+def turn(y, cosine, sine_up, sine_down):
+    return y * cosine + pltpu.roll(y, 16, 1) * sine_up + pltpu.roll(y, 112, 1) * sine_down
+
+
+def turn_tables(positions):
+    lane = jnp.arange(128) % HD
+    inverse = 10000.0 ** (-2.0 * jnp.arange(rot_width // 2, dtype=f32) / rot_width)
+    angle = positions[:, None].astype(f32) * inverse[None, :]
+    wide_angle = jnp.tile(angle, (1, 128 // (rot_width // 2)))
+    cosine = jnp.where(lane[None, :] < rot_width, jnp.cos(wide_angle), 1.0)
+    sine = jnp.sin(wide_angle)
+    second = (lane[None, :] >= rot_width // 2) & (lane[None, :] < rot_width)
+    sine_up = jnp.where(second, sine, 0.0)
+    sine_down = jnp.where(lane[None, :] < rot_width // 2, -sine, 0.0)
+    return (cosine, sine_up, sine_down)
+
+
+def qkv_kernel(n_ref, w_ref, cos_ref, up_ref, down_ref, out_ref):
+    part = pl.program_id(0)
+    y = dot_nn(n_ref[...], w_ref[...])
+
+    @pl.when(part < 2)
+    def _():
+        scale = jnp.where(part == 0, HD ** (-0.5), 1.0)
+        for j in range(PAIRS):
+            block = y[:, j * 128 : (j + 1) * 128]
+            turned = turn(block, cos_ref[...], up_ref[...], down_ref[...])
+            out_ref[:, j * 128 : (j + 1) * 128] = (turned * scale).astype(bf16)
+
+    @pl.when(part == 2)
+    def _():
+        out_ref[...] = y.astype(bf16)
+
+
+def qkv_project(n, w, tables, block=512):
+    rows = n.shape[0]
+    table = pl.BlockSpec((block, 128), lambda p, i: (i, 0))
+    return call(
+        qkv_kernel,
+        (3, rows // block),
+        [
+            pl.BlockSpec((block, D), lambda p, i: (i, 0)),
+            pl.BlockSpec((D, HALF), lambda p, i: (0, p)),
+            table,
+            table,
+            table,
+        ],
+        pl.BlockSpec((block, HALF), lambda p, i: (i, p)),
+        shape_of((rows, 3 * HALF), bf16),
+        [],
+        (2 * rows * D * 3 * HALF, 4 * rows * D * 2),
+        n,
+        w,
+        *tables,
+    )
+
+
+def attend_kernel(q_ref, k_ref, v_ref, k0_ref, v0_ref, o_ref, lse_ref, *, chunk, count):
+    q = q_ref[...]
+    rows = q.shape[0]
+    lane = lax.broadcasted_iota(jnp.int32, q.shape, 1)
+    k0 = k0_ref[0:1].astype(f32)
+    v0 = v0_ref[0:1].astype(f32)
+    outs = []
+    for head in range(2):
+        mine = jnp.where((lane // HD) == head, q, jnp.zeros_like(q))
+        top = jnp.sum(mine.astype(f32) * k0, 1, keepdims=True)
+        total = jnp.ones_like(top)
+        acc = jnp.broadcast_to(v0, (rows, 128))
+        for c in range(count):
+            s = dot_nt(mine, k_ref[c * chunk : (c + 1) * chunk])
+            new_top = jnp.maximum(top, jnp.max(s, 1, keepdims=True))
+            fade = jnp.exp(top - new_top)
+            p = jnp.exp(s - new_top)
+            total = total * fade + jnp.sum(p, 1, keepdims=True)
+            acc = acc * fade + dot_nn(p.astype(bf16), v_ref[c * chunk : (c + 1) * chunk])
+            top = new_top
+        outs.append(acc / total)
+        lse_ref[0, head : head + 1, :] = (top + jnp.log(total)).T
+    o_ref[...] = jnp.where(lane < HD, outs[0], outs[1]).astype(bf16)
+
+
+def attend_forward(qkv, k0, v0, block=1024, chunk=512):
+    rows = qkv.shape[0]
+    lead = pl.BlockSpec((16, 128), lambda j, i: (0, j))
+    return call(
+        functools.partial(attend_kernel, chunk=chunk, count=rows // chunk),
+        (PAIRS, rows // block),
+        [
+            pl.BlockSpec((block, 128), lambda j, i: (i, j)),
+            pl.BlockSpec((rows, 128), lambda j, i: (0, PAIRS + j)),
+            pl.BlockSpec((rows, 128), lambda j, i: (0, 2 * PAIRS + j)),
+            lead,
+            lead,
+        ],
+        [
+            pl.BlockSpec((block, 128), lambda j, i: (i, j)),
+            pl.BlockSpec((1, 2, block), lambda j, i: (j, 0, i)),
+        ],
+        [shape_of((rows, HALF), bf16), shape_of((PAIRS, 2, rows), f32)],
+        [],
+        (16 * rows * rows * HALF, 5 * rows * D * 2),
+        qkv,
+        qkv,
+        qkv,
+        k0,
+        v0,
+    )
+
+
+def attend_back_kernel(
+    q_ref, g_ref, o_ref, lse_ref, cos_ref, up_ref, down_ref,
+    k_ref, v_ref, k0_ref, v0_ref, kcos_ref, kup_ref, kdown_ref,
+    dq_ref, dk_ref, dv_ref, dk0_ref, dv0_ref,
+    kt, dka, dva, dk0a, dv0a, *, chunk, count, steps,
+):
+    i = pl.program_id(1)
+
+    @pl.when(i == 0)
+    def _():
+        kt[...] = k_ref[...].T
+        dka[...] = jnp.zeros_like(dka)
+        dva[...] = jnp.zeros_like(dva)
+        dk0a[...] = jnp.zeros_like(dk0a)
+        dv0a[...] = jnp.zeros_like(dv0a)
+
+    q = q_ref[...]
+    g = g_ref[...]
+    rows = q.shape[0]
+    lane = lax.broadcasted_iota(jnp.int32, q.shape, 1)
+    row = lax.broadcasted_iota(jnp.int32, (16, rows), 0)
+    go = (g.astype(f32) * o_ref[...].astype(f32)).T
+    k0t = k0_ref[...].T
+    dqs = []
+    for head in range(2):
+        sel = (lane // HD) == head
+        low_row, high_row = head * HD, (head + 1) * HD
+        qm = jnp.where(sel, q, jnp.zeros_like(q))
+        gm = jnp.where(sel, g, jnp.zeros_like(g))
+        lse = lse_ref[0, head : head + 1, :]
+        delta = jnp.sum(go[low_row:high_row], 0, keepdims=True)
+        s = dot_nt(k0_ref[...], qm)
+        p = jnp.where(row == 0, jnp.exp(s - lse), 0.0)
+        ds = (p * (dot_nt(v0_ref[...], gm) - delta)).astype(bf16)
+        dk0a[...] += dot_nn(ds, qm)
+        dv0a[...] += dot_nn(p.astype(bf16), gm)
+        dq = dot_nn(k0t[low_row:high_row], ds)
+        for c in range(count):
+            part = pl.ds(c * chunk, chunk)
+            p = jnp.exp(dot_nt(k_ref[part], qm) - lse)
+            ds = (p * (dot_nt(v_ref[part], gm) - delta)).astype(bf16)
+            dva[part] += dot_nn(p.astype(bf16), gm)
+            dka[part] += dot_nn(ds, qm)
+            dq = dq + dot_nn(kt[low_row:high_row, c * chunk : (c + 1) * chunk], ds)
+        dqs.append(dq)
+    dq = (jnp.concatenate(dqs, 0).T * HD ** (-0.5)).astype(bf16).astype(f32)
+    dq_ref[...] = turn(dq, cos_ref[...], -up_ref[...], -down_ref[...]).astype(bf16)
+
+    @pl.when(i == steps - 1)
+    def _():
+        dk = dka[...].astype(bf16).astype(f32)
+        dk_ref[...] = turn(dk, kcos_ref[...], -kup_ref[...], -kdown_ref[...]).astype(bf16)
+        dv_ref[...] = dva[...].astype(bf16)
+        dk0_ref[...] = dk0a[...]
+        dv0_ref[...] = dv0a[...]
+
+
+def attend_backward(qkv, g, o, lse, k0, v0, tables, block=512, chunk=512):
+    rows = qkv.shape[0]
+    q_spec = pl.BlockSpec((block, 128), lambda j, i: (i, j))
+    table = pl.BlockSpec((block, 128), lambda j, i: (i, 0))
+    whole_table = pl.BlockSpec((rows, 128), lambda j, i: (0, 0))
+    lead = pl.BlockSpec((16, 128), lambda j, i: (0, j))
+
+    def whole(n):
+        return pl.BlockSpec((rows, 128), lambda j, i: (0, n * PAIRS + j))
+
+    return call(
+        functools.partial(
+            attend_back_kernel, chunk=chunk, count=rows // chunk, steps=rows // block
+        ),
+        (PAIRS, rows // block),
+        [
+            q_spec, q_spec, q_spec,
+            pl.BlockSpec((1, 2, block), lambda j, i: (j, 0, i)),
+            table, table, table,
+            whole(1), whole(2), lead, lead,
+            whole_table, whole_table, whole_table,
+        ],
+        [q_spec, whole(0), whole(0), lead, lead],
+        [shape_of((rows, HALF), bf16)] * 3 + [shape_of((16, HALF), f32)] * 2,
+        [
+            pltpu.VMEM((128, rows), bf16),
+            pltpu.VMEM((rows, 128), f32),
+            pltpu.VMEM((rows, 128), f32),
+            pltpu.VMEM((16, 128), f32),
+            pltpu.VMEM((16, 128), f32),
+        ],
+        (32 * rows * rows * HALF, 10 * rows * D * 2),
+        qkv, g, o, lse, *tables, qkv, qkv, k0, v0, *tables,
+    )
+
+
+def prompt_probs(k, qm, mask):
+    s = dot_nt(k, qm) * HD ** (-0.5) + mask
+    e = jnp.exp(s - jnp.max(s, 0, keepdims=True))
+    return e / jnp.sum(e, 0, keepdims=True)
+
+
+def cross_kernel(q_ref, k_ref, v_ref, mask_ref, o_ref):
+    q = q_ref[...]
+    lane = lax.broadcasted_iota(jnp.int32, q.shape, 1)
+    vt = v_ref[...].T
+    outs = []
+    for head in range(2):
+        qm = jnp.where((lane // HD) == head, q, jnp.zeros_like(q))
+        p = prompt_probs(k_ref[...], qm, mask_ref[...])
+        outs.append(dot_nn(vt[head * HD : (head + 1) * HD], p.astype(bf16)))
+    o_ref[...] = jnp.concatenate(outs, 0).T.astype(bf16)
+
+
+def cross_back_kernel(
+    q_ref, g_ref, k_ref, v_ref, mask_ref, dq_ref, dk_ref, dv_ref, dka, dva, *, steps
+):
+    i = pl.program_id(1)
+
+    @pl.when(i == 0)
+    def _():
+        dka[...] = jnp.zeros_like(dka)
+        dva[...] = jnp.zeros_like(dva)
+
+    q = q_ref[...]
+    g = g_ref[...]
+    lane = lax.broadcasted_iota(jnp.int32, q.shape, 1)
+    kt = k_ref[...].T
+    dqs = []
+    for head in range(2):
+        sel = (lane // HD) == head
+        qm = jnp.where(sel, q, jnp.zeros_like(q))
+        gm = jnp.where(sel, g, jnp.zeros_like(g))
+        p = prompt_probs(k_ref[...], qm, mask_ref[...])
+        dp = dot_nt(v_ref[...], gm)
+        ds = (p * (dp - jnp.sum(dp * p, 0, keepdims=True)) * HD ** (-0.5)).astype(bf16)
+        dva[...] += dot_nn(p.astype(bf16), gm)
+        dka[...] += dot_nn(ds, qm)
+        dqs.append(dot_nn(kt[head * HD : (head + 1) * HD], ds))
+    dq_ref[...] = jnp.concatenate(dqs, 0).T.astype(bf16)
+
+    @pl.when(i == steps - 1)
+    def _():
+        dk_ref[...] = dka[...]
+        dv_ref[...] = dva[...]
+
+
+def cross_specs(rows, tokens, block):
+    q_spec = pl.BlockSpec((block, 128), lambda j, i: (i, j))
+    key_spec = pl.BlockSpec((tokens, 128), lambda j, i: (0, j))
+    value_spec = pl.BlockSpec((tokens, 128), lambda j, i: (0, PAIRS + j))
+    mask_spec = pl.BlockSpec((tokens, 1), lambda j, i: (0, 0))
+    return (q_spec, key_spec, value_spec, mask_spec)
+
+
+def cross_forward(q, kv, mask, block=1024):
+    rows, tokens = (q.shape[0], kv.shape[0])
+    q_spec, key_spec, value_spec, mask_spec = cross_specs(rows, tokens, block)
+    return call(
+        cross_kernel,
+        (PAIRS, rows // block),
+        [q_spec, key_spec, value_spec, mask_spec],
+        q_spec,
+        shape_of((rows, HALF), bf16),
+        [],
+        (16 * rows * tokens * HALF, 4 * rows * D),
+        q, kv, kv, mask,
+    )
+
+
+def cross_backward(q, g, kv, mask, block=1024):
+    rows, tokens = (q.shape[0], kv.shape[0])
+    q_spec, key_spec, value_spec, mask_spec = cross_specs(rows, tokens, block)
+    return call(
+        functools.partial(cross_back_kernel, steps=rows // block),
+        (PAIRS, rows // block),
+        [q_spec, q_spec, key_spec, value_spec, mask_spec],
+        [q_spec, key_spec, key_spec],
+        [
+            shape_of((rows, HALF), bf16),
+            shape_of((tokens, HALF), f32),
+            shape_of((tokens, HALF), f32),
+        ],
+        [pltpu.VMEM((tokens, 128), f32), pltpu.VMEM((tokens, 128), f32)],
+        (32 * rows * tokens * HALF, 8 * rows * D),
+        q, g, kv, kv, mask,
+    )
+
+
+def gate_up_kernel(n_ref, wg_ref, wu_ref, hidden_ref, gate_ref, up_ref):
+    n = n_ref[...]
+    gate = dot_nn(n, wg_ref[...])
+    up = dot_nn(n, wu_ref[...])
+    hidden_ref[...] = (gate / (1.0 + jnp.exp(-gate)) * up).astype(bf16)
+    gate_ref[...] = gate.astype(bf16)
+    up_ref[...] = up.astype(bf16)
+
+
+def gate_up(n, w, block=512, columns=512):
+    rows = n.shape[0]
+    count = HIDE // columns
+    out = pl.BlockSpec((block, columns), lambda j, i: (i, j))
+    return call(
+        gate_up_kernel,
+        (count, rows // block),
+        [
+            pl.BlockSpec((block, D), lambda j, i: (i, 0)),
+            pl.BlockSpec((D, columns), lambda j, i: (0, j)),
+            pl.BlockSpec((D, columns), lambda j, i: (0, count + j)),
+        ],
+        [out, out, out],
+        [shape_of((rows, HIDE), bf16)] * 3,
+        [],
+        (4 * rows * D * HIDE, 8 * rows * HIDE + 4 * D * HIDE),
+        n, w, w,
+    )
+
+
+def down_back_kernel(d_ref, w_ref, gate_ref, up_ref, dgate_ref, dup_ref):
+    d = dot_nt(d_ref[...], w_ref[...])
+    gate = gate_ref[...].astype(f32)
+    up = up_ref[...].astype(f32)
+    sig = 1.0 / (1.0 + jnp.exp(-gate))
+    dgate_ref[...] = (d * up * sig * (1.0 + gate * (1.0 - sig))).astype(bf16)
+    dup_ref[...] = (d * gate * sig).astype(bf16)
+
+
+def down_back(d, w, gate, up, block=512, columns=512):
+    rows = d.shape[0]
+    out = pl.BlockSpec((block, columns), lambda j, i: (i, j))
+    return call(
+        down_back_kernel,
+        (HIDE // columns, rows // block),
+        [
+            pl.BlockSpec((block, D), lambda j, i: (i, 0)),
+            pl.BlockSpec((columns, D), lambda j, i: (j, 0)),
+            out,
+            out,
+        ],
+        [out, out],
+        [shape_of((rows, HIDE), bf16)] * 2,
+        [],
+        (2 * rows * D * HIDE, 10 * rows * HIDE + 2 * D * HIDE),
+        d, w, gate, up,
+    )
+
+
+def chip_body(
+    latents, noise_draw, audio_len, bucket, timing, prompt, prompt_len, step_count,
+    edge_weight, edge_first, edge_second,
+    attend_weight, attend_first, attend_second,
+    square_weight, square_first, square_second,
+    cross_weight, cross_first, cross_second,
+    upward_weight, upward_first, upward_second,
+    down_weight, down_first, down_second,
+    gain_weight, gain_first, gain_second,
+    *, planes, chips,
+):
+    peers = ("seq", "z")
+    many = planes * chips
+    groups = latents.shape[0]
+    clips = groups * 2 * planes
+    frames = latents.shape[1] * chips
+    own = frames // 2
+    s_at, z_at, k_at = (lax.axis_index("seq"), lax.axis_index("z"), lax.axis_index("core"))
+    device = (s_at * planes + z_at) * 2 + k_at
+    first_core = k_at == 0
+
+    def swap(x):
+        return lax.ppermute(x, "core", [(0, 1), (1, 0)])
+
+    def across(x, axis, size, bit):
+        return lax.ppermute(x, axis, [(i, i ^ bit) for i in range(size)])
+
+    def bits(size):
+        found = []
+        bit = size // 2
+        while bit:
+            found.append(bit)
+            bit //= 2
+        return found
+
+    hops = [("z", planes, b) for b in bits(planes)] + [("seq", chips, b) for b in bits(chips)]
+
+    def in_order(mine, other, axis=0):
+        return jnp.where(
+            first_core,
+            jnp.concatenate([mine, other], axis),
+            jnp.concatenate([other, mine], axis),
+        )
+
+    def pick(x, index, axis):
+        return lax.dynamic_index_in_dim(x, index, axis, keepdims=False)
+
+    def halves_of(x, view, axis):
+        x = x.reshape(view)
+        rows = view[0]
+        return (
+            pick(x, k_at, axis).reshape(rows, -1),
+            pick(x, 1 - k_at, axis).reshape(rows, -1),
+        )
+
+    rows = attend_weight.shape[0]
+    attend_view = (rows, 3, 2, HALF)
+    square_view = (rows, 3, 2, HALF)
+    cross_view = (cross_weight.shape[0], 2, 2, HALF)
+    up_view = (rows, 2, many, 2, FF // (2 * many))
+    attend16 = attend_weight.astype(bf16)
+    edge16 = jnp.concatenate(
+        [edge_weight[: 2 * C].astype(bf16), gain_weight.astype(bf16)], 0
+    ).T
+    edge16 = jnp.pad(edge16, ((0, 0), (0, 256 - edge16.shape[1])))
+    mine, other = halves_of(attend16, attend_view, 2)
+    mine, other = (jnp.concatenate([mine, edge16], 1), jnp.concatenate([other, edge16], 1))
+    first_group = lax.all_gather(in_order(mine, swap(other)), peers, axis=0, tiled=True)
+    mine, other = halves_of(
+        square_weight[:3].astype(bf16).transpose(1, 0, 2), square_view, 2
+    )
+    square_cols = lax.all_gather(in_order(mine, swap(other)), peers, axis=0, tiled=True)
+    mine, other = halves_of(cross_weight.astype(bf16), cross_view, 2)
+    cross_w = lax.all_gather(in_order(mine, swap(other)), peers, axis=0, tiled=True)
+    mine, other = halves_of(upward_weight.astype(bf16), up_view, 3)
+    up_w = lax.all_gather(in_order(mine, swap(other)), peers, axis=0, tiled=True)
+    down_w = lax.all_gather(down_weight.astype(bf16), peers, axis=0, tiled=True)
+
+    attend_w = first_group[:, : 3 * HALF]
+    w_in_t = first_group[:, 3 * HALF : 3 * HALF + C]
+    w_out_t = first_group[:, 3 * HALF + C : 3 * HALF + 2 * C]
+    norm_gains = first_group[:, 3 * HALF + 2 * C : 3 * HALF + 2 * C + 4].astype(f32).T
+
+    def rows_half(columns):
+        mine_rows = lax.dynamic_slice_in_dim(columns, k_at * HALF, HALF, 0)
+        other_rows = lax.dynamic_slice_in_dim(columns, (1 - k_at) * HALF, HALF, 0)
+        return in_order(mine_rows, swap(other_rows), 1)
+
+    w_o = rows_half(square_cols[:, :HALF])
+    w_cq = square_cols[:, HALF : 2 * HALF]
+    w_co = rows_half(square_cols[:, 2 * HALF :])
+
+    local = jnp.stack(
+        [audio_len, bucket, timing[:, 0], timing[:, 1], prompt_len], 1
+    ).astype(f32)
+    clip_index = jnp.arange(clips)
+    place = (clip_index // groups) == (z_at * 2 + k_at)
+    scalars = jnp.where(place[:, None], jnp.tile(local, (clips // groups, 1)), 0.0)
+    scalars = scalars + swap(scalars)
+    for b in bits(planes):
+        scalars = scalars + across(scalars, "z", planes, b)
+    order = (z_at ^ (clip_index // chips)) * chips + (s_at ^ (clip_index % chips))
+    chosen = order[:, None] == clip_index[None, :]
+    scalars = jnp.sum(jnp.where(chosen[:, :, None], scalars[None], 0.0), 1)
+    lengths = scalars[:, 0]
+    t, keep_rates, noise_rates, clip_weights = plan(scalars[:, 1])
+    weight_sum = jnp.sum(clip_weights * lengths)
+    keep_rate, noise_rate, clip_weight = (keep_rates[0], noise_rates[0], clip_weights[0])
+
+    t_feat = time_features(t).astype(bf16)
+    z_feat = timing_features(scalars[:, 2:4]).astype(bf16)
+    w_t1 = edge_weight[2 * C : 2 * C + TF].astype(bf16)
+    w_t2 = square_weight[3].astype(bf16)
+    w_timing = edge_weight[2 * C + TF :].astype(bf16)
+    t_pre = dot_nn(t_feat, w_t1)
+    t_hidden = jax.nn.silu(t_pre).astype(bf16)
+    lead = lax.dynamic_update_slice(
+        jnp.zeros((clips, D), f32), dot_nn(z_feat, w_timing), (0, device * rows)
+    ) + dot_nn(t_hidden, w_t2)
+    for axis, size, bit in hops:
+        count = lead.shape[0] // 2
+        lead = lead[:count] + across(lead[count:], axis, size, bit)
+    lead = lead + swap(lead)
+    prefix_normed, prefix_std, prefix_dev = layer_normalize(lead, norm_gains[0])
+    n_prefix = jnp.pad(prefix_normed.astype(bf16), ((0, 15), (0, 0)))
+    kv_prefix = dot_nn(n_prefix, attend_w[:, HALF:]).astype(bf16)
+    k0, v0 = (kv_prefix[:, :HALF], kv_prefix[:, HALF:])
+
+    part = s_at // groups
+    member = s_at % groups
+    both = jnp.stack([latents, noise_draw])
+    plane = lax.all_gather(both, ("seq", "core"), axis=0, tiled=False)
+    plane = plane.reshape((chips, 2) + both.shape)
+    plane = pick(pick(plane, part, 1), member, 2)
+    clip = plane.transpose(1, 0, 2, 3).reshape(2, frames, C)
+
+    def mine_first(x, axis):
+        return jnp.concatenate(
+            [
+                lax.dynamic_slice_in_dim(x, k_at * own, own, axis),
+                lax.dynamic_slice_in_dim(x, (1 - k_at) * own, own, axis),
+            ],
+            axis,
+        )
+
+    clip = mine_first(clip, 1).astype(f32)
+    clean, noisy_part = (clip[0], clip[1])
+    frame = jnp.arange(frames)
+    positions = jnp.where(first_core, frame, (frame + own) % frames)
+    row_weight = clip_weight * (positions[:own].astype(f32) < lengths[0]).astype(f32)
+    local_prompt = pick(prompt, member, 0)
+    other_prompt = swap(local_prompt)
+    prompt_low = jnp.where(part == k_at, local_prompt, other_prompt)
+    tokens = prompt_low.shape[0]
+    mask = jnp.where(
+        jnp.arange(tokens)[:, None].astype(f32) < scalars[0, 4], 0.0, -1000000000.0
+    ).astype(f32)
+
+    def shared_sum(product):
+        given = product(1).astype(bf16)
+        return product(0) + swap(given).astype(f32)
+
+    def cut(x, which):
+        return x[which * own : (which + 1) * own]
+
+    def both_halves(x):
+        return jnp.concatenate([x, swap(x)], 0)
+
+    x_in = (keep_rate * clean + noise_rate * noisy_part).astype(bf16)
+    h0 = dot_nt(x_in, w_in_t)
+    n1 = layer_normalize(h0, norm_gains[0])[0].astype(bf16)
+    h0 = h0[:own]
+    tables = turn_tables(positions + 1)
+    qkv = qkv_project(n1, first_group, tables)
+    o, lse = attend_forward(qkv, k0, v0)
+    h1 = h0 + shared_sum(lambda i: dot_nn(cut(o, i), w_o))
+    n2 = both_halves(layer_normalize(h1, norm_gains[1])[0].astype(bf16))
+    cross_q = dot_nn(n2, w_cq).astype(bf16)
+    cross_kv = dot_nn(prompt_low, cross_w).astype(bf16)
+    co = cross_forward(cross_q, cross_kv, mask)
+    h2 = h1 + shared_sum(lambda i: dot_nn(cut(co, i), w_co))
+    n3 = both_halves(layer_normalize(h2, norm_gains[2])[0].astype(bf16))
+    hidden, gate, upper = gate_up(n3, up_w)
+    h3 = h2 + shared_sum(lambda i: dot_nn(cut(hidden, i), down_w))
+    n4, std4, dev4 = layer_normalize(h3, norm_gains[3])
+    n4 = n4.astype(bf16)
+    predicted = dot_nn(n4, w_out_t)
+    target = keep_rate * noisy_part[:own] - noise_rate * clean[:own]
+    error = predicted - target
+    loss_local = jnp.sum(row_weight[:, None] * error * error)
+
+    d_pred = (2.0 / (C * weight_sum) * row_weight[:, None] * error).astype(bf16)
+    g_out_t = dot_tn(n4, d_pred)
+    d_h, gain4 = norm_backward(dot_nt(d_pred, w_out_t), std4, dev4, norm_gains[3])
+    d_f = both_halves(d_h.astype(bf16))
+
+    def scattered(g):
+        return lax.psum_scatter(g.astype(bf16), peers, scatter_dimension=0, tiled=True)
+
+    s_down = scattered(dot_tn(hidden, d_f))
+    d_gate, d_up = down_back(d_f, down_w, gate, upper)
+    s_gate = scattered(dot_tn(n3, d_gate))
+    s_upper = scattered(dot_tn(n3, d_up))
+    d_n3 = shared_sum(
+        lambda i: dot_nt(cut(d_gate, i), up_w[:, :HIDE]) + dot_nt(cut(d_up, i), up_w[:, HIDE:])
+    )
+
+    def norm_again(d_n, h, gain):
+        _, std, dev = layer_normalize(h, gain)
+        return norm_backward(d_n, std, dev, gain)
+
+    d_part, gain3 = norm_again(d_n3, h2, norm_gains[2])
+    d_h = d_h + d_part
+    d_c = both_halves(d_h.astype(bf16))
+    g_co = dot_tn(co, d_c).astype(bf16)
+    d_co = dot_nt(d_c, w_co).astype(bf16)
+    d_cq, d_ck, d_cv = cross_backward(cross_q, d_co, cross_kv, mask)
+    g_cross = dot_tn(prompt_low, jnp.concatenate([d_ck, d_cv], 1).astype(bf16))
+    s_cross = scattered(g_cross)
+    g_cq = dot_tn(n2, d_cq).astype(bf16)
+    d_n2 = shared_sum(lambda i: dot_nt(cut(d_cq, i), w_cq))
+    d_part, gain2 = norm_again(d_n2, h1, norm_gains[1])
+    d_h = d_h + d_part
+    d_a = both_halves(d_h.astype(bf16))
+    g_o = dot_tn(o, d_a).astype(bf16)
+
+    def columns_half(g):
+        kept = lax.dynamic_slice_in_dim(g, k_at * HALF, HALF, 1)
+        given = lax.dynamic_slice_in_dim(g, (1 - k_at) * HALF, HALF, 1)
+        return in_order(kept, swap(given), 0)
+
+    s_square = scattered(jnp.concatenate([columns_half(g_o), g_cq, columns_half(g_co)], 1))
+    d_o = dot_nt(d_a, w_o).astype(bf16)
+    d_q, d_k, d_v, d_k0, d_v0 = attend_backward(qkv, d_o, o, lse, k0, v0, tables)
+    d_projected = jnp.concatenate([d_q, d_k, d_v], 1)
+    d_kv0 = jnp.concatenate([d_k0, d_v0], 1)
+    extra = n_prefix[0].astype(f32)[:, None] * jnp.pad(d_kv0[0], (HALF, 0))[None, :]
+    s_attend = scattered(dot_tn(n1, d_projected) + extra)
+    d_n1 = shared_sum(lambda i: dot_nt(cut(d_projected, i), attend_w))
+    d_part, gain1 = norm_again(d_n1, h0, norm_gains[0])
+    d_h = d_h + d_part
+    g_in_t = dot_tn(d_h.astype(bf16), x_in[:own])
+
+    high = d_kv0.astype(bf16)
+    rest = (d_kv0 - high.astype(f32)).astype(bf16)
+    d_np = dot_nt(jnp.concatenate([high, rest], 0), attend_w[:, HALF:])
+    d_np = d_np[:1] + d_np[16:17]
+    d_np = d_np + swap(d_np)
+    d_lead, prefix_gain = norm_backward(d_np, prefix_std, prefix_dev, norm_gains[0])
+    for axis, size, bit in reversed(hops):
+        d_lead = jnp.concatenate([d_lead, across(d_lead, axis, size, bit)], 0)
+    g_t2 = exact("ge,gd->ed", t_hidden.astype(f32), d_lead)
+    d_lead_here = lax.dynamic_slice(d_lead, (0, device * rows), (clips, rows))
+    g_timing = exact("gz,gd->zd", z_feat.astype(f32), d_lead_here)
+    d_t_hidden = exact("gd,ed->ge", d_lead, w_t2.astype(f32))
+    t_sig = jax.nn.sigmoid(t_pre)
+    d_t_pre = d_t_hidden * t_sig * (1.0 + t_pre * (1.0 - t_sig))
+    g_t1 = exact("gz,gd->zd", t_feat.astype(f32), d_t_pre)
+
+    gains = jnp.stack([gain1 + 0.5 * prefix_gain, gain2, gain3, gain4], 1)
+    s_edge = lax.psum_scatter(
+        jnp.concatenate([g_in_t, g_out_t, gains], 1),
+        ("seq", "z", "core"),
+        scatter_dimension=0,
+        tiled=True,
+    )
+
+    def to_owner(x, view, axis):
+        count = x.shape[0] // 2
+        kept = lax.dynamic_slice_in_dim(x, k_at * count, count, 0)
+        given = lax.dynamic_slice_in_dim(x, (1 - k_at) * count, count, 0)
+        taken = swap(given)
+        shape = view[:axis] + view[axis + 1 :]
+        joined = jnp.where(
+            first_core,
+            jnp.stack([kept.reshape(shape), taken.reshape(shape)], axis),
+            jnp.stack([taken.reshape(shape), kept.reshape(shape)], axis),
+        )
+        return joined.astype(f32)
+
+    g_attend = to_owner(s_attend, attend_view, 2).reshape(rows, 3 * D)
+    g_square = to_owner(s_square, square_view, 2).reshape(rows, 3, D).transpose(1, 0, 2)
+    g_square = jnp.concatenate([g_square, g_t2[None]], 0)
+    g_cross = to_owner(s_cross, cross_view, 2).reshape(cross_view[0], 2 * D)
+    g_up = to_owner(jnp.concatenate([s_gate, s_upper], 1), up_view, 3).reshape(rows, 2 * FF)
+    g_down = s_down.astype(f32)
+    g_edge = jnp.concatenate([s_edge[:, : 2 * C].T, g_t1, g_timing], 0)
+    g_gain = s_edge[:, 2 * C :].T
+    sharded = (g_edge, g_attend, g_square, g_cross, g_up, g_down, g_gain)
+    totals = jnp.stack([sum(jnp.sum(g * g) for g in sharded), loss_local])
+    totals = totals + swap(totals)
+    for axis, size, bit in hops:
+        totals = totals + across(totals, axis, size, bit)
+    grad_norm = jnp.sqrt(totals[0])
+    loss_value = totals[1] / (C * weight_sum)
+    factor = jnp.minimum(1.0, clip_norm / grad_norm)
+    count = step_count[0].astype(f32)
+    first_fix = 1.0 - 0.9**count
+    second_fix = 1.0 - 0.999**count
+    states = (
+        (edge_weight, edge_first, edge_second),
+        (attend_weight, attend_first, attend_second),
+        (square_weight, square_first, square_second),
+        (cross_weight, cross_first, cross_second),
+        (upward_weight, upward_first, upward_second),
+        (down_weight, down_first, down_second),
+        (gain_weight, gain_first, gain_second),
+    )
+    out = [
+        adam(w, m, v, g * factor, first_fix, second_fix)
+        for (w, m, v), g in zip(states, sharded)
+    ]
+    flat = [x for triple in out[:6] for x in triple]
+    return (loss_value, grad_norm, *flat, g_gain * factor, out[6][1], out[6][2])
+
+
 def solution(mesh):
-    return jax.shard_map(
-        body,
-        mesh=mesh,
-        in_specs=(
-            P("dp", "seq", None),
-            P("dp", "seq", None),
-            P("dp"),
-            P("dp"),
-            P("dp", None),
-            P("dp", None, None),
-            P("dp"),
-            P(),
-            P(None, ("seq", "dp")),
-            P(None, ("seq", "dp")),
-            P(None, ("seq", "dp")),
-            P(("seq", "dp"), None),
-            P(("seq", "dp"), None),
-            P(("seq", "dp"), None),
-            P(None, ("seq", "dp"), None),
-            P(None, ("seq", "dp"), None),
-            P(None, ("seq", "dp"), None),
-            P(("seq", "dp"), None),
-            P(("seq", "dp"), None),
-            P(("seq", "dp"), None),
-            P(("seq", "dp"), None),
-            P(("seq", "dp"), None),
-            P(("seq", "dp"), None),
-            P(("seq", "dp"), None),
-            P(("seq", "dp"), None),
-            P(("seq", "dp"), None),
-            P(None, ("seq", "dp")),
-            P(None, ("seq", "dp")),
-            P(None, ("seq", "dp")),
-        ),
-        out_specs=(
-            P(),
-            P(),
-            P(None, ("seq", "dp")),
-            P(None, ("seq", "dp")),
-            P(None, ("seq", "dp")),
-            P(("seq", "dp"), None),
-            P(("seq", "dp"), None),
-            P(("seq", "dp"), None),
-            P(None, ("seq", "dp"), None),
-            P(None, ("seq", "dp"), None),
-            P(None, ("seq", "dp"), None),
-            P(("seq", "dp"), None),
-            P(("seq", "dp"), None),
-            P(("seq", "dp"), None),
-            P(("seq", "dp"), None),
-            P(("seq", "dp"), None),
-            P(("seq", "dp"), None),
-            P(("seq", "dp"), None),
-            P(("seq", "dp"), None),
-            P(("seq", "dp"), None),
-            P(None, ("seq", "dp")),
-            P(None, ("seq", "dp")),
-            P(None, ("seq", "dp")),
-        ),
-        check_vma=False,
-    )
+    chips, spread = (mesh.shape["seq"], mesh.shape["dp"])
+    split_mesh = Mesh(mesh.devices.reshape(chips, spread // 2, 2), ("seq", "z", "core"))
+
+    def whole(*args):
+        groups = args[0].shape[0] // spread
+        one_clip_per_chip = groups * 2 == chips and chips & (chips - 1) == 0
+        if one_clip_per_chip:
+            inner = functools.partial(chip_body, planes=spread // 2, chips=chips)
+            dp, used = ("z", "core"), split_mesh
+        else:
+            inner, dp, used = (general_body, "dp", mesh)
+        every = ("seq",) + (dp if isinstance(dp, tuple) else (dp,))
+        by_row, by_column, by_middle = (P(every, None), P(None, every), P(None, every, None))
+        frames = P(dp, "seq", None)
+        clip = P(dp)
+        kinds = (by_column, by_row, by_middle, by_row, by_row, by_row, by_column)
+        weights = tuple(kind for kind in kinds for _ in range(3))
+        return jax.shard_map(
+            inner,
+            mesh=used,
+            in_specs=(frames, frames, clip, clip, P(dp, None), P(dp, None, None), clip, P())
+            + weights,
+            out_specs=(P(), P()) + weights,
+            check_vma=False,
+        )(*args)
+
+    return whole

time: 4070 us -> 2030 us (0.50)
  matrix products: 1390 us -> 343 us
  waiting for transfers between devices: 1960 us -> 1010 us
  Pallas kernels: 0 us -> 397 us
  other arithmetic: 308 us -> 107 us
  local copies, waits for them, and re-layouts: 261 us -> 104 us
  blocking collectives: 124 us -> 0 us
    dot_general x39 -> x36, matrix products: 1320 us -> 341 us  [the longest x13 136 us: dot_nt(): lax.dot_general(a, b, (((1,), (1,)), ((), ())), preferred_element_type=f32)]
    reduce_scatter x7, waiting for transfers between devices: 1630 us -> 661 us  [the longest x6 560 us: scattered(): lax.psum_scatter(g.astype(bf16), peers, scatter_dimension=0, tiled=True)]
    pallas_call x0 -> x7, Pallas kernels: none -> 397 us  [call(): pl.pallas_call(kernel, grid=grid, in_specs=in_specs, out_specs=out_specs,...]
    another operation x10 -> x7, other arithmetic: 88.8 us -> 7.08 us  [the longest x5 4.62 us: whole(): jax.shard_map(inner, mesh=used, in_specs=(frames, frames, clip, clip, P(d...]
    psum x2 -> x0, blocking collectives: 81 us -> none  [the longest x1 41.1 us: body(): weight_sum = lax.psum(jnp.sum(row_weight), ('seq', 'dp'))]
    ppermute x0 -> x42, waiting for transfers between devices: none -> 73 us  [the longest x28 42.8 us: swap(): return lax.ppermute(x, 'core', [(0, 1), (1, 0)])]
    reduce_sum x9 -> x11, other arithmetic: 77.9 us -> 9.46 us  [the longest x7 7.04 us: chip_body(): totals = jnp.stack([sum((jnp.sum(g * g) for g in sharded)), loss_local])]
    slice x19 -> x11, local copies, waits for them, and re-layouts: 63.5 us -> 5.99 us  [the longest x1 2.69 us: chip_body(): w_co = rows_half(square_cols[:, 2 * HALF:])]
  transfers between devices with their start and end apart: 16 -> 55, of which waited for: 9 -> 37; matrix products, arithmetic and copies ran while one was open for 39% -> 19% of each run, Pallas kernels for 0% -> 16%
where the time goes in v1:
time: 2030 us; the launch traced here: 2020 us
  waiting for transfers between devices  1010 us (50%)
  Pallas kernels  397 us (20%)
  matrix products  343 us (17%)
  other arithmetic  107 us (5%)
  local copies, waits for them, and re-layouts  104 us (5%)
  starting transfers between devices  30.9 us (2%)
  between operations  29 us (1%)
    reduce_scatter x6, waiting for transfers between devices, scattered(): lax.psum_scatter(g.astype(bf16), peers, scatter_dimension=0, tiled=True)  560 us
    pallas_call x7, Pallas kernels, call(): pl.pallas_call(kernel, grid=grid, in_specs=in_specs, out_specs=out_specs,...  397 us
    all_gather x4, waiting for transfers between devices, chip_body(): lax.all_gather(in_order(mine, swap(other)), peers, axis=0, tiled=True)  210 us
    dot_general x13, matrix products, dot_nt(): lax.dot_general(a, b, (((1,), (1,)), ((), ())), preferred_element_type=f32)  136 us
    dot_general x10, matrix products, dot_tn(): lax.dot_general(a, b, (((0,), (0,)), ((), ())), preferred_element_type=f32)  132 us
    reduce_scatter x1, waiting for transfers between devices, chip_body(): lax.psum_scatter(jnp.concatenate([g_in_t, g_out_t, gains], 1), ('seq', 'z...  101 us
    dot_general x13, matrix products, dot_nn(): lax.dot_general(a, b, (((1,), (0,)), ((), ())), preferred_element_type=f32)  73.6 us
    all_gather x1, waiting for transfers between devices, chip_body(): down_w = lax.all_gather(down_weight.astype(bf16), peers, axis=0, tiled=True)  68.4 us
  transfers between devices with their start and end apart: 55, of which 37 were waited for; matrix products, arithmetic and copies ran while one was open for 19% of the time, Pallas kernels for 16%

profile of v1, /device:TPU:0, one launch (start us, length us, event | category | flops | bytes accessed | tf_op | source)
XLA Modules:
  0.0 2023.9 jit_solution(2714370923632119708)
XLA Ops:
  33.9 10.0 dynamic-slice_reduce_fusion.1
  89.5 56.9 %all-gather.10.cloned.1.call-done = bf16[1536,2304]{1,0:T(8,128)(2,1)} async-done(((bf16[96,2304]{1,0:T(8,128)(2,1)}), bf16[1536,2304]{1,0:T(8,128)(2,1)}) %all-gather.10.cloned.1.call-update) | async-done | bytes 7077904 | tf_op jit(solution)/shard_map/all_gather | solution.py:967
  150.6 105.3 %all-gather.8.cloned.1.call-done.w_ref = bf16[1536,2560]{1,0:T(8,128)(2,1)} async-done(((bf16[96,2560]{1,0:T(8,128)(2,1)}), bf16[1536,2560]{1,0:T(8,128)(2,1)}) %all-gather.8.cloned.1.call-update) | async-done | bytes 7864336 | tf_op jit(solution)/shard_map/all_gather | solution.py:963
  256.0 7.3 fusion.167
  263.3 12.6 copy.274
  275.9 6.1 multiply_reduce_fusion
  293.4 29.2 %shard_map.452.q_ref.k_ref.v_ref = bf16[2048,2304]{1,0:T(8,128)(2,1)} custom-call(bf16[2048,1536]{1,0:T(8,128)(2,1)} %multiply_convert_fusion.n_ref, bf16[1536,2560]{1,0:T(8,128)(2,1)} %all-gather.8.cloned.1.call-done.w_ref, f32[2048,128]{1,0:T(8,128)} %broadcast_select_fusion.1.cos_ref.kcos_ref, f32[2048,128]{1,0:T(8,128)} %get-tuple-element.128.up_ref.kup_ref, ...), custom_call_target="tpu_custom_call" | custom-call | flops 14495514624 | bytes 25165824 | tf_op jit(solution)/shard_map/pallas_call | solution.py:526
  322.5 77.4 %shard_map.453 = (bf16[2048,768]{1,0:T(8,128)(2,1)}, f32[6,2,2048]{2,1,0:T(2,128)}) custom-call(bf16[2048,2304]{1,0:T(8,128)(2,1)} %shard_map.452.q_ref.k_ref.v_ref, bf16[2048,2304]{1,0:T(8,128)(2,1)} %shard_map.452.q_ref.k_ref.v_ref, bf16[2048,2304]{1,0:T(8,128)(2,1)} %shard_map.452.q_ref.k_ref.v_ref, bf16[16,768]{1,0:T(8,128)(2,1)} %get-tuple-element.144.k0_ref, ...), custom_call_target="tpu_custom_call" | custom-call | flops 51539607552 | bytes 31457280 | tf_op jit(solution)/shard_map/pallas_call | solution.py:526
  404.9 5.6 collective-permute-done.11
  410.6 6.4 fusion.168
  431.9 10.3 fusion.56.q_ref
  442.2 14.2 shard_map.454
  461.9 5.3 collective-permute-done.16
  474.9 5.3 collective-permute-done.17
  484.9 48.3 %all-gather.14.cloned.1.call-done.wg_ref.wu_ref = bf16[1536,6144]{1,0:T(8,128)(2,1)} async-done(((bf16[96,6144]{1,0:T(8,128)(2,1)}), bf16[1536,6144]{1,0:T(8,128)(2,1)}) %all-gather.14.cloned.1.call-update) | async-done | bytes 18874384 | tf_op jit(solution)/shard_map/all_gather | solution.py:971
  533.2 55.5 %shard_map.455 = (bf16[2048,3072]{1,0:T(8,128)(2,1)}, bf16[2048,3072]{1,0:T(8,128)(2,1)}, bf16[2048,3072]{1,0:T(8,128)(2,1)}) custom-call(bf16[2048,1536]{1,0:T(8,128)(2,1)} %pad_maximum_fusion.2.n_ref, bf16[1536,6144]{1,0:T(8,128)(2,1)} %all-gather.14.cloned.1.call-done.wg_ref.wu_ref, bf16[1536,6144]{1,0:T(8,128)(2,1)} %all-gather.14.cloned.1.call-done.wg_ref.wu_ref), custom_call_target="tpu_custom_call" | custom-call | flops 38654705664 | bytes 69206016 | tf_op jit(solution)/shard_map/pallas_call | solution.py:526
  588.6 68.4 %all-gather.16.cloned.1.call-done.w_ref = bf16[3072,1536]{1,0:T(8,128)(2,1)} async-done(((bf16[192,1536]{1,0:T(8,128)(2,1)}), bf16[3072,1536]{1,0:T(8,128)(2,1)}) %all-gather.16.cloned.1.call-update) | async-done | bytes 9437200 | tf_op jit(solution)/shard_map/all_gather | solution.py:972
  657.0 15.7 fusion.47
  678.6 15.0 fusion.170
  707.7 5.5 collective-permute-done.20
  716.8 47.3 %shard_map.456 = (bf16[2048,3072]{1,0:T(8,128)(2,1)}, bf16[2048,3072]{1,0:T(8,128)(2,1)}) custom-call(bf16[2048,1536]{1,0:T(8,128)(2,1)} %pad_maximum_fusion.3.d_ref, bf16[3072,1536]{1,0:T(8,128)(2,1)} %all-gather.16.cloned.1.call-done.w_ref, bf16[2048,3072]{1,0:T(8,128)(2,1)} %get-tuple-element.40.gate_ref, bf16[2048,3072]{1,0:T(8,128)(2,1)} %get-tuple-element.41.up_ref), custom_call_target="tpu_custom_call" | custom-call | flops 19327352832 | bytes 72351744 | tf_op jit(solution)/shard_map/pallas_call | solution.py:526
  764.1 14.4 fusion.1
  778.4 14.1 add_convert_fusion.1
  792.8 15.5 fusion.3
  808.4 22.0 %multiply_reduce_fusion.2 = (f32[1536]{0:T(1024)}, f32[1024]{0:T(1024)S(1)}, f32[1024]{0:T(1024)S(1)}, f32[1024,1536]{1,0:T(8,128)}) fusion(f32[1024,1536]{1,0:T(8,128)} %copy-done.3, f32[1024]{0:T(1024)S(1)} %copy-done.83, f32[1024]{0:T(1024)S(1)} %copy-done.75, f32[1536]{0:T(1024)S(1)} %copy-done.71, bf16[1024,1536]{1,0:T(8,128)(2,1)S(1)} %collective-permute-done.21, ...), kind=kOutput, calls=%fused_computation.22 | convolution fusion | flops 9680973824 | bytes 37777408 | tf_op jit(solution)/shard_map/dot_general | solution.py:514
  830.4 10.4 fusion.159
  841.2 5.3 collective-permute-done.22
  848.1 8.4 fusion.57.g_ref
  856.6 18.6 shard_map.457
  879.7 25.0 %convolution_convert_fusion.2 = bf16[1536,3072]{1,0:T(8,128)(2,1)} fusion(bf16[2048,3072]{1,0:T(8,128)(2,1)} %get-tuple-element.42, bf16[1024,1536]{1,0:T(8,128)(2,1)} %copy-done.27, bf16[1024,1536]{1,0:T(8,128)(2,1)S(1)} %copy-done.10), kind=kOutput, calls=%fused_computation.6 | convolution fusion | flops 19344654336 | bytes 28311552 | tf_op jit(solution)/shard_map/dot_general | solution.py:522
  910.7 5.3 collective-permute-done.23
  916.1 5.9 multiply_reduce_fusion.3
  927.4 24.0 %convolution_convert_fusion.1 = bf16[1536,3072]{1,0:T(8,128)(2,1)} fusion(bf16[2048,3072]{1,0:T(8,128)(2,1)} %get-tuple-element.43, bf16[1024,1536]{1,0:T(8,128)(2,1)S(1)} %copy-done.28, bf16[1024,1536]{1,0:T(8,128)(2,1)S(1)} %copy-done.11), kind=kOutput, calls=%fused_computation.5 | convolution fusion | flops 19344654336 | bytes 28311552 | tf_op jit(solution)/shard_map/dot_general | solution.py:522
  952.7 10.3 fusion.59.g_ref
  963.1 155.3 %shard_map.458 = (bf16[2048,768]{1,0:T(8,128)(2,1)}, bf16[2048,768]{1,0:T(8,128)(2,1)}, bf16[2048,768]{1,0:T(8,128)(2,1)}, f32[16,768]{1,0:T(8,128)}, f32[16,768]{1,0:T(8,128)}) custom-call(bf16[2048,2304]{1,0:T(8,128)(2,1)} %shard_map.452.q_ref.k_ref.v_ref, bf16[2048,768]{1,0:T(8,128)(2,1)} %fusion.59.g_ref, bf16[2048,768]{1,0:T(8,128)(2,1)} %get-tuple-element.38.o_ref, ...), custom_call_target="tpu_custom_call" | custom-call | flops 103079215104 | bytes 62914560 | tf_op jit(solution)/shard_map/pallas_call | solution.py:526
  1127.8 11.2 fusion.50
  1150.9 15.8 multiply_reduce_fusion.4
  1166.7 6.1 fusion.62
  1174.8 26.2 %convolution_convert_fusion = bf16[3072,1536]{1,0:T(8,128)(2,1)} fusion(bf16[2048,3072]{1,0:T(8,128)(2,1)} %get-tuple-element.39, bf16[1024,1536]{1,0:T(8,128)(2,1)} %copy-done.26, bf16[1024,1536]{1,0:T(8,128)(2,1)} %copy-done.12), kind=kOutput, calls=%fused_computation.3 | convolution fusion | flops 19344654336 | bytes 28311552 | tf_op jit(solution)/shard_map/dot_general | solution.py:522
  1201.7 20.8 %fusion = bf16[1536,2304]{1,0:T(8,128)(2,1)} fusion(bf16[2048,1536]{1,0:T(8,128)(2,1)} %multiply_convert_fusion.n_ref, bf16[2048,2304]{1,0:T(8,128)(2,1)} %constant_dynamic-update-slice_fusion, f32[2304]{0:T(1024)S(1)} %pad.14, f32[1536]{0:T(1024)S(1)} %copy-done.99), kind=kOutput, calls=%fused_computation.4 | convolution fusion | flops 14506131456 | bytes 22821888 | tf_op jit(solution)/shard_map/dot_general | solution.py:522
  1222.6 8.7 fusion.58
  1233.3 8.3 fusion.60
  1243.4 7.3 fusion.55
  1276.9 81.7 %reduce-scatter.18.cloned.1.call-done = bf16[96,3072]{1,0:T(8,128)(2,1)} async-done(((bf16[1536,3072]{1,0:T(8,128)(2,1)}), bf16[96,3072]{1,0:T(8,128)(2,1)}) %reduce-scatter.18.cloned.1.call-update) | async-done | bytes 589840 | tf_op jit(solution)/shard_map/reduce_scatter | solution.py:1093
  1360.2 100.8 %reduce-scatter.22.cloned.1.call-done = f32[48,132]{1,0:T(8,128)} async-done(((f32[1536,132]{1,0:T(8,128)}), f32[48,132]{1,0:T(8,128)}) %reduce-scatter.22.cloned.1.call-update) | async-done | bytes 25360 | tf_op jit(solution)/shard_map/reduce_scatter | solution.py:1156
  1464.7 173.0 %reduce-scatter.20.cloned.1.call-done = bf16[192,1536]{1,0:T(8,128)(2,1)} async-done(((bf16[3072,1536]{1,0:T(8,128)(2,1)}), bf16[192,1536]{1,0:T(8,128)(2,1)}) %reduce-scatter.20.cloned.1.call-update) | async-done | bytes 589840 | tf_op jit(solution)/shard_map/reduce_scatter | solution.py:1093
  1641.9 151.1 %reduce-scatter.10.cloned.1.call-done = bf16[96,2304]{1,0:T(8,128)(2,1)} async-done(((bf16[1536,2304]{1,0:T(8,128)(2,1)}), bf16[96,2304]{1,0:T(8,128)(2,1)}) %reduce-scatter.10.cloned.1.call-update) | async-done | bytes 442384 | tf_op jit(solution)/shard_map/reduce_scatter | solution.py:1093
  1794.2 153.9 %reduce-scatter.12.cloned.1.call-done = bf16[96,2304]{1,0:T(8,128)(2,1)} async-done(((bf16[1536,2304]{1,0:T(8,128)(2,1)}), bf16[96,2304]{1,0:T(8,128)(2,1)}) %reduce-scatter.12.cloned.1.call-update) | async-done | bytes 442384 | tf_op jit(solution)/shard_map/reduce_scatter | solution.py:1093
  (618 shorter events, 287.9 us)
Async XLA Ops:
  7.2 78.5 %all-gather.18.cloned.1.call-start = ((), (), s32[]{:S(2)}) async-start(), calls=%async_computation.18 | async-start | bytes 2359296 | tf_op jit(solution)/shard_map/all_gather | solution.py:1027
  9.0 137.4 %all-gather.10.cloned.1.call-start = ((), (), s32[]{:S(2)}) async-start(), calls=%async_computation.8 | async-start | bytes 7520256 | tf_op jit(solution)/shard_map/all_gather | solution.py:967
  15.1 240.8 %all-gather.8.cloned.1.call-start = ((), (), s32[]{:S(2)}) async-start(), calls=%async_computation.7 | async-start | bytes 8355840 | tf_op jit(solution)/shard_map/all_gather | solution.py:963
  26.0 400.5 %all-gather.12.cloned.1.call-start = ((), (), s32[]{:S(2)}) async-start(), calls=%async_computation.9 | async-start | bytes 2506752 | tf_op jit(solution)/shard_map/all_gather | solution.py:969
  29.3 503.9 %all-gather.14.cloned.1.call-start = ((), (), s32[]{:S(2)}) async-start(), calls=%async_computation.10 | async-start | bytes 20054016 | tf_op jit(solution)/shard_map/all_gather | solution.py:971
  49.0 608.0 %all-gather.16.cloned.1.call-start = ((), (), s32[]{:S(2)}) async-start(), calls=%async_computation.11 | async-start | bytes 10027008 | tf_op jit(solution)/shard_map/all_gather | solution.py:972
  50.8 5.6 collective-permute-start.1
  56.4 3.7 collective-permute-start.2
  63.3 6.1 collective-permute-start.4
  69.3 3.9 collective-permute-start.5
  73.2 3.9 collective-permute-start.6
  77.2 3.8 collective-permute-start.7
  150.6 249.3 %collective-permute-start.10 = (bf16[768,768]{1,0:T(8,128)(2,1)}, bf16[768,768]{1,0:T(8,128)(2,1)}, u32[]{:S(2)}, u32[]{:S(2)}) collective-permute-start(bf16[768,768]{1,0:T(8,128)(2,1)} %get-tuple-element.124), channel_id=1, source_target_pairs={{0,1},{1,0},{2,3},{3,2},{4,5},{5,4},{6,7},{7,6},{8,9},{9,8},{10,11... | collective-permute-start | bytes 3538952 | tf_op jit(solution)/shard_map/ppermute | solution.py:918
  404.9 5.7 collective-permute-start.11
  420.6 11.3 collective-permute-start.12
  421.7 843.4 %reduce-scatter.14.cloned.1.call-start = ((), (), s32[]{:S(2)}) async-start(), calls=%async_computation.14 | async-start | bytes 2506752 | tf_op jit(solution)/shard_map/reduce_scatter | solution.py:1093
  421.8 4.8 collective-permute-start.13
  431.8 24.6 %collective-permute-start.15 = (bf16[768,768]{1,0:T(8,128)(2,1)}, bf16[768,768]{1,0:T(8,128)(2,1)}, u32[]{:S(2)}, u32[]{:S(2)}) collective-permute-start(bf16[768,768]{1,0:T(8,128)(2,1)} %get-tuple-element.122), channel_id=1, source_target_pairs={{0,1},{1,0},{2,3},{3,2},{4,5},{5,4},{6,7},{7,6},{8,9},{9,8},{10,11... | collective-permute-start | bytes 3538952 | tf_op jit(solution)/shard_map/ppermute | solution.py:918
  461.4 5.7 collective-permute-start.16
  474.5 5.7 collective-permute-start.17
  672.7 5.9 collective-permute-start.19
  707.4 5.7 collective-permute-start.20
  792.6 15.7 collective-permute-start.21
  840.8 5.7 collective-permute-start.22
  879.6 396.1 %reduce-scatter.16.cloned.1.call-start = ((), (), s32[]{:S(2)}) async-start(), calls=%async_computation.15 | async-start | bytes 10027008 | tf_op jit(solution)/shard_map/reduce_scatter | solution.py:1093
  904.7 453.8 %reduce-scatter.18.cloned.1.call-start = ((), (), s32[]{:S(2)}) async-start(), calls=%async_computation.16 | async-start | bytes 10027008 | tf_op jit(solution)/shard_map/reduce_scatter | solution.py:1093
  910.3 5.8 collective-permute-start.23
  927.0 24.7 %collective-permute-start.24 = (bf16[1024,1536]{1,0:T(8,128)(2,1)}, bf16[1024,1536]{1,0:T(8,128)(2,1)}, u32[]{:S(2)}, u32[]{:S(2)}) collective-permute-start(bf16[1024,1536]{1,0:T(8,128)(2,1)} %get-tuple-element.103), channel_id=1, source_target_pairs={{0,1},{1,0},{2,3},{3,2},{4,5},{5,4},{6,7},{7,6},{8,9},{9,8},{10,11... | collective-permute-start | bytes 9437192 | tf_op jit(solution)/shard_map/ppermute | solution.py:918
  951.5 509.5 %reduce-scatter.22.cloned.1.call-start = ((), (), s32[]{:S(2)}) async-start(), calls=%async_computation.19 | async-start | bytes 1622016 | tf_op jit(solution)/shard_map/reduce_scatter | solution.py:1156
  1139.0 11.9 collective-permute-start.25
  1143.5 4.6 collective-permute-start.26
  1174.8 462.9 %reduce-scatter.20.cloned.1.call-start = ((), (), s32[]{:S(2)}) async-start(), calls=%async_computation.17 | async-start | bytes 10027008 | tf_op jit(solution)/shard_map/reduce_scatter | solution.py:1093
  1201.1 591.9 %reduce-scatter.10.cloned.1.call-start = ((), (), s32[]{:S(2)}) async-start(), calls=%async_computation.12 | async-start | bytes 7520256 | tf_op jit(solution)/shard_map/reduce_scatter | solution.py:1093
  1222.6 725.5 %reduce-scatter.12.cloned.1.call-start = ((), (), s32[]{:S(2)}) async-start(), calls=%async_computation.13 | async-start | bytes 7520256 | tf_op jit(solution)/shard_map/reduce_scatter | solution.py:1093
  1231.5 19.3 collective-permute-start.33
  1241.7 9.8 collective-permute-start.32
  1257.3 3.7 collective-permute-start.27
  1261.0 3.8 collective-permute-start.28
  1264.8 3.9 collective-permute-start.29
  1266.0 5.2 collective-permute-start.35
  1268.7 5.2 collective-permute-start.30
  1359.8 279.9 %collective-permute-start.36 = (bf16[48,6144]{1,0:T(8,128)(2,1)S(1)}, bf16[48,6144]{1,0:T(8,128)(2,1)}, u32[]{:S(2)}, u32[]{:S(2)}) collective-permute-start(bf16[48,6144]{1,0:T(8,128)(2,1)S(1)} %get-tuple-element.125), channel_id=1, source_target_pairs={{0,1},{1,0},{2,3},{3,2},{4,5},{5,4},{6,7},{7,6},{8,9},{9,8},{10,11... | collective-permute-start | bytes 1769480 | tf_op jit(solution)/shard_map/ppermute | solution.py:918
  1794.1 156.7 %collective-permute-start.31 = (bf16[48,2304]{1,0:T(8,128)(2,1)S(1)}, bf16[48,2304]{1,0:T(8,128)(2,1)}, u32[]{:S(2)}, u32[]{:S(2)}) collective-permute-start(bf16[48,2304]{1,0:T(8,128)(2,1)S(1)} %get-tuple-element.137), channel_id=1, source_target_pairs={{0,1},{1,0},{2,3},{3,2},{4,5},{5,4},{6,7},{7,6},{8,9},{9,8},{10,11... | collective-permute-start | bytes 663560 | tf_op jit(solution)/shard_map/ppermute | solution.py:918
  1949.1 5.0 collective-permute-start.34
  1962.3 4.4 collective-permute-start.38
  1967.4 3.5 collective-permute-start.39
  1971.0 3.5 collective-permute-start.40
  1974.5 3.5 collective-permute-start.41
  (143 other events, 3652.4 us)
Sparse Core Ops, SparseCore 0:
  10.5 30.5 all-gather.17
  44.5 101.8 all-gather.9
  149.7 106.2 all-gather.7
  259.2 60.4 all-gather.11
  322.9 210.2 all-gather.13
  536.4 120.6 all-gather.15
  879.7 125.7 reduce-scatter.13
  1012.2 170.2 reduce-scatter.15
  1188.2 170.3 reduce-scatter.17
  1365.1 95.8 reduce-scatter.21
  1467.6 170.0 reduce-scatter.19
  1642.9 150.0 reduce-scatter.9
  1798.3 149.6 reduce-scatter.11

commit v2 on v1

--- a/solution.py
+++ b/solution.py
@@ -507,7 +507,10 @@
 bf16 = jnp.bfloat16
 HALF = D // 2
 PAIRS = HALF // 128
+TRIO = PAIRS // 2
+THIRD = HALF // 2
 HIDE = FF // 2
+CROSS = 768
 
 
 def dot_nt(a, b):
@@ -556,14 +559,45 @@
     return (cosine, sine_up, sine_down)
 
 
+def start_kernel(x_ref, w_ref, gain_ref, h_ref, n_ref, *, own):
+    h = dot_nt(x_ref[...], w_ref[...])
+    n_ref[...] = layer_normalize(h, gain_ref[...])[0].astype(bf16)
+
+    @pl.when(pl.program_id(0) < own)
+    def _():
+        h_ref[...] = h
+
+
+def start_forward(x, w, gain, block=256):
+    rows = x.shape[0]
+    own = rows // 2 // block
+    return call(
+        functools.partial(start_kernel, own=own),
+        (rows // block,),
+        [
+            pl.BlockSpec((block, 128), lambda i: (i, 0)),
+            pl.BlockSpec((D, 128), lambda i: (0, 3 * PAIRS)),
+            pl.BlockSpec((1, D), lambda i: (0, 0)),
+        ],
+        [
+            pl.BlockSpec((block, D), lambda i: (jnp.minimum(i, own - 1), 0)),
+            pl.BlockSpec((block, D), lambda i: (i, 0)),
+        ],
+        [shape_of((rows // 2, D), f32), shape_of((rows, D), bf16)],
+        [],
+        (2 * rows * D * 128, 4 * rows * D),
+        x, w, gain,
+    )
+
+
 def qkv_kernel(n_ref, w_ref, cos_ref, up_ref, down_ref, out_ref):
-    part = pl.program_id(0)
+    part = pl.program_id(0) % 3
     y = dot_nn(n_ref[...], w_ref[...])
 
     @pl.when(part < 2)
     def _():
         scale = jnp.where(part == 0, HD ** (-0.5), 1.0)
-        for j in range(PAIRS):
+        for j in range(TRIO):
             block = y[:, j * 128 : (j + 1) * 128]
             turned = turn(block, cos_ref[...], up_ref[...], down_ref[...])
             out_ref[:, j * 128 : (j + 1) * 128] = (turned * scale).astype(bf16)
@@ -573,20 +607,20 @@
         out_ref[...] = y.astype(bf16)
 
 
-def qkv_project(n, w, tables, block=512):
+def qkv_project(n, w, tables, block=1024):
     rows = n.shape[0]
     table = pl.BlockSpec((block, 128), lambda p, i: (i, 0))
     return call(
         qkv_kernel,
-        (3, rows // block),
+        (6, rows // block),
         [
             pl.BlockSpec((block, D), lambda p, i: (i, 0)),
-            pl.BlockSpec((D, HALF), lambda p, i: (0, p)),
+            pl.BlockSpec((D, THIRD), lambda p, i: (0, p)),
             table,
             table,
             table,
         ],
-        pl.BlockSpec((block, HALF), lambda p, i: (i, p)),
+        pl.BlockSpec((block, THIRD), lambda p, i: (i, p)),
         shape_of((rows, 3 * HALF), bf16),
         [],
         (2 * rows * D * 3 * HALF, 4 * rows * D * 2),
@@ -621,18 +655,21 @@
     o_ref[...] = jnp.where(lane < HD, outs[0], outs[1]).astype(bf16)
 
 
-def attend_forward(qkv, k0, v0, block=1024, chunk=512):
+def column_of(j, which):
+    return (j // TRIO) * (3 * TRIO) + which * TRIO + j % TRIO
+
+
+def attend_forward(qkv, kv0, block=1024, chunk=1024):
     rows = qkv.shape[0]
-    lead = pl.BlockSpec((16, 128), lambda j, i: (0, j))
     return call(
         functools.partial(attend_kernel, chunk=chunk, count=rows // chunk),
         (PAIRS, rows // block),
         [
-            pl.BlockSpec((block, 128), lambda j, i: (i, j)),
-            pl.BlockSpec((rows, 128), lambda j, i: (0, PAIRS + j)),
-            pl.BlockSpec((rows, 128), lambda j, i: (0, 2 * PAIRS + j)),
-            lead,
-            lead,
+            pl.BlockSpec((block, 128), lambda j, i: (i, column_of(j, 0))),
+            pl.BlockSpec((rows, 128), lambda j, i: (0, column_of(j, 1))),
+            pl.BlockSpec((rows, 128), lambda j, i: (0, column_of(j, 2))),
+            pl.BlockSpec((16, 128), lambda j, i: (0, column_of(j, 1))),
+            pl.BlockSpec((16, 128), lambda j, i: (0, column_of(j, 2))),
         ],
         [
             pl.BlockSpec((block, 128), lambda j, i: (i, j)),
@@ -644,17 +681,19 @@
         qkv,
         qkv,
         qkv,
-        k0,
-        v0,
-    )
-
-
-def attend_back_kernel(
-    q_ref, g_ref, o_ref, lse_ref, cos_ref, up_ref, down_ref,
-    k_ref, v_ref, k0_ref, v0_ref, kcos_ref, kup_ref, kdown_ref,
-    dq_ref, dk_ref, dv_ref, dk0_ref, dv0_ref,
-    kt, dka, dva, dk0a, dv0a, *, chunk, count, steps,
-):
+        kv0,
+        kv0,
+    )
+
+
+def attend_back_kernel(*refs, chunk, count, steps, waits):
+    (
+        q_ref, g_ref, o_ref, lse_ref, cos_ref, up_ref, down_ref,
+        k_ref, v_ref, k0_ref, v0_ref, kcos_ref, kup_ref, kdown_ref,
+    ) = refs[:14]
+    (
+        dq_ref, dk_ref, dv_ref, dk0_ref, dv0_ref, kt, dka, dva, dk0a, dv0a,
+    ) = refs[14 + waits :]
     i = pl.program_id(1)
 
     @pl.when(i == 0)
@@ -706,30 +745,36 @@
         dv0_ref[...] = dv0a[...]
 
 
-def attend_backward(qkv, g, o, lse, k0, v0, tables, block=512, chunk=512):
+def attend_backward(qkv, g, o, lse, kv0, tables, half, after, block=1024, chunk=512):
     rows = qkv.shape[0]
-    q_spec = pl.BlockSpec((block, 128), lambda j, i: (i, j))
+    first = half * TRIO
+    out = pl.BlockSpec((block, 128), lambda j, i: (i, j))
+    head = pl.BlockSpec((block, 128), lambda j, i: (i, first + j))
     table = pl.BlockSpec((block, 128), lambda j, i: (i, 0))
     whole_table = pl.BlockSpec((rows, 128), lambda j, i: (0, 0))
+    whole = pl.BlockSpec((rows, 128), lambda j, i: (0, j))
     lead = pl.BlockSpec((16, 128), lambda j, i: (0, j))
 
-    def whole(n):
-        return pl.BlockSpec((rows, 128), lambda j, i: (0, n * PAIRS + j))
+    def part(size, which):
+        return pl.BlockSpec((size, 128), lambda j, i: (0, column_of(first + j, which)))
 
     return call(
         functools.partial(
-            attend_back_kernel, chunk=chunk, count=rows // chunk, steps=rows // block
+            attend_back_kernel,
+            chunk=chunk, count=rows // chunk, steps=rows // block, waits=len(after),
         ),
-        (PAIRS, rows // block),
+        (TRIO, rows // block),
         [
-            q_spec, q_spec, q_spec,
-            pl.BlockSpec((1, 2, block), lambda j, i: (j, 0, i)),
+            pl.BlockSpec((block, 128), lambda j, i: (i, column_of(first + j, 0))),
+            head, head,
+            pl.BlockSpec((1, 2, block), lambda j, i: (first + j, 0, i)),
             table, table, table,
-            whole(1), whole(2), lead, lead,
+            part(rows, 1), part(rows, 2), part(16, 1), part(16, 2),
             whole_table, whole_table, whole_table,
-        ],
-        [q_spec, whole(0), whole(0), lead, lead],
-        [shape_of((rows, HALF), bf16)] * 3 + [shape_of((16, HALF), f32)] * 2,
+        ]
+        + [pl.BlockSpec(memory_space=pl.ANY)] * len(after),
+        [out, whole, whole, lead, lead],
+        [shape_of((rows, THIRD), bf16)] * 3 + [shape_of((16, THIRD), f32)] * 2,
         [
             pltpu.VMEM((128, rows), bf16),
             pltpu.VMEM((rows, 128), f32),
@@ -737,8 +782,8 @@
             pltpu.VMEM((16, 128), f32),
             pltpu.VMEM((16, 128), f32),
         ],
-        (32 * rows * rows * HALF, 10 * rows * D * 2),
-        qkv, g, o, lse, *tables, qkv, qkv, k0, v0, *tables,
+        (16 * rows * rows * HALF, 5 * rows * D * 2),
+        qkv, g, o, lse, *tables, qkv, qkv, kv0, kv0, *tables, *after,
     )
 
 
@@ -864,16 +909,18 @@
     )
 
 
-def down_back_kernel(d_ref, w_ref, gate_ref, up_ref, dgate_ref, dup_ref):
-    d = dot_nt(d_ref[...], w_ref[...])
-    gate = gate_ref[...].astype(f32)
-    up = up_ref[...].astype(f32)
-    sig = 1.0 / (1.0 + jnp.exp(-gate))
-    dgate_ref[...] = (d * up * sig * (1.0 + gate * (1.0 - sig))).astype(bf16)
-    dup_ref[...] = (d * gate * sig).astype(bf16)
-
-
-def down_back(d, w, gate, up, block=512, columns=512):
+def down_back_kernel(d_ref, w_ref, gate_ref, up_ref, after_ref, dgate_ref, dup_ref):
+    for part in range(0, w_ref.shape[0], 256):
+        cols = slice(part, part + 256)
+        d = dot_nt(d_ref[...], w_ref[cols])
+        gate = gate_ref[:, cols].astype(f32)
+        sig = 1.0 / (1.0 + jnp.exp(-gate))
+        d_sig = d * sig
+        dgate_ref[:, cols] = (d_sig * up_ref[:, cols] * (1.0 + gate * (1.0 - sig))).astype(bf16)
+        dup_ref[:, cols] = (d_sig * gate).astype(bf16)
+
+
+def down_back(d, w, gate, up, after, block=512, columns=1024):
     rows = d.shape[0]
     out = pl.BlockSpec((block, columns), lambda j, i: (i, j))
     return call(
@@ -884,12 +931,13 @@
             pl.BlockSpec((columns, D), lambda j, i: (j, 0)),
             out,
             out,
+            pl.BlockSpec(memory_space=pl.ANY),
         ],
         [out, out],
         [shape_of((rows, HIDE), bf16)] * 2,
         [],
         (2 * rows * D * HIDE, 10 * rows * HIDE + 2 * D * HIDE),
-        d, w, gate, up,
+        d, w, gate, up, after,
     )
 
 
@@ -949,24 +997,28 @@
         )
 
     rows = attend_weight.shape[0]
-    attend_view = (rows, 3, 2, HALF)
+    attend_view = (rows, 2, 3, 2, THIRD)
     square_view = (rows, 3, 2, HALF)
     cross_view = (cross_weight.shape[0], 2, 2, HALF)
     up_view = (rows, 2, many, 2, FF // (2 * many))
-    attend16 = attend_weight.astype(bf16)
+    attend16 = attend_weight.astype(bf16).reshape(rows, 3, 2, 2, THIRD).transpose(0, 3, 1, 2, 4)
     edge16 = jnp.concatenate(
         [edge_weight[: 2 * C].astype(bf16), gain_weight.astype(bf16)], 0
     ).T
     edge16 = jnp.pad(edge16, ((0, 0), (0, 256 - edge16.shape[1])))
-    mine, other = halves_of(attend16, attend_view, 2)
+    mine, other = halves_of(attend16, attend_view, 3)
     mine, other = (jnp.concatenate([mine, edge16], 1), jnp.concatenate([other, edge16], 1))
     first_group = lax.all_gather(in_order(mine, swap(other)), peers, axis=0, tiled=True)
     mine, other = halves_of(
         square_weight[:3].astype(bf16).transpose(1, 0, 2), square_view, 2
     )
-    square_cols = lax.all_gather(in_order(mine, swap(other)), peers, axis=0, tiled=True)
+    square_mine = in_order(mine, swap(other))
     mine, other = halves_of(cross_weight.astype(bf16), cross_view, 2)
-    cross_w = lax.all_gather(in_order(mine, swap(other)), peers, axis=0, tiled=True)
+    cross_mine = in_order(mine, swap(other))
+    cross_mine = jnp.concatenate([cross_mine[:, :HALF], cross_mine[:, HALF:]], 0)
+    square_cols = lax.all_gather(
+        jnp.concatenate([square_mine, cross_mine], 1), peers, axis=0, tiled=True
+    )
     mine, other = halves_of(upward_weight.astype(bf16), up_view, 3)
     up_w = lax.all_gather(in_order(mine, swap(other)), peers, axis=0, tiled=True)
     down_w = lax.all_gather(down_weight.astype(bf16), peers, axis=0, tiled=True)
@@ -980,10 +1032,6 @@
         mine_rows = lax.dynamic_slice_in_dim(columns, k_at * HALF, HALF, 0)
         other_rows = lax.dynamic_slice_in_dim(columns, (1 - k_at) * HALF, HALF, 0)
         return in_order(mine_rows, swap(other_rows), 1)
-
-    w_o = rows_half(square_cols[:, :HALF])
-    w_cq = square_cols[:, HALF : 2 * HALF]
-    w_co = rows_half(square_cols[:, 2 * HALF :])
 
     local = jnp.stack(
         [audio_len, bucket, timing[:, 0], timing[:, 1], prompt_len], 1
@@ -1018,30 +1066,28 @@
     lead = lead + swap(lead)
     prefix_normed, prefix_std, prefix_dev = layer_normalize(lead, norm_gains[0])
     n_prefix = jnp.pad(prefix_normed.astype(bf16), ((0, 15), (0, 0)))
-    kv_prefix = dot_nn(n_prefix, attend_w[:, HALF:]).astype(bf16)
-    k0, v0 = (kv_prefix[:, :HALF], kv_prefix[:, HALF:])
+    kv_prefix = dot_nn(n_prefix, attend_w).astype(bf16)
 
     part = s_at // groups
     member = s_at % groups
     both = jnp.stack([latents, noise_draw])
-    plane = lax.all_gather(both, ("seq", "core"), axis=0, tiled=False)
-    plane = plane.reshape((chips, 2) + both.shape)
-    plane = pick(pick(plane, part, 1), member, 2)
-    clip = plane.transpose(1, 0, 2, 3).reshape(2, frames, C)
+    blocks = [pick(both, member, 1)]
+    for offset in range(1, chips):
+        given = pick(both, (s_at ^ offset) % groups, 1)
+        blocks.append(across(given, "seq", chips, offset))
+    blocks = jnp.stack(blocks, 1)
+    blocks = jnp.where(part == k_at, blocks, swap(blocks))
+    seen = s_at ^ jnp.arange(chips)
 
     def mine_first(x, axis):
-        return jnp.concatenate(
-            [
-                lax.dynamic_slice_in_dim(x, k_at * own, own, axis),
-                lax.dynamic_slice_in_dim(x, (1 - k_at) * own, own, axis),
-            ],
-            axis,
-        )
-
-    clip = mine_first(clip, 1).astype(f32)
+        low_half, high_half = jnp.split(x, 2, axis)
+        return in_order(low_half, high_half, axis)
+
+    clip = mine_first(blocks, 1).reshape(2, frames, C).astype(f32)
     clean, noisy_part = (clip[0], clip[1])
-    frame = jnp.arange(frames)
-    positions = jnp.where(first_core, frame, (frame + own) % frames)
+    positions = (
+        mine_first(seen, 0)[:, None] * latents.shape[1] + jnp.arange(latents.shape[1])
+    ).reshape(frames)
     row_weight = clip_weight * (positions[:own].astype(f32) < lengths[0]).astype(f32)
     local_prompt = pick(prompt, member, 0)
     other_prompt = swap(local_prompt)
@@ -1062,12 +1108,24 @@
         return jnp.concatenate([x, swap(x)], 0)
 
     x_in = (keep_rate * clean + noise_rate * noisy_part).astype(bf16)
-    h0 = dot_nt(x_in, w_in_t)
-    n1 = layer_normalize(h0, norm_gains[0])[0].astype(bf16)
-    h0 = h0[:own]
+    x_wide = jnp.pad(x_in, ((0, 0), (0, C)))
+    h0, n1 = start_forward(x_wide, first_group, norm_gains[:1])
     tables = turn_tables(positions + 1)
     qkv = qkv_project(n1, first_group, tables)
-    o, lse = attend_forward(qkv, k0, v0)
+    o, lse = attend_forward(qkv, kv_prefix)
+
+    def tie(x):
+        return x[0, 0].astype(f32) * 0.0
+
+    square_cols = square_cols[:] + tie(o).astype(bf16)
+    cross_w = square_cols[:, 3 * HALF :].reshape(many, 2, CROSS // many, HALF)
+    cross_w = jnp.concatenate(
+        [cross_w[:, 0].reshape(CROSS, HALF), cross_w[:, 1].reshape(CROSS, HALF)], 1
+    )
+    w_o = rows_half(square_cols[:, :HALF])
+    w_cq = square_cols[:, HALF : 2 * HALF]
+    w_co = rows_half(square_cols[:, 2 * HALF : 3 * HALF])
+
     h1 = h0 + shared_sum(lambda i: dot_nn(cut(o, i), w_o))
     n2 = both_halves(layer_normalize(h1, norm_gains[1])[0].astype(bf16))
     cross_q = dot_nn(n2, w_cq).astype(bf16)
@@ -1089,13 +1147,68 @@
     d_h, gain4 = norm_backward(dot_nt(d_pred, w_out_t), std4, dev4, norm_gains[3])
     d_f = both_halves(d_h.astype(bf16))
 
-    def scattered(g):
-        return lax.psum_scatter(g.astype(bf16), peers, scatter_dimension=0, tiled=True)
-
-    s_down = scattered(dot_tn(hidden, d_f))
-    d_gate, d_up = down_back(d_f, down_w, gate, upper)
-    s_gate = scattered(dot_tn(n3, d_gate))
-    s_upper = scattered(dot_tn(n3, d_up))
+    y_at, x_at = (s_at // 2, s_at % 2)
+
+    def half_at(x, at, size):
+        return lax.dynamic_slice_in_dim(x, at * size, size, 0)
+
+    class Scatter:
+        def __init__(self, product, depth, y_first):
+            self.product, self.quarter, self.y_first = (product, depth // chips, y_first)
+            self.bit, self.later, self.at = (2, 1, x_at) if y_first else (1, 2, y_at)
+            given = product(lambda x, axis: self.rows_at(x, axis, True)).astype(bf16)
+            self.sent = [given]
+            self.taken = across(given, "seq", chips, self.bit)
+
+        def rows_at(self, x, axis, flip):
+            quarter = self.quarter
+
+            def block(at):
+                return lax.dynamic_slice_in_dim(x, at * quarter, quarter, axis)
+
+            if self.y_first:
+                row = (1 - y_at if flip else y_at) * 2
+                return lax.dynamic_slice_in_dim(x, row * quarter, 2 * quarter, axis)
+            column = 1 - x_at if flip else x_at
+            return jnp.concatenate([block(column), block(2 + column)], axis)
+
+        def second(self, behind=0.0):
+            own_part = self.product(lambda x, axis: self.rows_at(x, axis, False))
+            kept = (own_part + self.taken.astype(f32) + behind).astype(bf16)
+            given = half_at(kept, 1 - self.at, self.quarter)
+            self.kept = half_at(kept, self.at, self.quarter)
+            self.sent = [given]
+            self.taken = across(given, "seq", chips, self.later)
+            return self
+
+        def third(self, behind=0.0):
+            kept = (self.kept.astype(f32) + self.taken.astype(f32) + behind).astype(bf16)
+            size = self.quarter // planes
+            self.kept = half_at(kept, z_at, size)
+            self.sent = [half_at(kept, z_at ^ offset, size) for offset in range(1, planes)]
+            self.taken = [
+                across(given, "z", planes, offset)
+                for offset, given in enumerate(self.sent, 1)
+            ]
+            return self
+
+        def total(self, behind=0.0):
+            return self.kept.astype(f32) + sum(x.astype(f32) for x in self.taken) + behind
+
+    def scattered(product, depth, y_first):
+        return Scatter(product, depth, y_first).second().third().total()
+
+    def gradient(left, right, y_first):
+        return Scatter(lambda cut_of: dot_tn(cut_of(left, 1), right), left.shape[1], y_first)
+
+    def gathered_sum(g):
+        return lax.psum_scatter(g, peers, scatter_dimension=0, tiled=True)
+
+    g_down = dot_tn(hidden, d_f).astype(bf16)
+    s_down = gathered_sum(g_down)
+    d_gate, d_up = down_back(d_f, down_w, gate, upper, g_down)
+    s_gate = gathered_sum(dot_tn(n3, d_gate).astype(bf16))
+    s_upper = gathered_sum(dot_tn(n3, d_up).astype(bf16))
     d_n3 = shared_sum(
         lambda i: dot_nt(cut(d_gate, i), up_w[:, :HIDE]) + dot_nt(cut(d_up, i), up_w[:, HIDE:])
     )
@@ -1110,9 +1223,8 @@
     g_co = dot_tn(co, d_c).astype(bf16)
     d_co = dot_nt(d_c, w_co).astype(bf16)
     d_cq, d_ck, d_cv = cross_backward(cross_q, d_co, cross_kv, mask)
-    g_cross = dot_tn(prompt_low, jnp.concatenate([d_ck, d_cv], 1).astype(bf16))
-    s_cross = scattered(g_cross)
-    g_cq = dot_tn(n2, d_cq).astype(bf16)
+    r_cross = gradient(prompt_low, jnp.concatenate([d_ck, d_cv], 1).astype(bf16), False)
+    r_cq = gradient(n2, d_cq, False)
     d_n2 = shared_sum(lambda i: dot_nt(cut(d_cq, i), w_cq))
     d_part, gain2 = norm_again(d_n2, h1, norm_gains[1])
     d_h = d_h + d_part
@@ -1124,21 +1236,49 @@
         given = lax.dynamic_slice_in_dim(g, (1 - k_at) * HALF, HALF, 1)
         return in_order(kept, swap(given), 0)
 
-    s_square = scattered(jnp.concatenate([columns_half(g_o), g_cq, columns_half(g_co)], 1))
+    side = jnp.concatenate([columns_half(g_o), columns_half(g_co)], 1)
+    r_side = Scatter(lambda cut_of: cut_of(side, 0).astype(f32), D, True)
     d_o = dot_nt(d_a, w_o).astype(bf16)
-    d_q, d_k, d_v, d_k0, d_v0 = attend_backward(qkv, d_o, o, lse, k0, v0, tables)
-    d_projected = jnp.concatenate([d_q, d_k, d_v], 1)
-    d_kv0 = jnp.concatenate([d_k0, d_v0], 1)
-    extra = n_prefix[0].astype(f32)[:, None] * jnp.pad(d_kv0[0], (HALF, 0))[None, :]
-    s_attend = scattered(dot_tn(n1, d_projected) + extra)
-    d_n1 = shared_sum(lambda i: dot_nt(cut(d_projected, i), attend_w))
+    lead_column = n_prefix[:1].astype(f32)
+
+    def attend_half(half, after):
+        d_q, d_k, d_v, d_k0, d_v0 = attend_backward(qkv, d_o, o, lse, kv_prefix, tables, half, after)
+        lead_row = jnp.concatenate([jnp.zeros_like(d_k0), d_k0, d_v0], 1)
+        return (jnp.concatenate([d_q, d_k, d_v], 1), lead_row, tie(d_q))
+
+    def attend_gradient(right, lead_row, y_first):
+        def product(cut_of):
+            return dot_tn(cut_of(n1, 1), right) + cut_of(lead_column, 1).T * lead_row[:1]
+
+        return Scatter(product, D, y_first)
+
+    after = [x for r in (r_cross, r_cq, r_side) for x in r.sent]
+    d_first, lead_first, behind_first = attend_half(0, after)
+    r_first = attend_gradient(d_first, lead_first, True)
+    for r in (r_cross, r_cq, r_side):
+        r.second(behind_first)
+    after = [x for r in (r_cross, r_cq, r_side, r_first) for x in r.sent]
+    d_second, lead_second, behind_second = attend_half(1, after)
+    edge_at = 5 * 128
+    r_second = attend_gradient(d_second[:, :edge_at], lead_second[:, :edge_at], True)
+    r_last = attend_gradient(d_second[:, edge_at:], lead_second[:, edge_at:], False)
+    for r in (r_first, r_second, r_last):
+        r.second(behind_second)
+    d_n1 = shared_sum(
+        lambda i: dot_nt(cut(d_first, i), attend_w[:, : 3 * THIRD])
+        + dot_nt(cut(d_second, i), attend_w[:, 3 * THIRD :])
+    )
     d_part, gain1 = norm_again(d_n1, h0, norm_gains[0])
     d_h = d_h + d_part
     g_in_t = dot_tn(d_h.astype(bf16), x_in[:own])
+    s_cross, s_cq, s_side = (r.third(behind_second).total() for r in (r_cross, r_cq, r_side))
+    s_square = jnp.concatenate([s_side[:, :HALF], s_cq, s_side[:, HALF:]], 1)
+    s_attend = jnp.concatenate([r.third().total() for r in (r_first, r_second, r_last)], 1)
+    d_kv0 = jnp.concatenate([lead_first, lead_second], 1)
 
     high = d_kv0.astype(bf16)
     rest = (d_kv0 - high.astype(f32)).astype(bf16)
-    d_np = dot_nt(jnp.concatenate([high, rest], 0), attend_w[:, HALF:])
+    d_np = dot_nt(jnp.concatenate([high, rest], 0), attend_w)
     d_np = d_np[:1] + d_np[16:17]
     d_np = d_np + swap(d_np)
     d_lead, prefix_gain = norm_backward(d_np, prefix_std, prefix_dev, norm_gains[0])
@@ -1152,35 +1292,34 @@
     d_t_pre = d_t_hidden * t_sig * (1.0 + t_pre * (1.0 - t_sig))
     g_t1 = exact("gz,gd->zd", t_feat.astype(f32), d_t_pre)
 
-    gains = jnp.stack([gain1 + 0.5 * prefix_gain, gain2, gain3, gain4], 1)
-    s_edge = lax.psum_scatter(
-        jnp.concatenate([g_in_t, g_out_t, gains], 1),
-        ("seq", "z", "core"),
-        scatter_dimension=0,
-        tiled=True,
-    )
-
     def to_owner(x, view, axis):
         count = x.shape[0] // 2
         kept = lax.dynamic_slice_in_dim(x, k_at * count, count, 0)
         given = lax.dynamic_slice_in_dim(x, (1 - k_at) * count, count, 0)
-        taken = swap(given)
+        taken = swap(given.astype(bf16)).astype(f32)
         shape = view[:axis] + view[axis + 1 :]
         joined = jnp.where(
             first_core,
             jnp.stack([kept.reshape(shape), taken.reshape(shape)], axis),
             jnp.stack([taken.reshape(shape), kept.reshape(shape)], axis),
         )
-        return joined.astype(f32)
-
-    g_attend = to_owner(s_attend, attend_view, 2).reshape(rows, 3 * D)
+        return joined
+
+    gains = jnp.stack([gain1 + 0.5 * prefix_gain, gain2, gain3, gain4], 1)
+    edges = jnp.concatenate([g_in_t, g_out_t], 1)
+    gains = jnp.pad(gains, ((0, 0), (0, 128 - gains.shape[1])))
+    edges = jnp.where(first_core, edges, gains) + swap(jnp.where(first_core, gains, edges))
+    s_edge = scattered(lambda cut_of: cut_of(edges, 0), D, True)
+    s_edge = to_owner(s_edge, (rows, 2, 128), 1).reshape(rows, 256)
+
+    g_attend = to_owner(s_attend, attend_view, 3).transpose(0, 2, 3, 1, 4).reshape(rows, 3 * D)
     g_square = to_owner(s_square, square_view, 2).reshape(rows, 3, D).transpose(1, 0, 2)
     g_square = jnp.concatenate([g_square, g_t2[None]], 0)
     g_cross = to_owner(s_cross, cross_view, 2).reshape(cross_view[0], 2 * D)
-    g_up = to_owner(jnp.concatenate([s_gate, s_upper], 1), up_view, 3).reshape(rows, 2 * FF)
+    g_up = to_owner(jnp.concatenate([s_gate, s_upper], 1).astype(f32), up_view, 3).reshape(rows, 2 * FF)
     g_down = s_down.astype(f32)
     g_edge = jnp.concatenate([s_edge[:, : 2 * C].T, g_t1, g_timing], 0)
-    g_gain = s_edge[:, 2 * C :].T
+    g_gain = s_edge[:, 2 * C : 2 * C + 4].T
     sharded = (g_edge, g_attend, g_square, g_cross, g_up, g_down, g_gain)
     totals = jnp.stack([sum(jnp.sum(g * g) for g in sharded), loss_local])
     totals = totals + swap(totals)
@@ -1215,7 +1354,7 @@
 
     def whole(*args):
         groups = args[0].shape[0] // spread
-        one_clip_per_chip = groups * 2 == chips and chips & (chips - 1) == 0
+        one_clip_per_chip = groups * 2 == chips == 4 and spread & (spread - 1) == 0
         if one_clip_per_chip:
             inner = functools.partial(chip_body, planes=spread // 2, chips=chips)
             dp, used = ("z", "core"), split_mesh

time: 2030 us -> 1530 us (0.75)
  waiting for transfers between devices: 1010 us -> 383 us
  starting transfers between devices: 30.9 us -> 89.9 us
  other arithmetic: 107 us -> 135 us
    reduce_scatter x7 -> x3, waiting for transfers between devices: 661 us -> 0.01 us  [gathered_sum(): return lax.psum_scatter(g, peers, scatter_dimension=0, tiled=True)]
    ppermute x14 -> x52, waiting for transfers between devices: 30.2 us -> 121 us  [across(): return lax.ppermute(x, axis, [(i, i ^ bit) for i in range(size)])]
    ppermute x14 -> x52, starting transfers between devices: 22.8 us -> 82.4 us  [across(): return lax.ppermute(x, axis, [(i, i ^ bit) for i in range(size)])]
    all_gather x4 -> x2, waiting for transfers between devices: 210 us -> 153 us  [chip_body(): lax.all_gather(in_order(mine, swap(other)), peers, axis=0, tiled=True)]
    dot_general x10 -> x17, matrix products: 132 us -> 145 us  [dot_tn(): lax.dot_general(a, b, (((0,), (0,)), ((), ())), preferred_element_type=f32)]
    dot_general x13 -> x14, matrix products: 136 us -> 144 us  [dot_nt(): lax.dot_general(a, b, (((1,), (1,)), ((), ())), preferred_element_type=f32)]
    ppermute x28 -> x31, waiting for transfers between devices: 42.8 us -> 40.4 us  [swap(): return lax.ppermute(x, 'core', [(0, 1), (1, 0)])]
    pallas_call x7 -> x9, Pallas kernels: 397 us -> 400 us  [call(): pl.pallas_call(kernel, grid=grid, in_specs=in_specs, out_specs=out_specs,...]
  transfers between devices with their start and end apart: 55 -> 90, of which waited for: 37 -> 42; matrix products, arithmetic and copies ran while one was open for 19% -> 29% of each run, Pallas kernels for 16% -> 24%
where the time goes in v2:
time: 1530 us; the launch traced here: 1520 us
  Pallas kernels  400 us (26%)
  waiting for transfers between devices  383 us (25%)
  matrix products  361 us (24%)
  other arithmetic  135 us (9%)
  local copies, waits for them, and re-layouts  123 us (8%)
  starting transfers between devices  89.9 us (6%)
  between operations  32.1 us (2%)
    pallas_call x9, Pallas kernels, call(): pl.pallas_call(kernel, grid=grid, in_specs=in_specs, out_specs=out_specs,...  400 us
    all_gather x2, waiting for transfers between devices, chip_body(): lax.all_gather(in_order(mine, swap(other)), peers, axis=0, tiled=True)  153 us
    dot_general x17, matrix products, dot_tn(): lax.dot_general(a, b, (((0,), (0,)), ((), ())), preferred_element_type=f32)  145 us
    dot_general x14, matrix products, dot_nt(): lax.dot_general(a, b, (((1,), (1,)), ((), ())), preferred_element_type=f32)  144 us
    ppermute x52, waiting for transfers between devices, across(): return lax.ppermute(x, axis, [(i, i ^ bit) for i in range(size)])  121 us
    ppermute x52, starting transfers between devices, across(): return lax.ppermute(x, axis, [(i, i ^ bit) for i in range(size)])  82.4 us
    dot_general x13, matrix products, dot_nn(): lax.dot_general(a, b, (((1,), (0,)), ((), ())), preferred_element_type=f32)  68.9 us
    all_gather x1, waiting for transfers between devices, chip_body(): down_w = lax.all_gather(down_weight.astype(bf16), peers, axis=0, tiled=True)  68.4 us
  transfers between devices with their start and end apart: 90, of which 42 were waited for; matrix products, arithmetic and copies ran while one was open for 29% of the time, Pallas kernels for 24%

profile of v2, /device:TPU:0, one launch (start us, length us, event | category | flops | bytes accessed | tf_op | source)
XLA Modules:
  0.0 1522.5 jit_solution(8192443976124817682)
XLA Ops:
  21.8 10.0 dynamic-slice_reduce_fusion.1
  83.2 44.5 %all-gather.5.cloned.1.call-done.w_ref = bf16[1536,2560]{1,0:T(8,128)(2,1)} async-done(((bf16[96,2560]{1,0:T(8,128)(2,1)}), bf16[1536,2560]{1,0:T(8,128)(2,1)}) %all-gather.5.cloned.1.call-update) | async-done | bytes 7864336 | tf_op jit(solution)/shard_map/all_gather | solution.py:1011
  132.8 10.2 shard_map.452
  147.7 36.2 %shard_map.453.q_ref.k_ref.v_ref.refs_0_.refs_7_.refs_8_ = bf16[2048,2304]{1,0:T(8,128)(2,1)} custom-call(bf16[2048,1536]{1,0:T(8,128)(2,1)} %get-tuple-element.46.n_ref, bf16[1536,2560]{1,0:T(8,128)(2,1)} %all-gather.5.cloned.1.call-done.w_ref, f32[2048,128]{1,0:T(8,128)} %broadcast_select_fusion.1.cos_ref.refs_4_.refs_11_, ...), custom_call_target="tpu_custom_call" | custom-call | flops 14495514624 | bytes 25165824 | tf_op jit(solution)/shard_map/pallas_call | solution.py:529
  183.9 73.2 %shard_map.454 = (bf16[2048,768]{1,0:T(8,128)(2,1)}, f32[6,2,2048]{2,1,0:T(2,128)}) custom-call(bf16[2048,2304]{1,0:T(8,128)(2,1)} %shard_map.453.q_ref.k_ref.v_ref.refs_0_.refs_7_.refs_8_, bf16[2048,2304]{1,0:T(8,128)(2,1)} %shard_map.453.q_ref.k_ref.v_ref.refs_0_.refs_7_.refs_8_, bf16[2048,2304]{1,0:T(8,128)(2,1)} %shard_map.453.q_ref.k_ref.v_ref.refs_0_.refs_7_.refs_8_, ...), custom_call_target="tpu_custom_call" | custom-call | flops 51539607552 | bytes 31457280 | tf_op jit(solution)/shard_map/pallas_call | solution.py:529
  259.0 8.7 broadcast_add_fusion
  267.7 5.8 fusion.216
  303.1 9.4 fusion.42.q_ref
  312.5 14.0 shard_map.455
  355.8 109.0 %all-gather.9.cloned.1.call-done.wg_ref.wu_ref = bf16[1536,6144]{1,0:T(8,128)(2,1)} async-done(((bf16[96,6144]{1,0:T(8,128)(2,1)}), bf16[1536,6144]{1,0:T(8,128)(2,1)}) %all-gather.9.cloned.1.call-update) | async-done | bytes 18874384 | tf_op jit(solution)/shard_map/all_gather | solution.py:1023
  464.8 55.5 %shard_map.456 = (bf16[2048,3072]{1,0:T(8,128)(2,1)}, bf16[2048,3072]{1,0:T(8,128)(2,1)}, bf16[2048,3072]{1,0:T(8,128)(2,1)}) custom-call(bf16[2048,1536]{1,0:T(8,128)(2,1)} %pad_maximum_fusion.2.n_ref, bf16[1536,6144]{1,0:T(8,128)(2,1)} %all-gather.9.cloned.1.call-done.wg_ref.wu_ref, bf16[1536,6144]{1,0:T(8,128)(2,1)} %all-gather.9.cloned.1.call-done.wg_ref.wu_ref), custom_call_target="tpu_custom_call" | custom-call | flops 38654705664 | bytes 69206016 | tf_op jit(solution)/shard_map/pallas_call | solution.py:529
  520.3 68.4 %all-gather.11.cloned.1.call-done.w_ref = bf16[3072,1536]{1,0:T(8,128)(2,1)} async-done(((bf16[192,1536]{1,0:T(8,128)(2,1)}), bf16[3072,1536]{1,0:T(8,128)(2,1)}) %all-gather.11.cloned.1.call-update) | async-done | bytes 9437200 | tf_op jit(solution)/shard_map/all_gather | solution.py:1024
  588.6 15.9 %fusion.35 = bf16[1024,1536]{1,0:T(8,128)(2,1)} fusion(bf16[3072,1536]{1,0:T(8,128)(2,1)} %all-gather.11.cloned.1.call-done.w_ref, bf16[2048,3072]{1,0:T(8,128)(2,1)} %get-tuple-element.48), kind=kOutput, calls=%fused_computation.84 | convolution fusion | flops 9665249280 | bytes 18874368 | tf_op jit(solution)/shard_map/dot_general | solution.py:521
  610.6 17.3 %fusion.226 = (f32[1024]{0:T(1024)S(1)}, f32[1024,1536]{1,0:T(8,128)S(1)}) fusion(f32[1024,1536]{1,0:T(8,128)} %copy-done.1, bf16[1024,1536]{1,0:T(8,128)(2,1)} %collective-permute-done.23, bf16[3072,1536]{1,0:T(8,128)(2,1)} %all-gather.11.cloned.1.call-done.w_ref, bf16[2048,3072]{1,0:T(8,128)(2,1)} %get-tuple-element.48), kind=kOutput, calls=%fused_computation.544 | convolution fusion | flops 9669966848 | bytes 31461376 | tf_op jit(solution)/shard_map/dot_general | solution.py:521
  648.1 24.2 %convolution_convert_fusion.after_ref = bf16[3072,1536]{1,0:T(8,128)(2,1)} fusion(bf16[2048,3072]{1,0:T(8,128)(2,1)} %get-tuple-element.48, bf16[1024,1536]{1,0:T(8,128)(2,1)S(1)} %collective-permute-done.24, bf16[1024,1536]{1,0:T(8,128)(2,1)S(1)} %get-tuple-element.190), kind=kOutput, calls=%fused_computation | convolution fusion | flops 19344654336 | bytes 28311552 | tf_op jit(solution)/shard_map/dot_general | solution.py:525
  677.2 38.8 %shard_map.457 = (bf16[2048,3072]{1,0:T(8,128)(2,1)}, bf16[2048,3072]{1,0:T(8,128)(2,1)}) custom-call(bf16[2048,1536]{1,0:T(8,128)(2,1)} %pad_maximum_fusion.3.d_ref, bf16[3072,1536]{1,0:T(8,128)(2,1)} %all-gather.11.cloned.1.call-done.w_ref, bf16[2048,3072]{1,0:T(8,128)(2,1)} %get-tuple-element.49.gate_ref, bf16[2048,3072]{1,0:T(8,128)(2,1)} %get-tuple-element.50.up_ref, ...), custom_call_target="tpu_custom_call" | custom-call | flops 19327352832 | bytes 72351744 | tf_op jit(solution)/shard_map/pallas_call | solution.py:529
  716.1 25.0 %convolution_convert_fusion.2 = bf16[1536,3072]{1,0:T(8,128)(2,1)} fusion(bf16[2048,3072]{1,0:T(8,128)(2,1)} %get-tuple-element.51, bf16[1024,1536]{1,0:T(8,128)(2,1)} %copy-done.37, bf16[1024,1536]{1,0:T(8,128)(2,1)S(1)} %copy-done.14), kind=kOutput, calls=%fused_computation.2 | convolution fusion | flops 19344654336 | bytes 28311552 | tf_op jit(solution)/shard_map/dot_general | solution.py:525
  741.1 14.6 fusion
  755.8 15.9 %add_convert_fusion.2 = bf16[1024,1536]{1,0:T(8,128)(2,1)} fusion(f32[1024,1536]{1,0:T(8,128)S(1)} %fusion, bf16[1536,6144]{1,0:T(8,128)(2,1)} %all-gather.9.cloned.1.call-done.wg_ref.wu_ref, bf16[2048,3072]{1,0:T(8,128)(2,1)} %get-tuple-element.51), kind=kOutput, calls=%fused_computation.40 | convolution fusion | flops 9666822144 | bytes 25165824 | tf_op jit(solution)/shard_map/dot_general | solution.py:517
  771.9 24.8 %convolution_convert_fusion.1 = bf16[1536,3072]{1,0:T(8,128)(2,1)} fusion(bf16[2048,3072]{1,0:T(8,128)(2,1)} %get-tuple-element.52, bf16[1024,1536]{1,0:T(8,128)(2,1)S(1)} %copy-done.38, bf16[1024,1536]{1,0:T(8,128)(2,1)S(1)} %copy-done.14), kind=kOutput, calls=%fused_computation.1 | convolution fusion | flops 19344654336 | bytes 28311552 | tf_op jit(solution)/shard_map/dot_general | solution.py:525
  796.8 15.8 %fusion.2 = f32[1024,1536]{1,0:T(8,128)} fusion(bf16[1536,6144]{1,0:T(8,128)(2,1)} %all-gather.9.cloned.1.call-done.wg_ref.wu_ref, bf16[2048,3072]{1,0:T(8,128)(2,1)} %get-tuple-element.52), kind=kOutput, calls=%fused_computation.14 | convolution fusion | flops 9663676416 | bytes 22020096 | tf_op jit(solution)/shard_map/dot_general | solution.py:517
  812.7 22.1 %multiply_reduce_fusion.1 = (f32[1536]{0:T(1024)S(1)}, f32[1024]{0:T(1024)S(1)}, f32[1024]{0:T(1024)S(1)}, f32[1024,1536]{1,0:T(8,128)}) fusion(f32[1024,1536]{1,0:T(8,128)} %copy-done.1, f32[1024]{0:T(1024)S(1)} %copy-done.120, f32[1024]{0:T(1024)S(1)} %copy-done.109, f32[1536]{0:T(1024)S(1)} %copy-done.105, ...), kind=kOutput, calls=%fused_computation.26 | convolution fusion | flops 9680973824 | bytes 37777408 | tf_op jit(solution)/shard_map/dot_general | solution.py:517
  834.7 10.7 fusion.213
  853.1 8.5 fusion.38.g_ref
  861.5 18.7 %shard_map.458 = (bf16[2048,768]{1,0:T(8,128)(2,1)}, f32[128,768]{1,0:T(8,128)}, f32[128,768]{1,0:T(8,128)}) custom-call(bf16[2048,768]{1,0:T(8,128)(2,1)} %fusion.42.q_ref, bf16[2048,768]{1,0:T(8,128)(2,1)} %fusion.38.g_ref, bf16[128,1536]{1,0:T(8,128)(2,1)} %convolution_convert_fusion.7.k_ref.v_ref, ...), custom_call_target="tpu_custom_call" | custom-call | flops 6442450944 | bytes 25165824 | tf_op jit(solution)/shard_map/pallas_call | solution.py:529
  880.3 6.5 convolution_convert_fusion.3
  897.8 6.4 constant_dynamic-slice_fusion.24
  904.3 7.6 multiply_reduce_fusion.2
  919.4 8.2 fusion.39
  929.9 6.5 fusion.97
  940.5 6.3 fusion.107.refs_15_
  953.0 8.4 fusion.41
  963.1 9.8 fusion.40.refs_1_
  977.2 76.5 %shard_map.459 = (bf16[2048,384]{1,0:T(8,128)(2,1)}, bf16[2048,384]{1,0:T(8,128)(2,1)}, bf16[2048,384]{1,0:T(8,128)(2,1)}, f32[16,384]{1,0:T(8,128)}, f32[16,384]{1,0:T(8,128)}) custom-call(bf16[2048,2304]{1,0:T(8,128)(2,1)} %shard_map.453.q_ref.k_ref.v_ref.refs_0_.refs_7_.refs_8_, bf16[2048,768]{1,0:T(8,128)(2,1)} %fusion.40.refs_1_, ...), custom_call_target="tpu_custom_call" | custom-call | flops 51539607552 | bytes 31457280 | tf_op jit(solution)/shard_map/pallas_call | solution.py:529
  1075.7 6.2 fusion.66
  1081.9 6.2 fusion.68
  1093.1 76.5 %shard_map.460 = (bf16[2048,384]{1,0:T(8,128)(2,1)}, bf16[2048,384]{1,0:T(8,128)(2,1)}, bf16[2048,384]{1,0:T(8,128)(2,1)}, f32[16,384]{1,0:T(8,128)}, f32[16,384]{1,0:T(8,128)}) custom-call(bf16[2048,2304]{1,0:T(8,128)(2,1)} %shard_map.453.q_ref.k_ref.v_ref.refs_0_.refs_7_.refs_8_, bf16[2048,768]{1,0:T(8,128)(2,1)} %fusion.40.refs_1_, ...), custom_call_target="tpu_custom_call" | custom-call | flops 51539607552 | bytes 31457280 | tf_op jit(solution)/shard_map/pallas_call | solution.py:529
  1189.9 10.2 add_convert_fusion.4
  1200.2 8.2 add_convert_fusion.1
  1217.2 6.5 add_convert_fusion.9
  1251.4 12.4 collective-permute-done.69
  1278.9 10.5 collective-permute-done.48
  1305.1 5.6 collective-permute-done.50
  1314.5 14.7 collective-permute-start.60
  1332.1 24.6 %collective-permute-done.60 = bf16[96,512]{1,0:T(8,128)(2,1)S(1)} collective-permute-done((bf16[96,512]{1,0:T(8,128)(2,1)S(1)}, bf16[96,512]{1,0:T(8,128)(2,1)S(1)}, u32[]{:S(2)}, u32[]{:S(2)}) %collective-permute-start.60) | collective-permute-done | bytes 98336 | tf_op jit(solution)/shard_map/ppermute | solution.py:969
  1357.8 12.6 collective-permute-done.53
  1378.2 5.6 collective-permute-done.55
  1390.7 12.9 multiply_reduce_fusion.3
  (882 shorter events, 444.2 us)
Async XLA Ops:
  7.2 120.5 %all-gather.5.cloned.1.call-start = ((), (), s32[]{:S(2)}) async-start(), calls=%async_computation.3 | async-start | bytes 8355840 | tf_op jit(solution)/shard_map/all_gather | solution.py:1011
  13.0 246.0 %all-gather.7.cloned.1.call-start = ((), (), s32[]{:S(2)}) async-start(), calls=%async_computation.4 | async-start | bytes 10027008 | tf_op jit(solution)/shard_map/all_gather | solution.py:1019
  19.5 445.3 %all-gather.9.cloned.1.call-start = ((), (), s32[]{:S(2)}) async-start(), calls=%async_computation.5 | async-start | bytes 20054016 | tf_op jit(solution)/shard_map/all_gather | solution.py:1023
  37.1 551.6 %all-gather.11.cloned.1.call-start = ((), (), s32[]{:S(2)}) async-start(), calls=%async_computation.6 | async-start | bytes 10027008 | tf_op jit(solution)/shard_map/all_gather | solution.py:1024
  37.8 36.7 %collective-permute-start.4 = (bf16[2,512,64]{1,2,0:T(8,128)(2,1)S(1)}, bf16[2,512,64]{1,2,0:T(8,128)(2,1)S(1)}, u32[]{:S(2)}, u32[]{:S(2)}) collective-permute-start(bf16[2,512,64]{1,2,0:T(8,128)(2,1)S(1)} %get-tuple-element.254), channel_id=1, source_target_pairs={{0,16},{8,24},{16,0},{24,8},{1,17},{9,25},{17,1},{25,9},{2,18},{10... | collective-permute-start | bytes 393224 | tf_op jit(solution)/shard_map/ppermute | solution.py:969
  40.7 33.8 %collective-permute-start.5 = (bf16[2,512,64]{1,2,0:T(8,128)(2,1)S(1)}, bf16[2,512,64]{1,2,0:T(8,128)(2,1)S(1)}, u32[]{:S(2)}, u32[]{:S(2)}) collective-permute-start(bf16[2,512,64]{1,2,0:T(8,128)(2,1)S(1)} %get-tuple-element.255), channel_id=1, source_target_pairs={{0,24},{8,16},{16,8},{24,0},{1,25},{9,17},{17,9},{25,1},{2,26},{10... | collective-permute-start | bytes 393224 | tf_op jit(solution)/shard_map/ppermute | solution.py:969
  42.2 32.4 %collective-permute-start.3 = (bf16[2,512,64]{1,2,0:T(8,128)(2,1)S(1)}, bf16[2,512,64]{1,2,0:T(8,128)(2,1)S(1)}, u32[]{:S(2)}, u32[]{:S(2)}) collective-permute-start(bf16[2,512,64]{1,2,0:T(8,128)(2,1)S(1)} %get-tuple-element.253), channel_id=1, source_target_pairs={{0,8},{8,0},{16,24},{24,16},{1,9},{9,1},{17,25},{25,17},{2,10},{10... | collective-permute-start | bytes 393224 | tf_op jit(solution)/shard_map/ppermute | solution.py:969
  292.2 10.9 collective-permute-start.17
  293.9 1115.2 %reduce-scatter.4.cloned.1.call-start = ((), (), s32[]{:S(2)}) async-start(), calls=%async_computation.7 | async-start | bytes 10027008 | tf_op jit(solution)/shard_map/reduce_scatter | solution.py:1205
  301.5 25.0 %collective-permute-start.19 = (bf16[768,768]{1,0:T(8,128)(2,1)}, bf16[768,768]{1,0:T(8,128)(2,1)}, u32[]{:S(2)}, u32[]{:S(2)}) collective-permute-start(bf16[768,768]{1,0:T(8,128)(2,1)} %get-tuple-element.212), channel_id=1, source_target_pairs={{0,1},{1,0},{2,3},{3,2},{4,5},{5,4},{6,7},{7,6},{8,9},{9,8},{10,11... | collective-permute-start | bytes 3538952 | tf_op jit(solution)/shard_map/ppermute | solution.py:966
  741.1 668.0 %reduce-scatter.6.cloned.1.call-start = ((), (), s32[]{:S(2)}) async-start(), calls=%async_computation.8 | async-start | bytes 10027008 | tf_op jit(solution)/shard_map/reduce_scatter | solution.py:1205
  771.7 40.9 %collective-permute-start.25 = (bf16[1024,1536]{1,0:T(8,128)(2,1)}, bf16[1024,1536]{1,0:T(8,128)(2,1)}, u32[]{:S(2)}, u32[]{:S(2)}) collective-permute-start(bf16[1024,1536]{1,0:T(8,128)(2,1)} %add_convert_fusion.2), channel_id=1, source_target_pairs={{0,1},{1,0},{2,3},{3,2},{4,5},{5,4},{6,7},{7,6},{8,9},{9,8},{10,11... | collective-permute-start | bytes 9437192 | tf_op jit(solution)/shard_map/ppermute | solution.py:966
  796.7 626.2 %reduce-scatter.8.cloned.1.call-start = ((), (), s32[]{:S(2)}) async-start(), calls=%async_computation.9 | async-start | bytes 10027008 | tf_op jit(solution)/shard_map/reduce_scatter | solution.py:1205
  886.8 17.4 %collective-permute-start.27 = (bf16[1024,1536]{1,0:T(8,128)(2,1)}, bf16[1024,1536]{1,0:T(8,128)(2,1)}, u32[]{:S(2)}, u32[]{:S(2)}) collective-permute-start(bf16[1024,1536]{1,0:T(8,128)(2,1)} %convolution_convert_fusion.3), channel_id=1, source_target_pairs={{0,1},{1,0},{2,3},{3,2},{4,5},{5,4},{6,7},{7,6},{8,9},{9,8},{10,11... | collective-permute-start | bytes 9437192 | tf_op jit(solution)/shard_map/ppermute | solution.py:966
  916.6 36.3 %collective-permute-start.28 = (bf16[1024,1536]{1,0:T(8,128)(2,1)}, bf16[1024,1536]{1,0:T(8,128)(2,1)}, u32[]{:S(2)}, u32[]{:S(2)}) collective-permute-start(bf16[1024,1536]{1,0:T(8,128)(2,1)} %get-tuple-element.186), channel_id=1, source_target_pairs={{0,1},{1,0},{2,3},{3,2},{4,5},{5,4},{6,7},{7,6},{8,9},{9,8},{10,11... | collective-permute-start | bytes 9437192 | tf_op jit(solution)/shard_map/ppermute | solution.py:966
  928.8 21.6 %collective-permute-start.30 = (bf16[768,768]{1,0:T(8,128)(2,1)}, bf16[768,768]{1,0:T(8,128)(2,1)}, u32[]{:S(2)}, u32[]{:S(2)}) collective-permute-start(bf16[768,768]{1,0:T(8,128)(2,1)} %get-tuple-element.208), channel_id=1, source_target_pairs={{0,1},{1,0},{2,3},{3,2},{4,5},{5,4},{6,7},{7,6},{8,9},{9,8},{10,11... | collective-permute-start | bytes 3538952 | tf_op jit(solution)/shard_map/ppermute | solution.py:966
  946.8 112.4 %collective-permute-start.32 = (bf16[768,768]{1,0:T(8,128)(2,1)}, bf16[768,768]{1,0:T(8,128)(2,1)}, u32[]{:S(2)}, u32[]{:S(2)}) collective-permute-start(bf16[768,768]{1,0:T(8,128)(2,1)} %fusion.107.refs_15_), channel_id=1, source_target_pairs={{0,8},{8,0},{16,24},{24,16},{1,9},{9,1},{17,25},{25,17},{2,10},{10... | collective-permute-start | bytes 3538952 | tf_op jit(solution)/shard_map/ppermute | solution.py:969
  949.8 105.8 %collective-permute-start.31 = (bf16[384,1536]{1,0:T(8,128)(2,1)}, bf16[384,1536]{1,0:T(8,128)(2,1)}, u32[]{:S(2)}, u32[]{:S(2)}) collective-permute-start(bf16[384,1536]{1,0:T(8,128)(2,1)} %convolution_convert_fusion.6.refs_14_), channel_id=1, source_target_pairs={{0,8},{8,0},{16,24},{24,16},{1,9},{9,1},{17,25},{25,17},{2,10},{10... | collective-permute-start | bytes 3538952 | tf_op jit(solution)/shard_map/ppermute | solution.py:969
  961.6 11.3 collective-permute-start.29
  975.7 112.4 %collective-permute-start.33 = (bf16[768,1536]{1,0:T(8,128)(2,1)}, bf16[768,1536]{1,0:T(8,128)(2,1)}, u32[]{:S(2)}, u32[]{:S(2)}) collective-permute-start(bf16[768,1536]{1,0:T(8,128)(2,1)} %fusion.80.refs_16_), channel_id=1, source_target_pairs={{0,16},{8,24},{16,0},{24,8},{1,17},{9,25},{17,1},{25,9},{2,18},{10... | collective-permute-start | bytes 7077896 | tf_op jit(solution)/shard_map/ppermute | solution.py:969
  1058.5 114.1 %collective-permute-start.72 = (bf16[192,1536]{1,0:T(8,128)(2,1)}, bf16[192,1536]{1,0:T(8,128)(2,1)S(1)}, u32[]{:S(2)}, u32[]{:S(2)}) collective-permute-start(bf16[192,1536]{1,0:T(8,128)(2,1)} %constant_dynamic-slice_fusion.41.refs_14_), channel_id=1, source_target_pairs={{0,16},{8,24},{16,0},{24,8},{1,17},{9,25},{17,1},{25,9},{2,18},{10... | collective-permute-start | bytes 1769480 | tf_op jit(solution)/shard_map/ppermute | solution.py:969
  1065.3 164.4 %collective-permute-start.67 = (bf16[384,768]{1,0:T(8,128)(2,1)}, bf16[384,768]{1,0:T(8,128)(2,1)}, u32[]{:S(2)}, u32[]{:S(2)}) collective-permute-start(bf16[384,768]{1,0:T(8,128)(2,1)} %constant_dynamic-slice_fusion.40.refs_15_), channel_id=1, source_target_pairs={{0,16},{8,24},{16,0},{24,8},{1,17},{9,25},{17,1},{25,9},{2,18},{10... | collective-permute-start | bytes 1769480 | tf_op jit(solution)/shard_map/ppermute | solution.py:969
  1073.1 116.7 %collective-permute-start.47 = (bf16[768,1152]{1,0:T(8,128)(2,1)}, bf16[768,1152]{1,0:T(8,128)(2,1)}, u32[]{:S(2)}, u32[]{:S(2)}) collective-permute-start(bf16[768,1152]{1,0:T(8,128)(2,1)} %fusion.43.refs_17_), channel_id=1, source_target_pairs={{0,16},{8,24},{16,0},{24,8},{1,17},{9,25},{17,1},{25,9},{2,18},{10... | collective-permute-start | bytes 5308424 | tf_op jit(solution)/shard_map/ppermute | solution.py:969
  1169.5 129.9 %collective-permute-start.63 = (bf16[384,1536]{1,0:T(8,128)(2,1)}, bf16[384,1536]{1,0:T(8,128)(2,1)}, u32[]{:S(2)}, u32[]{:S(2)}) collective-permute-start(bf16[384,1536]{1,0:T(8,128)(2,1)} %constant_dynamic-slice_fusion.39.refs_16_), channel_id=1, source_target_pairs={{0,8},{8,0},{16,24},{24,16},{1,9},{9,1},{17,25},{25,17},{2,10},{10... | collective-permute-start | bytes 3538952 | tf_op jit(solution)/shard_map/ppermute | solution.py:969
  1173.6 70.6 %collective-permute-start.73 = (bf16[48,1536]{1,0:T(8,128)(2,1)}, bf16[48,1536]{1,0:T(8,128)(2,1)}, u32[]{:S(2)}, u32[]{:S(2)}) collective-permute-start(bf16[48,1536]{1,0:T(8,128)(2,1)} %get-tuple-element.232), channel_id=1, source_target_pairs={{0,2},{2,0},{4,6},{6,4},{1,3},{3,1},{5,7},{7,5},{8,10},{10,8},{12,... | collective-permute-start | bytes 442376 | tf_op jit(solution)/shard_map/ppermute | solution.py:969
  1174.0 71.8 %collective-permute-start.74 = (bf16[48,1536]{1,0:T(8,128)(2,1)}, bf16[48,1536]{1,0:T(8,128)(2,1)}, u32[]{:S(2)}, u32[]{:S(2)}) collective-permute-start(bf16[48,1536]{1,0:T(8,128)(2,1)} %get-tuple-element.234), channel_id=1, source_target_pairs={{0,4},{2,6},{4,0},{6,2},{1,5},{3,7},{5,1},{7,3},{8,12},{10,14},{12... | collective-permute-start | bytes 442376 | tf_op jit(solution)/shard_map/ppermute | solution.py:969
  1189.8 21.5 %collective-permute-start.35 = (f32[1,1536]{1,0:T(1,128)S(1)}, f32[1,1536]{1,0:T(1,128)S(1)}, u32[]{:S(2)}, u32[]{:S(2)}) collective-permute-start(f32[1,1536]{1,0:T(1,128)S(1)} %copy.378), channel_id=1, source_target_pairs={{0,1},{1,0},{2,3},{3,2},{4,5},{5,4},{6,7},{7,6},{8,9},{9,8},{10,11... | collective-permute-start | bytes 18440 | tf_op jit(solution)/shard_map/ppermute | solution.py:966
  1227.5 20.1 %collective-permute-start.75 = (bf16[48,1536]{1,0:T(8,128)(2,1)}, bf16[48,1536]{1,0:T(8,128)(2,1)S(1)}, u32[]{:S(2)}, u32[]{:S(2)}) collective-permute-start(bf16[48,1536]{1,0:T(8,128)(2,1)} %get-tuple-element.233), channel_id=1, source_target_pairs={{0,6},{2,4},{4,2},{6,0},{1,7},{3,5},{5,3},{7,1},{8,14},{10,12},{12... | collective-permute-start | bytes 442376 | tf_op jit(solution)/shard_map/ppermute | solution.py:969
  1244.2 19.6 %collective-permute-start.69 = (bf16[96,768]{1,0:T(8,128)(2,1)}, bf16[96,768]{1,0:T(8,128)(2,1)S(1)}, u32[]{:S(2)}, u32[]{:S(2)}) collective-permute-start(bf16[96,768]{1,0:T(8,128)(2,1)} %get-tuple-element.239), channel_id=1, source_target_pairs={{0,4},{2,6},{4,0},{6,2},{1,5},{3,7},{5,1},{7,3},{8,12},{10,14},{12... | collective-permute-start | bytes 442376 | tf_op jit(solution)/shard_map/ppermute | solution.py:969
  1245.7 19.1 %collective-permute-start.70 = (bf16[96,768]{1,0:T(8,128)(2,1)}, bf16[96,768]{1,0:T(8,128)(2,1)S(1)}, u32[]{:S(2)}, u32[]{:S(2)}) collective-permute-start(bf16[96,768]{1,0:T(8,128)(2,1)} %get-tuple-element.238), channel_id=1, source_target_pairs={{0,6},{2,4},{4,2},{6,0},{1,7},{3,5},{5,3},{7,1},{8,14},{10,12},{12... | collective-permute-start | bytes 442376 | tf_op jit(solution)/shard_map/ppermute | solution.py:969
  1247.6 24.8 %collective-permute-start.57 = (bf16[768,512]{1,0:T(8,128)(2,1)}, bf16[768,512]{1,0:T(8,128)(2,1)}, u32[]{:S(2)}, u32[]{:S(2)}) collective-permute-start(bf16[768,512]{1,0:T(8,128)(2,1)} %add_convert_fusion.12), channel_id=1, source_target_pairs={{0,8},{8,0},{16,24},{24,16},{1,9},{9,1},{17,25},{25,17},{2,10},{10... | collective-permute-start | bytes 2359304 | tf_op jit(solution)/shard_map/ppermute | solution.py:969
  1250.7 38.6 %collective-permute-start.48 = (bf16[384,1152]{1,0:T(8,128)(2,1)}, bf16[384,1152]{1,0:T(8,128)(2,1)}, u32[]{:S(2)}, u32[]{:S(2)}) collective-permute-start(bf16[384,1152]{1,0:T(8,128)(2,1)} %constant_dynamic-slice_fusion.32), channel_id=1, source_target_pairs={{0,8},{8,0},{16,24},{24,16},{1,9},{9,1},{17,25},{25,17},{2,10},{10... | collective-permute-start | bytes 2654216 | tf_op jit(solution)/shard_map/ppermute | solution.py:969
  1263.8 29.4 %collective-permute-start.52 = (bf16[768,640]{1,0:T(8,128)(2,1)}, bf16[768,640]{1,0:T(8,128)(2,1)}, u32[]{:S(2)}, u32[]{:S(2)}) collective-permute-start(bf16[768,640]{1,0:T(8,128)(2,1)} %add_convert_fusion.9), channel_id=1, source_target_pairs={{0,16},{8,24},{16,0},{24,8},{1,17},{9,25},{17,1},{25,9},{2,18},{10... | collective-permute-start | bytes 2949128 | tf_op jit(solution)/shard_map/ppermute | solution.py:969
  1277.4 21.8 %collective-permute-start.58 = (bf16[384,512]{1,0:T(8,128)(2,1)S(1)}, bf16[384,512]{1,0:T(8,128)(2,1)S(1)}, u32[]{:S(2)}, u32[]{:S(2)}) collective-permute-start(bf16[384,512]{1,0:T(8,128)(2,1)S(1)} %constant_dynamic-slice_fusion.16), channel_id=1, source_target_pairs={{0,16},{8,24},{16,0},{24,8},{1,17},{9,25},{17,1},{25,9},{2,18},{10... | collective-permute-start | bytes 1179656 | tf_op jit(solution)/shard_map/ppermute | solution.py:969
  1290.8 12.7 collective-permute-start.49
  1290.8 19.9 %collective-permute-start.50 = (bf16[96,1152]{1,0:T(8,128)(2,1)S(1)}, bf16[96,1152]{1,0:T(8,128)(2,1)S(1)}, u32[]{:S(2)}, u32[]{:S(2)}) collective-permute-start(bf16[96,1152]{1,0:T(8,128)(2,1)S(1)} %get-tuple-element.224), channel_id=1, source_target_pairs={{0,4},{2,6},{4,0},{6,2},{1,5},{3,7},{5,1},{7,3},{8,12},{10,14},{12... | collective-permute-start | bytes 663560 | tf_op jit(solution)/shard_map/ppermute | solution.py:969
  1293.2 21.3 %collective-permute-start.51 = (bf16[96,1152]{1,0:T(8,128)(2,1)S(1)}, bf16[96,1152]{1,0:T(8,128)(2,1)S(1)}, u32[]{:S(2)}, u32[]{:S(2)}) collective-permute-start(bf16[96,1152]{1,0:T(8,128)(2,1)S(1)} %get-tuple-element.223), channel_id=1, source_target_pairs={{0,6},{2,4},{4,2},{6,0},{1,7},{3,5},{5,3},{7,1},{8,14},{10,12},{12... | collective-permute-start | bytes 663560 | tf_op jit(solution)/shard_map/ppermute | solution.py:969
  1299.4 29.8 %collective-permute-start.59 = (bf16[96,512]{1,0:T(8,128)(2,1)S(1)}, bf16[96,512]{1,0:T(8,128)(2,1)S(1)}, u32[]{:S(2)}, u32[]{:S(2)}) collective-permute-start(bf16[96,512]{1,0:T(8,128)(2,1)S(1)} %get-tuple-element.249), channel_id=1, source_target_pairs={{0,2},{2,0},{4,6},{6,4},{1,3},{3,1},{5,7},{7,5},{8,10},{10,8},{12,... | collective-permute-start | bytes 294920 | tf_op jit(solution)/shard_map/ppermute | solution.py:969
  1302.7 54.5 %collective-permute-start.64 = (bf16[96,1536]{1,0:T(8,128)(2,1)S(1)}, bf16[96,1536]{1,0:T(8,128)(2,1)S(1)}, u32[]{:S(2)}, u32[]{:S(2)}) collective-permute-start(bf16[96,1536]{1,0:T(8,128)(2,1)S(1)} %get-tuple-element.217), channel_id=1, source_target_pairs={{0,2},{2,0},{4,6},{6,4},{1,3},{3,1},{5,7},{7,5},{8,10},{10,8},{12,... | collective-permute-start | bytes 884744 | tf_op jit(solution)/shard_map/ppermute | solution.py:969
  1303.4 53.7 %collective-permute-start.65 = (bf16[96,1536]{1,0:T(8,128)(2,1)S(1)}, bf16[96,1536]{1,0:T(8,128)(2,1)S(1)}, u32[]{:S(2)}, u32[]{:S(2)}) collective-permute-start(bf16[96,1536]{1,0:T(8,128)(2,1)S(1)} %get-tuple-element.219), channel_id=1, source_target_pairs={{0,4},{2,6},{4,0},{6,2},{1,5},{3,7},{5,1},{7,3},{8,12},{10,14},{12... | collective-permute-start | bytes 884744 | tf_op jit(solution)/shard_map/ppermute | solution.py:969
  1310.7 46.4 %collective-permute-start.66 = (bf16[96,1536]{1,0:T(8,128)(2,1)S(1)}, bf16[96,1536]{1,0:T(8,128)(2,1)S(1)}, u32[]{:S(2)}, u32[]{:S(2)}) collective-permute-start(bf16[96,1536]{1,0:T(8,128)(2,1)S(1)} %get-tuple-element.218), channel_id=1, source_target_pairs={{0,6},{2,4},{4,2},{6,0},{1,7},{3,5},{5,3},{7,1},{8,14},{10,12},{12... | collective-permute-start | bytes 884744 | tf_op jit(solution)/shard_map/ppermute | solution.py:969
  1314.5 42.3 %collective-permute-start.60 = (bf16[96,512]{1,0:T(8,128)(2,1)S(1)}, bf16[96,512]{1,0:T(8,128)(2,1)S(1)}, u32[]{:S(2)}, u32[]{:S(2)}) collective-permute-start(bf16[96,512]{1,0:T(8,128)(2,1)S(1)} %get-tuple-element.251), channel_id=1, source_target_pairs={{0,4},{2,6},{4,0},{6,2},{1,5},{3,7},{5,1},{7,3},{8,12},{10,14},{12... | collective-permute-start | bytes 294920 | tf_op jit(solution)/shard_map/ppermute | solution.py:969
  1329.1 27.6 %collective-permute-start.61 = (bf16[96,512]{1,0:T(8,128)(2,1)S(1)}, bf16[96,512]{1,0:T(8,128)(2,1)S(1)}, u32[]{:S(2)}, u32[]{:S(2)}) collective-permute-start(bf16[96,512]{1,0:T(8,128)(2,1)S(1)} %get-tuple-element.250), channel_id=1, source_target_pairs={{0,6},{2,4},{4,2},{6,0},{1,7},{3,5},{5,3},{7,1},{8,14},{10,12},{12... | collective-permute-start | bytes 294920 | tf_op jit(solution)/shard_map/ppermute | solution.py:969
  1356.7 33.9 %collective-permute-start.34 = (bf16[1024,1536]{1,0:T(8,128)(2,1)}, bf16[1024,1536]{1,0:T(8,128)(2,1)}, u32[]{:S(2)}, u32[]{:S(2)}) collective-permute-start(bf16[1024,1536]{1,0:T(8,128)(2,1)} %add_convert_fusion.1), channel_id=1, source_target_pairs={{0,1},{1,0},{2,3},{3,2},{4,5},{5,4},{6,7},{7,6},{8,9},{9,8},{10,11... | collective-permute-start | bytes 9437192 | tf_op jit(solution)/shard_map/ppermute | solution.py:966
  1356.7 13.6 collective-permute-start.53
  1357.5 27.9 %collective-permute-start.71 = (bf16[48,2304]{1,0:T(8,128)(2,1)S(1)}, bf16[48,2304]{1,0:T(8,128)(2,1)S(1)}, u32[]{:S(2)}, u32[]{:S(2)}) collective-permute-start(bf16[48,2304]{1,0:T(8,128)(2,1)S(1)} %dynamic-slice_convert_fusion.1), channel_id=1, source_target_pairs={{0,1},{1,0},{2,3},{3,2},{4,5},{5,4},{6,7},{7,6},{8,9},{9,8},{10,11... | collective-permute-start | bytes 663560 | tf_op jit(solution)/shard_map/ppermute | solution.py:966
  1371.2 12.6 collective-permute-start.55
  1411.4 13.5 collective-permute-start.77
  (234 other events, 2320.3 us)
Sparse Core Ops, SparseCore 0:
  13.1 114.5 all-gather.4
  131.0 120.6 all-gather.6
  255.1 209.6 all-gather.8
  468.0 120.6 all-gather.10
  741.2 169.5 reduce-scatter.3
  917.3 199.3 reduce-scatter.5
  1122.3 210.2 reduce-scatter.7

commit v3 on v2

--- a/solution.py
+++ b/solution.py
@@ -941,6 +941,146 @@
     )
 
 
+def chip_sum_kernel(*refs, inputs, jobs, planes):
+    ins, outs = (refs[:inputs], refs[inputs : 2 * inputs])
+    scratch = list(refs[2 * inputs : -3])
+    send_sem, recv_sem, local_sem = refs[-3:]
+    s_at, z_at = (lax.axis_index("seq"), lax.axis_index("z"))
+    y_at, x_at = (s_at // 2, s_at % 2)
+    y_mate = (1 - y_at) * 2 + x_at
+    x_mate = y_at * 2 + (1 - x_at)
+    z_mates = [(z_at + offset) % planes for offset in range(1, planes)]
+    z_froms = [(z_at + planes - offset) % planes for offset in range(1, planes)]
+    barrier = pltpu.get_barrier_semaphore()
+    for mate in (y_mate, x_mate):
+        pl.semaphore_signal(
+            barrier, inc=1, device_id={"seq": mate}, device_id_type=pl.DeviceIdType.MESH
+        )
+    for mate in z_mates:
+        pl.semaphore_signal(
+            barrier, inc=1, device_id={"z": mate}, device_id_type=pl.DeviceIdType.MESH
+        )
+    pl.semaphore_wait(barrier, 1 + planes)
+
+    def remote(job, which, source, target, device):
+        copy = pltpu.make_async_remote_copy(
+            src_ref=source,
+            dst_ref=target,
+            send_sem=send_sem.at[job, which],
+            recv_sem=recv_sem.at[job, which],
+            device_id=device,
+            device_id_type=pl.DeviceIdType.MESH,
+        )
+        copy.start()
+        return copy
+
+    def along_z(job, source, received):
+        return [
+            remote(job, 2 + n, source.at[mate], received.at[n], {"z": mate})
+            for n, mate in enumerate(z_mates)
+        ]
+
+    state = []
+    copies = []
+    for n, (full, at, low_col, width, y_first) in enumerate(jobs):
+        cols = pl.ds(low_col, width)
+        if full:
+            own, first, second, third = (scratch.pop(0) for _ in range(4))
+            view = ins[at].at[:, :, :, :, cols]
+            given = view.at[1 - y_at] if y_first else view.at[:, 1 - x_at]
+            kept = view.at[y_at] if y_first else view.at[:, x_at]
+            mate = {"seq": y_mate if y_first else x_mate}
+            moving = [remote(n, 0, given, first, mate)]
+        else:
+            own, third = (scratch.pop(0) for _ in range(2))
+            first, second = (None, None)
+            view = ins[at].at[:, :, cols]
+            kept = view.at[z_at]
+            moving = along_z(n, view, third)
+        local = pltpu.make_async_copy(kept, own, local_sem.at[n])
+        local.start()
+        copies += moving
+        state.append((own, first, second, third, local, moving))
+
+    waiting = []
+    for n, (full, at, low_col, width, y_first) in enumerate(jobs):
+        own, first, second, third, local, moving = state[n]
+        local.wait()
+        if not full:
+            waiting.append(moving)
+            continue
+        moving[0].wait_recv()
+
+        def add_first(i, carry):
+            half, plane = (i // planes, i % planes)
+            own[half, plane] = (
+                own[half, plane].astype(f32) + first[half, plane].astype(f32)
+            ).astype(bf16)
+            return carry
+
+        lax.fori_loop(0, 2 * planes, add_first, 0)
+        here = x_at if y_first else y_at
+        mate = {"seq": x_mate if y_first else y_mate}
+        copy = remote(n, 1, own.at[1 - here], second, mate)
+        copies.append(copy)
+        waiting.append([copy])
+    for n, (full, at, low_col, width, y_first) in enumerate(jobs):
+        if not full:
+            continue
+        own, first, second, third, local, moving = state[n]
+        here = x_at if y_first else y_at
+        waiting[n][0].wait_recv()
+
+        def add_second(plane, carry):
+            second[plane] = (
+                own[here, plane].astype(f32) + second[plane].astype(f32)
+            ).astype(bf16)
+            return carry
+
+        lax.fori_loop(0, planes, add_second, 0)
+        waiting[n] = along_z(n, second, third)
+        copies += waiting[n]
+    for n, (full, at, low_col, width, y_first) in enumerate(jobs):
+        own, first, second, third, local, moving = state[n]
+        for copy in waiting[n]:
+            copy.wait_recv()
+        total = (second[z_at] if full else own[...]).astype(f32)
+        for m in range(planes - 1):
+            total = total + third[m].astype(f32)
+        outs[at][:, low_col : low_col + width] = total
+    for copy in copies:
+        copy.wait_send()
+
+
+def chip_sums(arrays, jobs, planes):
+    scratch = []
+    for full, at, _, width, _ in jobs:
+        rows = arrays[at].shape[-2]
+        if full:
+            scratch += [pltpu.VMEM((2, planes, rows, width), bf16)] * 2
+            scratch += [pltpu.VMEM((planes, rows, width), bf16)]
+        else:
+            scratch += [pltpu.VMEM((rows, width), bf16)]
+        scratch += [pltpu.VMEM((planes - 1, rows, width), bf16)]
+    count = len(jobs)
+    scratch += [
+        pltpu.SemaphoreType.DMA((count, 1 + planes)),
+        pltpu.SemaphoreType.DMA((count, 1 + planes)),
+        pltpu.SemaphoreType.DMA((count,)),
+    ]
+    return pl.pallas_call(
+        functools.partial(chip_sum_kernel, inputs=len(arrays), jobs=jobs, planes=planes),
+        in_specs=[pl.BlockSpec(memory_space=pl.ANY)] * len(arrays),
+        out_specs=[pl.BlockSpec(memory_space=pltpu.VMEM)] * len(arrays),
+        out_shape=[shape_of(x.shape[-2:], f32) for x in arrays],
+        scratch_shapes=scratch,
+        cost_estimate=pl.CostEstimate(flops=10**11, bytes_accessed=10**7, transcendentals=0),
+        compiler_params=pltpu.CompilerParams(
+            vmem_limit_bytes=56 << 20, collective_id=0, has_side_effects=True
+        ),
+    )(*arrays)
+
+
 def chip_body(
     latents, noise_draw, audio_len, bucket, timing, prompt, prompt_len, step_count,
     edge_weight, edge_first, edge_second,
@@ -996,6 +1136,41 @@
             pick(x, 1 - k_at, axis).reshape(rows, -1),
         )
 
+    def tie(x):
+        return x.reshape(-1, x.shape[-1])[0, 0].astype(f32) * 0.0
+
+    y_at, x_at = (s_at // 2, s_at % 2)
+
+    def gather_chips(x, parts):
+        piece = x.shape[0] // parts
+        shape = (planes, piece, x.shape[1])
+        total = jnp.zeros((2, 2, parts) + shape, x.dtype).swapaxes(2, 3)
+
+        def put(total, block, y, column, z, part):
+            return lax.dynamic_update_slice(
+                total, block[None, None, :, None], (y, column, z, part, 0, 0)
+            )
+
+        for part in range(parts):
+            mine = x[part * piece : (part + 1) * piece]
+            block = lax.dynamic_update_slice(jnp.zeros(shape, x.dtype), mine[None], (z_at, 0, 0))
+            for offset in range(1, planes):
+                taken = across(mine, "z", planes, offset)
+                block = lax.dynamic_update_slice(block, taken[None], (z_at ^ offset, 0, 0))
+            from_x, from_y = (across(block, "seq", chips, 1), across(block, "seq", chips, 2))
+            half = planes // 2
+            first = across(from_y[:half], "seq", chips, 1)
+            second = across(from_x[half:], "seq", chips, 2)
+            for taken, y, column, z in (
+                (block, y_at, x_at, 0),
+                (from_x, y_at, 1 - x_at, 0),
+                (from_y, 1 - y_at, x_at, 0),
+                (first, 1 - y_at, 1 - x_at, 0),
+                (second, 1 - y_at, 1 - x_at, half),
+            ):
+                total = put(total, taken, y, column, z, part)
+        return (total.reshape(-1, x.shape[1]), block, from_x)
+
     rows = attend_weight.shape[0]
     attend_view = (rows, 2, 3, 2, THIRD)
     square_view = (rows, 3, 2, HALF)
@@ -1016,9 +1191,7 @@
     mine, other = halves_of(cross_weight.astype(bf16), cross_view, 2)
     cross_mine = in_order(mine, swap(other))
     cross_mine = jnp.concatenate([cross_mine[:, :HALF], cross_mine[:, HALF:]], 0)
-    square_cols = lax.all_gather(
-        jnp.concatenate([square_mine, cross_mine], 1), peers, axis=0, tiled=True
-    )
+    square_cols = gather_chips(jnp.concatenate([square_mine, cross_mine], 1), 1)[0]
     mine, other = halves_of(upward_weight.astype(bf16), up_view, 3)
     up_w = lax.all_gather(in_order(mine, swap(other)), peers, axis=0, tiled=True)
     down_w = lax.all_gather(down_weight.astype(bf16), peers, axis=0, tiled=True)
@@ -1114,10 +1287,7 @@
     qkv = qkv_project(n1, first_group, tables)
     o, lse = attend_forward(qkv, kv_prefix)
 
-    def tie(x):
-        return x[0, 0].astype(f32) * 0.0
-
-    square_cols = square_cols[:] + tie(o).astype(bf16)
+    square_cols = square_cols + tie(o).astype(bf16)
     cross_w = square_cols[:, 3 * HALF :].reshape(many, 2, CROSS // many, HALF)
     cross_w = jnp.concatenate(
         [cross_w[:, 0].reshape(CROSS, HALF), cross_w[:, 1].reshape(CROSS, HALF)], 1
@@ -1147,8 +1317,6 @@
     d_h, gain4 = norm_backward(dot_nt(d_pred, w_out_t), std4, dev4, norm_gains[3])
     d_f = both_halves(d_h.astype(bf16))
 
-    y_at, x_at = (s_at // 2, s_at % 2)
-
     def half_at(x, at, size):
         return lax.dynamic_slice_in_dim(x, at * size, size, 0)
 
@@ -1181,22 +1349,9 @@
             self.taken = across(given, "seq", chips, self.later)
             return self
 
-        def third(self, behind=0.0):
+        def folded(self, behind):
             kept = (self.kept.astype(f32) + self.taken.astype(f32) + behind).astype(bf16)
-            size = self.quarter // planes
-            self.kept = half_at(kept, z_at, size)
-            self.sent = [half_at(kept, z_at ^ offset, size) for offset in range(1, planes)]
-            self.taken = [
-                across(given, "z", planes, offset)
-                for offset, given in enumerate(self.sent, 1)
-            ]
-            return self
-
-        def total(self, behind=0.0):
-            return self.kept.astype(f32) + sum(x.astype(f32) for x in self.taken) + behind
-
-    def scattered(product, depth, y_first):
-        return Scatter(product, depth, y_first).second().third().total()
+            return kept.reshape(planes, -1, kept.shape[1])
 
     def gradient(left, right, y_first):
         return Scatter(lambda cut_of: dot_tn(cut_of(left, 1), right), left.shape[1], y_first)
@@ -1246,24 +1401,17 @@
         lead_row = jnp.concatenate([jnp.zeros_like(d_k0), d_k0, d_v0], 1)
         return (jnp.concatenate([d_q, d_k, d_v], 1), lead_row, tie(d_q))
 
-    def attend_gradient(right, lead_row, y_first):
-        def product(cut_of):
-            return dot_tn(cut_of(n1, 1), right) + cut_of(lead_column, 1).T * lead_row[:1]
-
-        return Scatter(product, D, y_first)
+    def attend_gradient(right, lead_row):
+        return (dot_tn(n1, right) + lead_column.T * lead_row[:1]).astype(bf16)
 
     after = [x for r in (r_cross, r_cq, r_side) for x in r.sent]
     d_first, lead_first, behind_first = attend_half(0, after)
-    r_first = attend_gradient(d_first, lead_first, True)
+    g_first = attend_gradient(d_first, lead_first)
     for r in (r_cross, r_cq, r_side):
         r.second(behind_first)
-    after = [x for r in (r_cross, r_cq, r_side, r_first) for x in r.sent]
+    after = [x for r in (r_cross, r_cq, r_side) for x in r.sent] + [g_first]
     d_second, lead_second, behind_second = attend_half(1, after)
-    edge_at = 5 * 128
-    r_second = attend_gradient(d_second[:, :edge_at], lead_second[:, :edge_at], True)
-    r_last = attend_gradient(d_second[:, edge_at:], lead_second[:, edge_at:], False)
-    for r in (r_first, r_second, r_last):
-        r.second(behind_second)
+    g_second = attend_gradient(d_second, lead_second)
     d_n1 = shared_sum(
         lambda i: dot_nt(cut(d_first, i), attend_w[:, : 3 * THIRD])
         + dot_nt(cut(d_second, i), attend_w[:, 3 * THIRD :])
@@ -1271,9 +1419,7 @@
     d_part, gain1 = norm_again(d_n1, h0, norm_gains[0])
     d_h = d_h + d_part
     g_in_t = dot_tn(d_h.astype(bf16), x_in[:own])
-    s_cross, s_cq, s_side = (r.third(behind_second).total() for r in (r_cross, r_cq, r_side))
-    s_square = jnp.concatenate([s_side[:, :HALF], s_cq, s_side[:, HALF:]], 1)
-    s_attend = jnp.concatenate([r.third().total() for r in (r_first, r_second, r_last)], 1)
+    short = [r.folded(behind_second) for r in (r_cross, r_cq, r_side)]
     d_kv0 = jnp.concatenate([lead_first, lead_second], 1)
 
     high = d_kv0.astype(bf16)
@@ -1282,15 +1428,6 @@
     d_np = d_np[:1] + d_np[16:17]
     d_np = d_np + swap(d_np)
     d_lead, prefix_gain = norm_backward(d_np, prefix_std, prefix_dev, norm_gains[0])
-    for axis, size, bit in reversed(hops):
-        d_lead = jnp.concatenate([d_lead, across(d_lead, axis, size, bit)], 0)
-    g_t2 = exact("ge,gd->ed", t_hidden.astype(f32), d_lead)
-    d_lead_here = lax.dynamic_slice(d_lead, (0, device * rows), (clips, rows))
-    g_timing = exact("gz,gd->zd", z_feat.astype(f32), d_lead_here)
-    d_t_hidden = exact("gd,ed->ge", d_lead, w_t2.astype(f32))
-    t_sig = jax.nn.sigmoid(t_pre)
-    d_t_pre = d_t_hidden * t_sig * (1.0 + t_pre * (1.0 - t_sig))
-    g_t1 = exact("gz,gd->zd", t_feat.astype(f32), d_t_pre)
 
     def to_owner(x, view, axis):
         count = x.shape[0] // 2
@@ -1309,18 +1446,50 @@
     edges = jnp.concatenate([g_in_t, g_out_t], 1)
     gains = jnp.pad(gains, ((0, 0), (0, 128 - gains.shape[1])))
     edges = jnp.where(first_core, edges, gains) + swap(jnp.where(first_core, gains, edges))
-    s_edge = scattered(lambda cut_of: cut_of(edges, 0), D, True)
+
+    def blocks_of(g):
+        return g.astype(bf16).reshape(2, 2, planes, -1, g.shape[1])
+
+    wide, narrow = (5 * 128, 4 * 128)
+    jobs = (
+        (True, 0, 0, wide, True),
+        (True, 0, wide, narrow, False),
+        (True, 1, 0, wide, False),
+        (True, 1, wide, narrow, True),
+        (True, 2, 0, 128, True),
+        (False, 3, 0, 2 * HALF, True),
+        (False, 4, 0, HALF, True),
+        (False, 5, 0, 2 * HALF, True),
+    )
+    s_first, s_second, s_edge, s_cross, s_cq, s_side = chip_sums(
+        [blocks_of(g_first), blocks_of(g_second), blocks_of(edges)] + short, jobs, planes
+    )
+    s_square = jnp.concatenate([s_side[:, :HALF], s_cq, s_side[:, HALF:]], 1)
+    s_attend = jnp.concatenate([s_first, s_second], 1)
     s_edge = to_owner(s_edge, (rows, 2, 128), 1).reshape(rows, 256)
 
+    d_lead = d_lead + tie(s_first)
+    for axis, size, bit in reversed(hops):
+        d_lead = jnp.concatenate([d_lead, across(d_lead, axis, size, bit)], 0)
+    g_t2 = exact("ge,gd->ed", t_hidden.astype(f32), d_lead)
+    d_lead_here = lax.dynamic_slice(d_lead, (0, device * rows), (clips, rows))
+    g_timing = exact("gz,gd->zd", z_feat.astype(f32), d_lead_here)
+    d_t_hidden = exact("gd,ed->ge", d_lead, w_t2.astype(f32))
+    t_sig = jax.nn.sigmoid(t_pre)
+    d_t_pre = d_t_hidden * t_sig * (1.0 + t_pre * (1.0 - t_sig))
+    g_t1 = exact("gz,gd->zd", t_feat.astype(f32), d_t_pre)
     g_attend = to_owner(s_attend, attend_view, 3).transpose(0, 2, 3, 1, 4).reshape(rows, 3 * D)
     g_square = to_owner(s_square, square_view, 2).reshape(rows, 3, D).transpose(1, 0, 2)
     g_square = jnp.concatenate([g_square, g_t2[None]], 0)
     g_cross = to_owner(s_cross, cross_view, 2).reshape(cross_view[0], 2 * D)
-    g_up = to_owner(jnp.concatenate([s_gate, s_upper], 1).astype(f32), up_view, 3).reshape(rows, 2 * FF)
+    g_up = to_owner(jnp.concatenate([s_gate.astype(f32), s_upper.astype(f32) + tie(s_first)], 1), up_view, 3).reshape(rows, 2 * FF)
     g_down = s_down.astype(f32)
     g_edge = jnp.concatenate([s_edge[:, : 2 * C].T, g_t1, g_timing], 0)
     g_gain = s_edge[:, 2 * C : 2 * C + 4].T
-    sharded = (g_edge, g_attend, g_square, g_cross, g_up, g_down, g_gain)
+    sharded = lax.optimization_barrier(
+        (g_edge, g_attend, g_square, g_cross, g_up, g_down, g_gain)
+    )
+    g_gain = sharded[6]
     totals = jnp.stack([sum(jnp.sum(g * g) for g in sharded), loss_local])
     totals = totals + swap(totals)
     for axis, size, bit in hops:

time: 1530 us -> 1470 us (0.961)
  waiting for transfers between devices: 383 us -> 256 us
  Pallas kernels: 400 us -> 497 us
  starting transfers between devices: 89.9 us -> 41.2 us
  local copies, waits for them, and re-layouts: 123 us -> 141 us
    all_gather x2, waiting for transfers between devices: 153 us -> 0.01 us  [chip_body(): lax.all_gather(in_order(mine, swap(other)), peers, axis=0, tiled=True)]
    pallas_call x0 -> x1, Pallas kernels: none -> 97 us  [chip_sums(): pl.pallas_call(functools.partial(chip_sum_kernel, inputs=len(arrays), job...]
    ppermute x52 -> x30, waiting for transfers between devices: 121 us -> 183 us  [across(): return lax.ppermute(x, axis, [(i, i ^ bit) for i in range(size)])]
    ppermute x52 -> x30, starting transfers between devices: 82.4 us -> 33.5 us  [across(): return lax.ppermute(x, axis, [(i, i ^ bit) for i in range(size)])]
    all_gather x1, waiting for transfers between devices: 68.4 us -> 35.5 us  [chip_body(): down_w = lax.all_gather(down_weight.astype(bf16), peers, axis=0, tiled=True)]
    dot_general x17 -> x13, matrix products: 145 us -> 137 us  [dot_tn(): lax.dot_general(a, b, (((0,), (0,)), ((), ())), preferred_element_type=f32)]
  transfers between devices with their start and end apart: 90 -> 67, of which waited for: 42 -> 30; matrix products, arithmetic and copies ran while one was open for 29% -> 34% of each run, Pallas kernels for 24% -> 34%
where the time goes in v3:
time: 1470 us
  Pallas kernels  497 us (34%)
  matrix products  355 us (24%)
  waiting for transfers between devices  256 us (17%)
  other arithmetic  147 us (10%)
  local copies, waits for them, and re-layouts  141 us (10%)
  starting transfers between devices  41.2 us (3%)
  between operations  32.1 us (2%)
    pallas_call x9, Pallas kernels, call(): pl.pallas_call(kernel, grid=grid, in_specs=in_specs, out_specs=out_specs,...  400 us
    ppermute x30, waiting for transfers between devices, across(): return lax.ppermute(x, axis, [(i, i ^ bit) for i in range(size)])  183 us
    dot_general x14, matrix products, dot_nt(): lax.dot_general(a, b, (((1,), (1,)), ((), ())), preferred_element_type=f32)  146 us
    dot_general x13, matrix products, dot_tn(): lax.dot_general(a, b, (((0,), (0,)), ((), ())), preferred_element_type=f32)  137 us
    pallas_call x1, Pallas kernels, chip_sums(): pl.pallas_call(functools.partial(chip_sum_kernel, inputs=len(arrays), job...  97 us
    dot_general x13, matrix products, dot_nn(): lax.dot_general(a, b, (((1,), (0,)), ((), ())), preferred_element_type=f32)  68 us
    ppermute x31, waiting for transfers between devices, swap(): return lax.ppermute(x, 'core', [(0, 1), (1, 0)])  37.2 us
    all_gather x1, waiting for transfers between devices, chip_body(): down_w = lax.all_gather(down_weight.astype(bf16), peers, axis=0, tiled=True)  35.5 us
  transfers between devices with their start and end apart: 67, of which 30 were waited for; matrix products, arithmetic and copies ran while one was open for 34% of the time, Pallas kernels for 34%

profile of v3, /device:TPU:0, one launch (start us, length us, event | category | flops | bytes accessed | tf_op | source)
XLA Modules:
  0.0 1468.3 jit_solution(12786928399514175058)
XLA Ops:
  16.5 10.0 dynamic-slice_reduce_fusion.1
  84.1 40.6 %collective-permute-done.15 = bf16[96,3072]{1,0:T(8,128)(2,1)S(1)} collective-permute-done((bf16[96,3072]{1,0:T(8,128)(2,1)S(1)}, bf16[96,3072]{1,0:T(8,128)(2,1)S(1)}, u32[]{:S(2)}, u32[]{:S(2)}) %collective-permute-start.15) | collective-permute-done | bytes 589856 | tf_op jit(solution)/shard_map/ppermute | solution.py:1109
  124.8 25.6 %collective-permute-done.16 = bf16[96,3072]{1,0:T(8,128)(2,1)S(1)} collective-permute-done((bf16[96,3072]{1,0:T(8,128)(2,1)S(1)}, bf16[96,3072]{1,0:T(8,128)(2,1)S(1)}, u32[]{:S(2)}, u32[]{:S(2)}) %collective-permute-start.16) | collective-permute-done | bytes 589856 | tf_op jit(solution)/shard_map/ppermute | solution.py:1109
  177.1 33.8 %collective-permute-done.19 = bf16[4,96,3072]{2,1,0:T(8,128)(2,1)} collective-permute-done((bf16[4,96,3072]{2,1,0:T(8,128)(2,1)S(1)}, bf16[4,96,3072]{2,1,0:T(8,128)(2,1)}, u32[]{:S(2)}, u32[]{:S(2)}) %collective-permute-start.19) | collective-permute-done | bytes 2359328 | tf_op jit(solution)/shard_map/ppermute | solution.py:1109
  224.6 38.3 %collective-permute-done.20 = bf16[2,96,3072]{2,1,0:T(8,128)(2,1)S(1)} collective-permute-done((bf16[2,96,3072]{2,1,0:T(8,128)(2,1)S(1)}, bf16[2,96,3072]{2,1,0:T(8,128)(2,1)S(1)}, u32[]{:S(2)}, u32[]{:S(2)}) %collective-permute-start.20) | collective-permute-done | bytes 1179680 | tf_op jit(solution)/shard_map/ppermute | solution.py:1109
  270.2 10.2 shard_map.452
  285.2 36.4 %shard_map.453.q_ref.k_ref.v_ref.refs_0_.refs_7_.refs_8_ = bf16[2048,2304]{1,0:T(8,128)(2,1)} custom-call(bf16[2048,1536]{1,0:T(8,128)(2,1)} %get-tuple-element.58.n_ref, bf16[1536,2560]{1,0:T(8,128)(2,1)} %all-gather.4.cloned.1.call-done.w_ref, f32[2048,128]{1,0:T(8,128)} %broadcast_select_fusion.1.cos_ref.refs_4_.refs_11_, ...), custom_call_target="tpu_custom_call" | custom-call | flops 14495514624 | bytes 25165824 | tf_op jit(solution)/shard_map/pallas_call | solution.py:529
  321.5 73.2 %shard_map.454 = (bf16[2048,768]{1,0:T(8,128)(2,1)}, f32[6,2,2048]{2,1,0:T(2,128)}) custom-call(bf16[2048,2304]{1,0:T(8,128)(2,1)} %shard_map.453.q_ref.k_ref.v_ref.refs_0_.refs_7_.refs_8_, bf16[2048,2304]{1,0:T(8,128)(2,1)} %shard_map.453.q_ref.k_ref.v_ref.refs_0_.refs_7_.refs_8_, bf16[2048,2304]{1,0:T(8,128)(2,1)} %shard_map.453.q_ref.k_ref.v_ref.refs_0_.refs_7_.refs_8_, ...), custom_call_target="tpu_custom_call" | custom-call | flops 51539607552 | bytes 31457280 | tf_op jit(solution)/shard_map/pallas_call | solution.py:529
  396.6 7.9 broadcast_add_fusion
  404.5 5.8 fusion.188
  416.8 5.5 collective-permute-done.23
  439.8 9.4 fusion.44.q_ref
  449.2 14.0 shard_map.455
  468.6 5.3 collective-permute-done.27
  482.5 5.3 collective-permute-done.28
  492.6 55.4 %shard_map.456 = (bf16[2048,3072]{1,0:T(8,128)(2,1)}, bf16[2048,3072]{1,0:T(8,128)(2,1)}, bf16[2048,3072]{1,0:T(8,128)(2,1)}) custom-call(bf16[2048,1536]{1,0:T(8,128)(2,1)} %pad_maximum_fusion.2.n_ref, bf16[1536,6144]{1,0:T(8,128)(2,1)} %all-gather.6.cloned.1.call-done.wg_ref.wu_ref, bf16[1536,6144]{1,0:T(8,128)(2,1)} %all-gather.6.cloned.1.call-done.wg_ref.wu_ref), custom_call_target="tpu_custom_call" | custom-call | flops 38654705664 | bytes 69206016 | tf_op jit(solution)/shard_map/pallas_call | solution.py:529
  548.0 35.5 %all-gather.8.cloned.1.call-done.w_ref = bf16[3072,1536]{1,0:T(8,128)(2,1)} async-done(((bf16[192,1536]{1,0:T(8,128)(2,1)}), bf16[3072,1536]{1,0:T(8,128)(2,1)}) %all-gather.8.cloned.1.call-update) | async-done | bytes 9437200 | tf_op jit(solution)/shard_map/all_gather | solution.py:1197
  583.5 15.9 %fusion.37 = bf16[1024,1536]{1,0:T(8,128)(2,1)} fusion(bf16[3072,1536]{1,0:T(8,128)(2,1)} %all-gather.8.cloned.1.call-done.w_ref, bf16[2048,3072]{1,0:T(8,128)(2,1)} %get-tuple-element.61), kind=kOutput, calls=%fused_computation.86 | convolution fusion | flops 9665249280 | bytes 18874368 | tf_op jit(solution)/shard_map/dot_general | solution.py:521
  605.5 17.4 %fusion.198 = (f32[1024]{0:T(1024)S(1)}, f32[1024,1536]{1,0:T(8,128)S(1)}) fusion(f32[1024,1536]{1,0:T(8,128)} %copy-done.1, bf16[1024,1536]{1,0:T(8,128)(2,1)} %collective-permute-done.30, bf16[3072,1536]{1,0:T(8,128)(2,1)} %all-gather.8.cloned.1.call-done.w_ref, bf16[2048,3072]{1,0:T(8,128)(2,1)} %get-tuple-element.61), kind=kOutput, calls=%fused_computation.479 | convolution fusion | flops 9669966848 | bytes 31461376 | tf_op jit(solution)/shard_map/dot_general | solution.py:521
  636.0 5.5 collective-permute-done.31
  643.1 24.2 %convolution_convert_fusion.after_ref = bf16[3072,1536]{1,0:T(8,128)(2,1)} fusion(bf16[2048,3072]{1,0:T(8,128)(2,1)} %get-tuple-element.61, bf16[1024,1536]{1,0:T(8,128)(2,1)S(1)} %collective-permute-done.31, bf16[1024,1536]{1,0:T(8,128)(2,1)S(1)} %get-tuple-element.260), kind=kOutput, calls=%fused_computation | convolution fusion | flops 19344654336 | bytes 28311552 | tf_op jit(solution)/shard_map/dot_general | solution.py:525
  672.3 39.8 %shard_map.457 = (bf16[2048,3072]{1,0:T(8,128)(2,1)}, bf16[2048,3072]{1,0:T(8,128)(2,1)}) custom-call(bf16[2048,1536]{1,0:T(8,128)(2,1)} %pad_maximum_fusion.3.d_ref, bf16[3072,1536]{1,0:T(8,128)(2,1)} %all-gather.8.cloned.1.call-done.w_ref, bf16[2048,3072]{1,0:T(8,128)(2,1)} %get-tuple-element.62.gate_ref, bf16[2048,3072]{1,0:T(8,128)(2,1)} %get-tuple-element.63.up_ref, ...), custom_call_target="tpu_custom_call" | custom-call | flops 19327352832 | bytes 72351744 | tf_op jit(solution)/shard_map/pallas_call | solution.py:529
  712.1 14.6 fusion
  726.7 16.0 %add_convert_fusion.2 = bf16[1024,1536]{1,0:T(8,128)(2,1)} fusion(f32[1024,1536]{1,0:T(8,128)S(1)} %fusion, bf16[1536,6144]{1,0:T(8,128)(2,1)} %all-gather.6.cloned.1.call-done.wg_ref.wu_ref, bf16[2048,3072]{1,0:T(8,128)(2,1)} %get-tuple-element.64), kind=kOutput, calls=%fused_computation.44 | convolution fusion | flops 9666822144 | bytes 25165824 | tf_op jit(solution)/shard_map/dot_general | solution.py:517
  742.8 24.2 %convolution_convert_fusion.2 = bf16[1536,3072]{1,0:T(8,128)(2,1)} fusion(bf16[2048,3072]{1,0:T(8,128)(2,1)} %get-tuple-element.64, bf16[1024,1536]{1,0:T(8,128)(2,1)S(1)} %copy-done.34, bf16[1024,1536]{1,0:T(8,128)(2,1)S(1)} %copy-done.14), kind=kOutput, calls=%fused_computation.2 | convolution fusion | flops 19344654336 | bytes 28311552 | tf_op jit(solution)/shard_map/dot_general | solution.py:525
  767.0 16.0 %fusion.2 = f32[1024,1536]{1,0:T(8,128)} fusion(bf16[1536,6144]{1,0:T(8,128)(2,1)} %all-gather.6.cloned.1.call-done.wg_ref.wu_ref, bf16[2048,3072]{1,0:T(8,128)(2,1)} %get-tuple-element.65), kind=kOutput, calls=%fused_computation.16 | convolution fusion | flops 9663676416 | bytes 22020096 | tf_op jit(solution)/shard_map/dot_general | solution.py:517
  783.1 22.0 %multiply_reduce_fusion.1 = (f32[1536]{0:T(1024)S(1)}, f32[1024]{0:T(1024)S(1)}, f32[1024]{0:T(1024)S(1)}, f32[1024,1536]{1,0:T(8,128)}) fusion(f32[1024,1536]{1,0:T(8,128)} %copy-done.1, f32[1024]{0:T(1024)S(1)} %copy-done.118, f32[1024]{0:T(1024)S(1)} %copy-done.105, f32[1536]{0:T(1024)S(1)} %copy-done.101, ...), kind=kOutput, calls=%fused_computation.30 | convolution fusion | flops 9680973824 | bytes 37777408 | tf_op jit(solution)/shard_map/dot_general | solution.py:517
  805.1 11.4 fusion.185
  823.0 11.2 fusion.40.g_ref
  834.3 18.3 %shard_map.458 = (bf16[2048,768]{1,0:T(8,128)(2,1)}, f32[128,768]{1,0:T(8,128)}, f32[128,768]{1,0:T(8,128)}) custom-call(bf16[2048,768]{1,0:T(8,128)(2,1)} %fusion.44.q_ref, bf16[2048,768]{1,0:T(8,128)(2,1)} %fusion.40.g_ref, bf16[128,1536]{1,0:T(8,128)(2,1)} %convolution_convert_fusion.7.k_ref.v_ref, ...), custom_call_target="tpu_custom_call" | custom-call | flops 6442450944 | bytes 25165824 | tf_op jit(solution)/shard_map/pallas_call | solution.py:529
  852.6 6.6 convolution_convert_fusion.3
  869.0 6.8 fusion.83
  877.9 8.6 fusion.41
  889.3 7.5 multiply_reduce_fusion.2
  902.0 25.4 %convolution_convert_fusion.1 = bf16[1536,3072]{1,0:T(8,128)(2,1)} fusion(bf16[2048,3072]{1,0:T(8,128)(2,1)} %get-tuple-element.65, bf16[1024,1536]{1,0:T(8,128)(2,1)S(1)} %copy-done.35, bf16[1024,1536]{1,0:T(8,128)(2,1)S(1)} %copy-done.14), kind=kOutput, calls=%fused_computation.1 | convolution fusion | flops 19344654336 | bytes 28311552 | tf_op jit(solution)/shard_map/dot_general | solution.py:525
  931.6 6.2 fusion.93.refs_15_
  941.2 8.4 fusion.43
  951.2 9.6 fusion.42.refs_1_
  964.9 76.3 %shard_map.459 = (bf16[2048,384]{1,0:T(8,128)(2,1)}, bf16[2048,384]{1,0:T(8,128)(2,1)}, bf16[2048,384]{1,0:T(8,128)(2,1)}, f32[16,384]{1,0:T(8,128)}, f32[16,384]{1,0:T(8,128)}) custom-call(bf16[2048,2304]{1,0:T(8,128)(2,1)} %shard_map.453.q_ref.k_ref.v_ref.refs_0_.refs_7_.refs_8_, bf16[2048,768]{1,0:T(8,128)(2,1)} %fusion.42.refs_1_, ...), custom_call_target="tpu_custom_call" | custom-call | flops 51539607552 | bytes 31457280 | tf_op jit(solution)/shard_map/pallas_call | solution.py:529
  1043.0 6.4 add_convert_fusion.6
  1057.7 6.3 fusion.59
  1064.0 6.2 fusion.61
  1071.5 10.2 fusion.8.refs_17_
  1087.3 76.3 %shard_map.460 = (bf16[2048,384]{1,0:T(8,128)(2,1)}, bf16[2048,384]{1,0:T(8,128)(2,1)}, bf16[2048,384]{1,0:T(8,128)(2,1)}, f32[16,384]{1,0:T(8,128)}, f32[16,384]{1,0:T(8,128)}) custom-call(bf16[2048,2304]{1,0:T(8,128)(2,1)} %shard_map.453.q_ref.k_ref.v_ref.refs_0_.refs_7_.refs_8_, bf16[2048,768]{1,0:T(8,128)(2,1)} %fusion.42.refs_1_, ...), custom_call_target="tpu_custom_call" | custom-call | flops 51539607552 | bytes 31457280 | tf_op jit(solution)/shard_map/pallas_call | solution.py:529
  1166.4 10.8 add_convert_fusion.1
  1181.0 13.4 fusion.9
  1201.1 13.2 multiply_reduce_fusion.3
  1233.7 97.0 %shard_map.461 = (f32[96,1152]{1,0:T(8,128)}, f32[96,1152]{1,0:T(8,128)}, f32[96,128]{1,0:T(8,128)}, f32[48,1536]{1,0:T(8,128)}, f32[96,768]{1,0:T(8,128)}, /*index=5*/f32[96,1536]{1,0:T(8,128)}) custom-call(bf16[2,2,4,96,1152]{4,3,2,1,0:T(8,128)(2,1)} %bitcast.239, bf16[2,2,4,96,1152]{4,3,2,1,0:T(8,128)(2,1)} %bitcast.240, ...), custom_call_target="tpu_custom_call" | custom-call | flops 99999997952 | bytes 10000000 | tf_op jit(solution)/shard_map/pallas_call | solution.py:1071
  (778 shorter events, 392.3 us)
Async XLA Ops:
  7.2 257.9 %all-gather.4.cloned.1.call-start = ((), (), s32[]{:S(2)}) async-start(), calls=%async_computation.3 | async-start | bytes 8355840 | tf_op jit(solution)/shard_map/all_gather | solution.py:1186
  14.2 478.4 %all-gather.6.cloned.1.call-start = ((), (), s32[]{:S(2)}) async-start(), calls=%async_computation.4 | async-start | bytes 20054016 | tf_op jit(solution)/shard_map/all_gather | solution.py:1196
  31.8 551.7 %all-gather.8.cloned.1.call-start = ((), (), s32[]{:S(2)}) async-start(), calls=%async_computation.5 | async-start | bytes 10027008 | tf_op jit(solution)/shard_map/all_gather | solution.py:1197
  32.7 13.2 collective-permute-start
  35.4 29.9 %collective-permute-start.14 = (bf16[24,1536]{1,0:T(8,128)(2,1)}, bf16[24,1536]{1,0:T(8,128)(2,1)}, u32[]{:S(2)}, u32[]{:S(2)}) collective-permute-start(bf16[24,1536]{1,0:T(8,128)(2,1)} %bitcast.91), channel_id=1, source_target_pairs={{0,1},{1,0},{2,3},{3,2},{4,5},{5,4},{6,7},{7,6},{8,9},{9,8},{10,11... | collective-permute-start | bytes 221192 | tf_op jit(solution)/shard_map/ppermute | solution.py:1106
  36.3 42.7 %collective-permute-start.3 = (bf16[2,512,64]{1,2,0:T(8,128)(2,1)}, bf16[2,512,64]{1,2,0:T(8,128)(2,1)S(1)}, u32[]{:S(2)}, u32[]{:S(2)}) collective-permute-start(bf16[2,512,64]{1,2,0:T(8,128)(2,1)} %get-tuple-element.297), channel_id=1, source_target_pairs={{0,8},{8,0},{16,24},{24,16},{1,9},{9,1},{17,25},{25,17},{2,10},{10... | collective-permute-start | bytes 393224 | tf_op jit(solution)/shard_map/ppermute | solution.py:1109
  39.1 39.8 %collective-permute-start.4 = (bf16[2,512,64]{1,2,0:T(8,128)(2,1)}, bf16[2,512,64]{1,2,0:T(8,128)(2,1)S(1)}, u32[]{:S(2)}, u32[]{:S(2)}) collective-permute-start(bf16[2,512,64]{1,2,0:T(8,128)(2,1)} %get-tuple-element.298), channel_id=1, source_target_pairs={{0,16},{8,24},{16,0},{24,8},{1,17},{9,25},{17,1},{25,9},{2,18},{10... | collective-permute-start | bytes 393224 | tf_op jit(solution)/shard_map/ppermute | solution.py:1109
  40.7 38.3 %collective-permute-start.5 = (bf16[2,512,64]{1,2,0:T(8,128)(2,1)}, bf16[2,512,64]{1,2,0:T(8,128)(2,1)}, u32[]{:S(2)}, u32[]{:S(2)}) collective-permute-start(bf16[2,512,64]{1,2,0:T(8,128)(2,1)} %get-tuple-element.299), channel_id=1, source_target_pairs={{0,24},{8,16},{16,8},{24,0},{1,25},{9,17},{17,9},{25,1},{2,26},{10... | collective-permute-start | bytes 393224 | tf_op jit(solution)/shard_map/ppermute | solution.py:1109
  57.7 7.5 collective-permute-start.8
  65.3 10.9 collective-permute-start.13
  65.3 6.1 collective-permute-start.9
  76.3 48.5 %collective-permute-start.15 = (bf16[96,3072]{1,0:T(8,128)(2,1)S(1)}, bf16[96,3072]{1,0:T(8,128)(2,1)S(1)}, u32[]{:S(2)}, u32[]{:S(2)}) collective-permute-start(bf16[96,3072]{1,0:T(8,128)(2,1)S(1)} %maximum_maximum_fusion), channel_id=1, source_target_pairs={{0,2},{2,0},{4,6},{6,4},{1,3},{3,1},{5,7},{7,5},{8,10},{10,8},{12,... | collective-permute-start | bytes 1769480 | tf_op jit(solution)/shard_map/ppermute | solution.py:1109
  78.9 80.1 %collective-permute-start.12 = (f32[1,1536]{1,0:T(1,128)S(1)}, f32[1,1536]{1,0:T(1,128)S(1)}, u32[]{:S(2)}, u32[]{:S(2)}) collective-permute-start(f32[1,1536]{1,0:T(1,128)S(1)} %slice_add_fusion.4), channel_id=1, source_target_pairs={{0,1},{1,0},{2,3},{3,2},{4,5},{5,4},{6,7},{7,6},{8,9},{9,8},{10,11... | collective-permute-start | bytes 18440 | tf_op jit(solution)/shard_map/ppermute | solution.py:1106
  80.8 83.7 %collective-permute-start.6 = (bf16[2,4,512,64]{2,3,1,0:T(8,128)(2,1)}, bf16[2,4,512,64]{2,3,1,0:T(8,128)(2,1)}, u32[]{:S(2)}, u32[]{:S(2)}) collective-permute-start(bf16[2,4,512,64]{2,3,1,0:T(8,128)(2,1)} %pad_maximum_fusion.23), channel_id=1, source_target_pairs={{0,1},{1,0},{2,3},{3,2},{4,5},{5,4},{6,7},{7,6},{8,9},{9,8},{10,11... | collective-permute-start | bytes 1572872 | tf_op jit(solution)/shard_map/ppermute | solution.py:1106
  81.2 69.2 %collective-permute-start.16 = (bf16[96,3072]{1,0:T(8,128)(2,1)S(1)}, bf16[96,3072]{1,0:T(8,128)(2,1)S(1)}, u32[]{:S(2)}, u32[]{:S(2)}) collective-permute-start(bf16[96,3072]{1,0:T(8,128)(2,1)S(1)} %maximum_maximum_fusion), channel_id=1, source_target_pairs={{0,4},{2,6},{4,0},{6,2},{1,5},{3,7},{5,1},{7,3},{8,12},{10,14},{12... | collective-permute-start | bytes 1769480 | tf_op jit(solution)/shard_map/ppermute | solution.py:1109
  82.9 72.3 %collective-permute-start.17 = (bf16[96,3072]{1,0:T(8,128)(2,1)S(1)}, bf16[96,3072]{1,0:T(8,128)(2,1)S(1)}, u32[]{:S(2)}, u32[]{:S(2)}) collective-permute-start(bf16[96,3072]{1,0:T(8,128)(2,1)S(1)} %maximum_maximum_fusion), channel_id=1, source_target_pairs={{0,6},{2,4},{4,2},{6,0},{1,7},{3,5},{5,3},{7,1},{8,14},{10,12},{12... | collective-permute-start | bytes 1769480 | tf_op jit(solution)/shard_map/ppermute | solution.py:1109
  155.3 55.6 %collective-permute-start.19 = (bf16[4,96,3072]{2,1,0:T(8,128)(2,1)S(1)}, bf16[4,96,3072]{2,1,0:T(8,128)(2,1)}, u32[]{:S(2)}, u32[]{:S(2)}) collective-permute-start(bf16[4,96,3072]{2,1,0:T(8,128)(2,1)S(1)} %bitcast_dynamic-update-slice_fusion.5), channel_id=1, source_target_pairs={{0,16},{8,24},{16,0},{24,8},{1,17},{9,25},{17,1},{25,9},{2,18},{10... | collective-permute-start | bytes 7077896 | tf_op jit(solution)/shard_map/ppermute | solution.py:1109
  156.7 58.3 %collective-permute-start.18 = (bf16[4,96,3072]{2,1,0:T(8,128)(2,1)S(1)}, bf16[4,96,3072]{2,1,0:T(8,128)(2,1)}, u32[]{:S(2)}, u32[]{:S(2)}) collective-permute-start(bf16[4,96,3072]{2,1,0:T(8,128)(2,1)S(1)} %bitcast_dynamic-update-slice_fusion.5), channel_id=1, source_target_pairs={{0,8},{8,0},{16,24},{24,16},{1,9},{9,1},{17,25},{25,17},{2,10},{10... | collective-permute-start | bytes 7077896 | tf_op jit(solution)/shard_map/ppermute | solution.py:1109
  212.3 50.6 %collective-permute-start.20 = (bf16[2,96,3072]{2,1,0:T(8,128)(2,1)S(1)}, bf16[2,96,3072]{2,1,0:T(8,128)(2,1)S(1)}, u32[]{:S(2)}, u32[]{:S(2)}) collective-permute-start(bf16[2,96,3072]{2,1,0:T(8,128)(2,1)S(1)} %slice.380), channel_id=1, source_target_pairs={{0,8},{8,0},{16,24},{24,16},{1,9},{9,1},{17,25},{25,17},{2,10},{10... | collective-permute-start | bytes 3538952 | tf_op jit(solution)/shard_map/ppermute | solution.py:1109
  216.4 47.6 %collective-permute-start.21 = (bf16[2,96,3072]{2,1,0:T(8,128)(2,1)S(1)}, bf16[2,96,3072]{2,1,0:T(8,128)(2,1)S(1)}, u32[]{:S(2)}, u32[]{:S(2)}) collective-permute-start(bf16[2,96,3072]{2,1,0:T(8,128)(2,1)S(1)} %slice.381), channel_id=1, source_target_pairs={{0,16},{8,24},{16,0},{24,8},{1,17},{9,25},{17,1},{25,9},{2,18},{10... | collective-permute-start | bytes 3538952 | tf_op jit(solution)/shard_map/ppermute | solution.py:1109
  429.0 10.9 collective-permute-start.24
  430.6 797.5 %reduce-scatter.8.cloned.1.call-start = ((), (), s32[]{:S(2)}) async-start(), calls=%async_computation.8 | async-start | bytes 10027008 | tf_op jit(solution)/shard_map/reduce_scatter | solution.py:1360
  438.3 25.0 %collective-permute-start.26 = (bf16[768,768]{1,0:T(8,128)(2,1)}, bf16[768,768]{1,0:T(8,128)(2,1)}, u32[]{:S(2)}, u32[]{:S(2)}) collective-permute-start(bf16[768,768]{1,0:T(8,128)(2,1)} %get-tuple-element.278), channel_id=1, source_target_pairs={{0,1},{1,0},{2,3},{3,2},{4,5},{5,4},{6,7},{7,6},{8,9},{9,8},{10,11... | collective-permute-start | bytes 3538952 | tf_op jit(solution)/shard_map/ppermute | solution.py:1106
  482.0 5.7 collective-permute-start.28
  599.5 6.0 collective-permute-start.30
  667.4 561.9 %reduce-scatter.4.cloned.1.call-start = ((), (), s32[]{:S(2)}) async-start(), calls=%async_computation.6 | async-start | bytes 10027008 | tf_op jit(solution)/shard_map/reduce_scatter | solution.py:1360
  742.7 40.3 %collective-permute-start.32 = (bf16[1024,1536]{1,0:T(8,128)(2,1)}, bf16[1024,1536]{1,0:T(8,128)(2,1)}, u32[]{:S(2)}, u32[]{:S(2)}) collective-permute-start(bf16[1024,1536]{1,0:T(8,128)(2,1)} %add_convert_fusion.2), channel_id=1, source_target_pairs={{0,1},{1,0},{2,3},{3,2},{4,5},{5,4},{6,7},{7,6},{8,9},{9,8},{10,11... | collective-permute-start | bytes 9437192 | tf_op jit(solution)/shard_map/ppermute | solution.py:1106
  767.0 565.6 %reduce-scatter.6.cloned.1.call-start = ((), (), s32[]{:S(2)}) async-start(), calls=%async_computation.7 | async-start | bytes 10027008 | tf_op jit(solution)/shard_map/reduce_scatter | solution.py:1360
  816.4 6.6 collective-permute-start.33
  859.2 29.0 %collective-permute-start.34 = (bf16[1024,1536]{1,0:T(8,128)(2,1)}, bf16[1024,1536]{1,0:T(8,128)(2,1)}, u32[]{:S(2)}, u32[]{:S(2)}) collective-permute-start(bf16[1024,1536]{1,0:T(8,128)(2,1)} %convolution_convert_fusion.3), channel_id=1, source_target_pairs={{0,1},{1,0},{2,3},{3,2},{4,5},{5,4},{6,7},{7,6},{8,9},{9,8},{10,11... | collective-permute-start | bytes 9437192 | tf_op jit(solution)/shard_map/ppermute | solution.py:1106
  888.1 50.3 %collective-permute-start.37 = (bf16[768,768]{1,0:T(8,128)(2,1)}, bf16[768,768]{1,0:T(8,128)(2,1)}, u32[]{:S(2)}, u32[]{:S(2)}) collective-permute-start(bf16[768,768]{1,0:T(8,128)(2,1)} %get-tuple-element.274), channel_id=1, source_target_pairs={{0,1},{1,0},{2,3},{3,2},{4,5},{5,4},{6,7},{7,6},{8,9},{9,8},{10,11... | collective-permute-start | bytes 3538952 | tf_op jit(solution)/shard_map/ppermute | solution.py:1106
  901.7 39.5 %collective-permute-start.35 = (bf16[1024,1536]{1,0:T(8,128)(2,1)}, bf16[1024,1536]{1,0:T(8,128)(2,1)}, u32[]{:S(2)}, u32[]{:S(2)}) collective-permute-start(bf16[1024,1536]{1,0:T(8,128)(2,1)} %get-tuple-element.256), channel_id=1, source_target_pairs={{0,1},{1,0},{2,3},{3,2},{4,5},{5,4},{6,7},{7,6},{8,9},{9,8},{10,11... | collective-permute-start | bytes 9437192 | tf_op jit(solution)/shard_map/ppermute | solution.py:1106
  930.1 120.9 %collective-permute-start.38 = (bf16[384,1536]{1,0:T(8,128)(2,1)}, bf16[384,1536]{1,0:T(8,128)(2,1)S(1)}, u32[]{:S(2)}, u32[]{:S(2)}) collective-permute-start(bf16[384,1536]{1,0:T(8,128)(2,1)} %convolution_convert_fusion.6.refs_14_), channel_id=1, source_target_pairs={{0,8},{8,0},{16,24},{24,16},{1,9},{9,1},{17,25},{25,17},{2,10},{10... | collective-permute-start | bytes 3538952 | tf_op jit(solution)/shard_map/ppermute | solution.py:1109
  937.8 105.2 %collective-permute-start.39 = (bf16[768,768]{1,0:T(8,128)(2,1)}, bf16[768,768]{1,0:T(8,128)(2,1)}, u32[]{:S(2)}, u32[]{:S(2)}) collective-permute-start(bf16[768,768]{1,0:T(8,128)(2,1)} %fusion.93.refs_15_), channel_id=1, source_target_pairs={{0,8},{8,0},{16,24},{24,16},{1,9},{9,1},{17,25},{25,17},{2,10},{10... | collective-permute-start | bytes 3538952 | tf_op jit(solution)/shard_map/ppermute | solution.py:1109
  949.8 11.0 collective-permute-start.36
  963.6 118.1 %collective-permute-start.40 = (bf16[768,1536]{1,0:T(8,128)(2,1)}, bf16[768,1536]{1,0:T(8,128)(2,1)}, u32[]{:S(2)}, u32[]{:S(2)}) collective-permute-start(bf16[768,1536]{1,0:T(8,128)(2,1)} %fusion.67.refs_16_), channel_id=1, source_target_pairs={{0,16},{8,24},{16,0},{24,8},{1,17},{9,25},{17,1},{25,9},{2,18},{10... | collective-permute-start | bytes 7077896 | tf_op jit(solution)/shard_map/ppermute | solution.py:1109
  1050.3 171.4 %collective-permute-start.45 = (bf16[384,768]{1,0:T(8,128)(2,1)}, bf16[384,768]{1,0:T(8,128)(2,1)}, u32[]{:S(2)}, u32[]{:S(2)}) collective-permute-start(bf16[384,768]{1,0:T(8,128)(2,1)} %constant_dynamic-slice_fusion.5.refs_15_), channel_id=1, source_target_pairs={{0,16},{8,24},{16,0},{24,8},{1,17},{9,25},{17,1},{25,9},{2,18},{10... | collective-permute-start | bytes 1769480 | tf_op jit(solution)/shard_map/ppermute | solution.py:1109
  1054.9 164.7 %collective-permute-start.44 = (bf16[192,1536]{1,0:T(8,128)(2,1)}, bf16[192,1536]{1,0:T(8,128)(2,1)}, u32[]{:S(2)}, u32[]{:S(2)}) collective-permute-start(bf16[192,1536]{1,0:T(8,128)(2,1)} %constant_dynamic-slice_fusion.6.refs_14_), channel_id=1, source_target_pairs={{0,16},{8,24},{16,0},{24,8},{1,17},{9,25},{17,1},{25,9},{2,18},{10... | collective-permute-start | bytes 1769480 | tf_op jit(solution)/shard_map/ppermute | solution.py:1109
  1086.6 138.5 %collective-permute-start.46 = (bf16[384,1536]{1,0:T(8,128)(2,1)}, bf16[384,1536]{1,0:T(8,128)(2,1)}, u32[]{:S(2)}, u32[]{:S(2)}) collective-permute-start(bf16[384,1536]{1,0:T(8,128)(2,1)} %constant_dynamic-slice_fusion.4.refs_16_), channel_id=1, source_target_pairs={{0,8},{8,0},{16,24},{24,16},{1,9},{9,1},{17,25},{25,17},{2,10},{10... | collective-permute-start | bytes 3538952 | tf_op jit(solution)/shard_map/ppermute | solution.py:1109
  1177.2 23.8 %collective-permute-start.41 = (bf16[1024,1536]{1,0:T(8,128)(2,1)}, bf16[1024,1536]{1,0:T(8,128)(2,1)}, u32[]{:S(2)}, u32[]{:S(2)}) collective-permute-start(bf16[1024,1536]{1,0:T(8,128)(2,1)} %add_convert_fusion.1), channel_id=1, source_target_pairs={{0,1},{1,0},{2,3},{3,2},{4,5},{5,4},{6,7},{7,6},{8,9},{9,8},{10,11... | collective-permute-start | bytes 9437192 | tf_op jit(solution)/shard_map/ppermute | solution.py:1106
  1180.5 15.8 %collective-permute-start.42 = (f32[1,1536]{1,0:T(1,128)}, f32[1,1536]{1,0:T(1,128)}, u32[]{:S(2)}, u32[]{:S(2)}) collective-permute-start(f32[1,1536]{1,0:T(1,128)} %copy.289), channel_id=1, source_target_pairs={{0,1},{1,0},{2,3},{3,2},{4,5},{5,4},{6,7},{7,6},{8,9},{9,8},{10,11... | collective-permute-start | bytes 18440 | tf_op jit(solution)/shard_map/ppermute | solution.py:1106
  1219.5 12.0 collective-permute-start.43
  1342.4 11.5 collective-permute-start.48
  1343.8 10.2 collective-permute-start.47
  1347.8 15.9 %collective-permute-start.54 = (bf16[24,1536]{1,0:T(8,128)(2,1)}, bf16[24,1536]{1,0:T(8,128)(2,1)S(1)}, u32[]{:S(2)}, u32[]{:S(2)}) collective-permute-start(bf16[24,1536]{1,0:T(8,128)(2,1)} %dynamic-slice_convert_fusion.2), channel_id=1, source_target_pairs={{0,1},{1,0},{2,3},{3,2},{4,5},{5,4},{6,7},{7,6},{8,9},{9,8},{10,11... | collective-permute-start | bytes 221192 | tf_op jit(solution)/shard_map/ppermute | solution.py:1106
  1352.4 23.6 %collective-permute-start.53 = (bf16[48,2304]{1,0:T(8,128)(2,1)}, bf16[48,2304]{1,0:T(8,128)(2,1)}, u32[]{:S(2)}, u32[]{:S(2)}) collective-permute-start(bf16[48,2304]{1,0:T(8,128)(2,1)} %dynamic-slice_convert_fusion), channel_id=1, source_target_pairs={{0,1},{1,0},{2,3},{3,2},{4,5},{5,4},{6,7},{7,6},{8,9},{9,8},{10,11... | collective-permute-start | bytes 663560 | tf_op jit(solution)/shard_map/ppermute | solution.py:1106
  1352.4 40.2 %collective-permute-start.55 = (bf16[48,6144]{1,0:T(8,128)(2,1)}, bf16[48,6144]{1,0:T(8,128)(2,1)}, u32[]{:S(2)}, u32[]{:S(2)}) collective-permute-start(bf16[48,6144]{1,0:T(8,128)(2,1)} %fusion.99), channel_id=1, source_target_pairs={{0,1},{1,0},{2,3},{3,2},{4,5},{5,4},{6,7},{7,6},{8,9},{9,8},{10,11... | collective-permute-start | bytes 1769480 | tf_op jit(solution)/shard_map/ppermute | solution.py:1106
  1353.9 29.4 %collective-permute-start.52 = (bf16[48,2304]{1,0:T(8,128)(2,1)}, bf16[48,2304]{1,0:T(8,128)(2,1)}, u32[]{:S(2)}, u32[]{:S(2)}) collective-permute-start(bf16[48,2304]{1,0:T(8,128)(2,1)} %dynamic-slice_convert_fusion.1), channel_id=1, source_target_pairs={{0,1},{1,0},{2,3},{3,2},{4,5},{5,4},{6,7},{7,6},{8,9},{9,8},{10,11... | collective-permute-start | bytes 663560 | tf_op jit(solution)/shard_map/ppermute | solution.py:1106
  (194 other events, 2045.6 us)
Sparse Core Ops, SparseCore 0:
  14.3 152.9 all-gather.3
  170.6 245.9 all-gather.5
  430.7 152.8 all-gather.7
  667.5 169.2 reduce-scatter.7
  843.3 189.9 reduce-scatter.3
  1038.8 180.4 reduce-scatter.5

commit v4 on v3

--- a/solution.py
+++ b/solution.py
@@ -1141,36 +1141,6 @@
 
     y_at, x_at = (s_at // 2, s_at % 2)
 
-    def gather_chips(x, parts):
-        piece = x.shape[0] // parts
-        shape = (planes, piece, x.shape[1])
-        total = jnp.zeros((2, 2, parts) + shape, x.dtype).swapaxes(2, 3)
-
-        def put(total, block, y, column, z, part):
-            return lax.dynamic_update_slice(
-                total, block[None, None, :, None], (y, column, z, part, 0, 0)
-            )
-
-        for part in range(parts):
-            mine = x[part * piece : (part + 1) * piece]
-            block = lax.dynamic_update_slice(jnp.zeros(shape, x.dtype), mine[None], (z_at, 0, 0))
-            for offset in range(1, planes):
-                taken = across(mine, "z", planes, offset)
-                block = lax.dynamic_update_slice(block, taken[None], (z_at ^ offset, 0, 0))
-            from_x, from_y = (across(block, "seq", chips, 1), across(block, "seq", chips, 2))
-            half = planes // 2
-            first = across(from_y[:half], "seq", chips, 1)
-            second = across(from_x[half:], "seq", chips, 2)
-            for taken, y, column, z in (
-                (block, y_at, x_at, 0),
-                (from_x, y_at, 1 - x_at, 0),
-                (from_y, 1 - y_at, x_at, 0),
-                (first, 1 - y_at, 1 - x_at, 0),
-                (second, 1 - y_at, 1 - x_at, half),
-            ):
-                total = put(total, taken, y, column, z, part)
-        return (total.reshape(-1, x.shape[1]), block, from_x)
-
     rows = attend_weight.shape[0]
     attend_view = (rows, 2, 3, 2, THIRD)
     square_view = (rows, 3, 2, HALF)
@@ -1183,7 +1153,7 @@
     edge16 = jnp.pad(edge16, ((0, 0), (0, 256 - edge16.shape[1])))
     mine, other = halves_of(attend16, attend_view, 3)
     mine, other = (jnp.concatenate([mine, edge16], 1), jnp.concatenate([other, edge16], 1))
-    first_group = lax.all_gather(in_order(mine, swap(other)), peers, axis=0, tiled=True)
+    first_mine = in_order(mine, swap(other))
     mine, other = halves_of(
         square_weight[:3].astype(bf16).transpose(1, 0, 2), square_view, 2
     )
@@ -1191,7 +1161,10 @@
     mine, other = halves_of(cross_weight.astype(bf16), cross_view, 2)
     cross_mine = in_order(mine, swap(other))
     cross_mine = jnp.concatenate([cross_mine[:, :HALF], cross_mine[:, HALF:]], 0)
-    square_cols = gather_chips(jnp.concatenate([square_mine, cross_mine], 1), 1)[0]
+    first_group = lax.all_gather(
+        jnp.concatenate([first_mine, square_mine, cross_mine], 1), peers, axis=0, tiled=True
+    )
+    square_cols = first_group[:, first_mine.shape[1] :]
     mine, other = halves_of(upward_weight.astype(bf16), up_view, 3)
     up_w = lax.all_gather(in_order(mine, swap(other)), peers, axis=0, tiled=True)
     down_w = lax.all_gather(down_weight.astype(bf16), peers, axis=0, tiled=True)
@@ -1287,7 +1260,6 @@
     qkv = qkv_project(n1, first_group, tables)
     o, lse = attend_forward(qkv, kv_prefix)
 
-    square_cols = square_cols + tie(o).astype(bf16)
     cross_w = square_cols[:, 3 * HALF :].reshape(many, 2, CROSS // many, HALF)
     cross_w = jnp.concatenate(
         [cross_w[:, 0].reshape(CROSS, HALF), cross_w[:, 1].reshape(CROSS, HALF)], 1
@@ -1466,11 +1438,13 @@
     )
     s_square = jnp.concatenate([s_side[:, :HALF], s_cq, s_side[:, HALF:]], 1)
     s_attend = jnp.concatenate([s_first, s_second], 1)
+    s_edge_part = s_edge
     s_edge = to_owner(s_edge, (rows, 2, 128), 1).reshape(rows, 256)
 
     d_lead = d_lead + tie(s_first)
-    for axis, size, bit in reversed(hops):
-        d_lead = jnp.concatenate([d_lead, across(d_lead, axis, size, bit)], 0)
+    for axis, size in (("seq", chips), ("z", planes)):
+        taken = [across(d_lead, axis, size, offset) for offset in range(1, size)]
+        d_lead = jnp.concatenate([d_lead] + taken, 0)
     g_t2 = exact("ge,gd->ed", t_hidden.astype(f32), d_lead)
     d_lead_here = lax.dynamic_slice(d_lead, (0, device * rows), (clips, rows))
     g_timing = exact("gz,gd->zd", z_feat.astype(f32), d_lead_here)
@@ -1482,7 +1456,12 @@
     g_square = to_owner(s_square, square_view, 2).reshape(rows, 3, D).transpose(1, 0, 2)
     g_square = jnp.concatenate([g_square, g_t2[None]], 0)
     g_cross = to_owner(s_cross, cross_view, 2).reshape(cross_view[0], 2 * D)
-    g_up = to_owner(jnp.concatenate([s_gate.astype(f32), s_upper.astype(f32) + tie(s_first)], 1), up_view, 3).reshape(rows, 2 * FF)
+    s_upper = s_upper.astype(f32) + tie(s_first)
+    s_gate = s_gate.astype(f32)
+    half_view = (rows, many, 2, FF // (2 * many))
+    g_up = jnp.concatenate(
+        [to_owner(x, half_view, 2).reshape(rows, FF) for x in (s_gate, s_upper)], 1
+    )
     g_down = s_down.astype(f32)
     g_edge = jnp.concatenate([s_edge[:, : 2 * C].T, g_t1, g_timing], 0)
     g_gain = s_edge[:, 2 * C : 2 * C + 4].T
@@ -1490,7 +1469,9 @@
         (g_edge, g_attend, g_square, g_cross, g_up, g_down, g_gain)
     )
     g_gain = sharded[6]
-    totals = jnp.stack([sum(jnp.sum(g * g) for g in sharded), loss_local])
+    parts = (s_first, s_second, s_edge_part, s_cross, s_cq, s_side, s_gate, s_upper, g_down)
+    parts = parts + (g_t1, g_t2, g_timing)
+    totals = jnp.stack([sum(jnp.sum(g * g) for g in parts), loss_local])
     totals = totals + swap(totals)
     for axis, size, bit in hops:
         totals = totals + across(totals, axis, size, bit)

time: 1470 us -> 1450 us (0.986)
  local copies, waits for them, and re-layouts: 141 us -> 98.2 us
  Pallas kernels: 497 us -> 522 us
  other arithmetic: 147 us -> 123 us
    ppermute x30 -> x25, waiting for transfers between devices: 183 us -> 22 us  [across(): return lax.ppermute(x, axis, [(i, i ^ bit) for i in range(size)])]
    all_gather x0 -> x1, waiting for transfers between devices: none -> 138 us  [chip_body(): lax.all_gather(jnp.concatenate([first_mine, square_mine, cross_mine], 1),...]
    all_gather x1, waiting for transfers between devices: 35.5 us -> 62.6 us  [chip_body(): down_w = lax.all_gather(down_weight.astype(bf16), peers, axis=0, tiled=True)]
    pallas_call x1, Pallas kernels: 97 us -> 124 us  [chip_sums(): pl.pallas_call(functools.partial(chip_sum_kernel, inputs=len(arrays), job...]
    ppermute x31 -> x32, waiting for transfers between devices: 37.2 us -> 33.2 us  [swap(): return lax.ppermute(x, 'core', [(0, 1), (1, 0)])]
    ppermute x30 -> x25, starting transfers between devices: 33.5 us -> 36.3 us  [across(): return lax.ppermute(x, axis, [(i, i ^ bit) for i in range(size)])]
  transfers between devices with their start and end apart: 67 -> 63, of which waited for: 30 -> 25; matrix products, arithmetic and copies ran while one was open for 34% -> 30% of each run, Pallas kernels for 34% -> 34%
where the time goes in v4:
time: 1450 us; the launch traced here: 1440 us
  Pallas kernels  522 us (36%)
  matrix products  362 us (25%)
  waiting for transfers between devices  256 us (18%)
  other arithmetic  123 us (8%)
  local copies, waits for them, and re-layouts  98.2 us (7%)
  starting transfers between devices  43.4 us (3%)
  between operations  34.7 us (2%)
    pallas_call x9, Pallas kernels, call(): pl.pallas_call(kernel, grid=grid, in_specs=in_specs, out_specs=out_specs,...  398 us
    dot_general x14, matrix products, dot_nt(): lax.dot_general(a, b, (((1,), (1,)), ((), ())), preferred_element_type=f32)  152 us
    all_gather x1, waiting for transfers between devices, chip_body(): lax.all_gather(jnp.concatenate([first_mine, square_mine, cross_mine], 1),...  138 us
    dot_general x13, matrix products, dot_tn(): lax.dot_general(a, b, (((0,), (0,)), ((), ())), preferred_element_type=f32)  131 us
    pallas_call x1, Pallas kernels, chip_sums(): pl.pallas_call(functools.partial(chip_sum_kernel, inputs=len(arrays), job...  124 us
    dot_general x13, matrix products, dot_nn(): lax.dot_general(a, b, (((1,), (0,)), ((), ())), preferred_element_type=f32)  73.7 us
    all_gather x1, waiting for transfers between devices, chip_body(): down_w = lax.all_gather(down_weight.astype(bf16), peers, axis=0, tiled=True)  62.6 us
    ppermute x25, starting transfers between devices, across(): return lax.ppermute(x, axis, [(i, i ^ bit) for i in range(size)])  36.3 us
  transfers between devices with their start and end apart: 63, of which 25 were waited for; matrix products, arithmetic and copies ran while one was open for 30% of the time, Pallas kernels for 34%

profile of v4, /device:TPU:0, one launch (start us, length us, event | category | flops | bytes accessed | tf_op | source)
XLA Modules:
  0.0 1439.0 jit_solution(2959299819801308554)
XLA Ops:
  22.8 10.0 dynamic-slice_reduce_fusion.1
  82.5 138.3 %all-gather.4.cloned.1.call-done.w_ref = bf16[1536,5632]{1,0:T(8,128)(2,1)} async-done(((bf16[96,5632]{1,0:T(8,128)(2,1)}), bf16[1536,5632]{1,0:T(8,128)(2,1)}) %all-gather.4.cloned.1.call-update) | async-done | bytes 17301520 | tf_op jit(solution)/shard_map/all_gather | solution.py:1164
  226.0 5.8 fusion.186
  232.0 10.6 shard_map.452
  247.4 35.9 %shard_map.453.q_ref.k_ref.v_ref.refs_0_.refs_7_.refs_8_ = bf16[2048,2304]{1,0:T(8,128)(2,1)} custom-call(bf16[2048,1536]{1,0:T(8,128)(2,1)} %get-tuple-element.58.n_ref, bf16[1536,5632]{1,0:T(8,128)(2,1)} %all-gather.4.cloned.1.call-done.w_ref, f32[2048,128]{1,0:T(8,128)} %broadcast_select_fusion.1.cos_ref.refs_4_.refs_11_, ...), custom_call_target="tpu_custom_call" | custom-call | flops 14495514624 | bytes 25165824 | tf_op jit(solution)/shard_map/pallas_call | solution.py:529
  283.3 73.2 %shard_map.454 = (bf16[2048,768]{1,0:T(8,128)(2,1)}, f32[6,2,2048]{2,1,0:T(2,128)}) custom-call(bf16[2048,2304]{1,0:T(8,128)(2,1)} %shard_map.453.q_ref.k_ref.v_ref.refs_0_.refs_7_.refs_8_, bf16[2048,2304]{1,0:T(8,128)(2,1)} %shard_map.453.q_ref.k_ref.v_ref.refs_0_.refs_7_.refs_8_, bf16[2048,2304]{1,0:T(8,128)(2,1)} %shard_map.453.q_ref.k_ref.v_ref.refs_0_.refs_7_.refs_8_, ...), custom_call_target="tpu_custom_call" | custom-call | flops 51539607552 | bytes 31457280 | tf_op jit(solution)/shard_map/pallas_call | solution.py:529
  356.5 4.9 convolution_convert_fusion.5
  361.5 5.6 collective-permute-done.16
  367.2 6.4 fusion.194
  387.9 9.4 fusion.44.q_ref
  397.3 14.0 shard_map.455
  411.3 4.9 convolution_convert_fusion.4
  416.7 5.3 collective-permute-done.20
  430.6 5.3 collective-permute-done.21
  440.8 54.6 %shard_map.456 = (bf16[2048,3072]{1,0:T(8,128)(2,1)}, bf16[2048,3072]{1,0:T(8,128)(2,1)}, bf16[2048,3072]{1,0:T(8,128)(2,1)}) custom-call(bf16[2048,1536]{1,0:T(8,128)(2,1)} %pad_maximum_fusion.2.n_ref, bf16[1536,6144]{1,0:T(8,128)(2,1)} %all-gather.6.cloned.1.call-done.wg_ref.wu_ref, bf16[1536,6144]{1,0:T(8,128)(2,1)} %all-gather.6.cloned.1.call-done.wg_ref.wu_ref), custom_call_target="tpu_custom_call" | custom-call | flops 38654705664 | bytes 69206016 | tf_op jit(solution)/shard_map/pallas_call | solution.py:529
  495.3 62.6 %all-gather.8.cloned.1.call-done.w_ref = bf16[3072,1536]{1,0:T(8,128)(2,1)} async-done(((bf16[192,1536]{1,0:T(8,128)(2,1)}), bf16[3072,1536]{1,0:T(8,128)(2,1)}) %all-gather.8.cloned.1.call-update) | async-done | bytes 9437200 | tf_op jit(solution)/shard_map/all_gather | solution.py:1170
  557.9 15.9 %fusion.37 = bf16[1024,1536]{1,0:T(8,128)(2,1)} fusion(bf16[3072,1536]{1,0:T(8,128)(2,1)} %all-gather.8.cloned.1.call-done.w_ref, bf16[2048,3072]{1,0:T(8,128)(2,1)} %get-tuple-element.61), kind=kOutput, calls=%fused_computation.85 | convolution fusion | flops 9665249280 | bytes 18874368 | tf_op jit(solution)/shard_map/dot_general | solution.py:521
  579.8 17.2 %fusion.196 = (f32[1024]{0:T(1024)S(1)}, f32[1024,1536]{1,0:T(8,128)S(1)}) fusion(f32[1024,1536]{1,0:T(8,128)} %copy-done.1, bf16[1024,1536]{1,0:T(8,128)(2,1)} %collective-permute-done.23, bf16[3072,1536]{1,0:T(8,128)(2,1)} %all-gather.8.cloned.1.call-done.w_ref, bf16[2048,3072]{1,0:T(8,128)(2,1)} %get-tuple-element.61), kind=kOutput, calls=%fused_computation.471 | convolution fusion | flops 9669966848 | bytes 31461376 | tf_op jit(solution)/shard_map/dot_general | solution.py:521
  610.1 5.5 collective-permute-done.24
  617.3 24.2 %convolution_convert_fusion.after_ref = bf16[3072,1536]{1,0:T(8,128)(2,1)} fusion(bf16[2048,3072]{1,0:T(8,128)(2,1)} %get-tuple-element.61, bf16[1024,1536]{1,0:T(8,128)(2,1)S(1)} %collective-permute-done.24, bf16[1024,1536]{1,0:T(8,128)(2,1)S(1)} %get-tuple-element.260), kind=kOutput, calls=%fused_computation | convolution fusion | flops 19344654336 | bytes 28311552 | tf_op jit(solution)/shard_map/dot_general | solution.py:525
  646.4 38.9 %shard_map.457 = (bf16[2048,3072]{1,0:T(8,128)(2,1)}, bf16[2048,3072]{1,0:T(8,128)(2,1)}) custom-call(bf16[2048,1536]{1,0:T(8,128)(2,1)} %pad_maximum_fusion.3.d_ref, bf16[3072,1536]{1,0:T(8,128)(2,1)} %all-gather.8.cloned.1.call-done.w_ref, bf16[2048,3072]{1,0:T(8,128)(2,1)} %get-tuple-element.62.gate_ref, bf16[2048,3072]{1,0:T(8,128)(2,1)} %get-tuple-element.63.up_ref, ...), custom_call_target="tpu_custom_call" | custom-call | flops 19327352832 | bytes 72351744 | tf_op jit(solution)/shard_map/pallas_call | solution.py:529
  685.3 25.1 %convolution_convert_fusion.2 = bf16[1536,3072]{1,0:T(8,128)(2,1)} fusion(bf16[2048,3072]{1,0:T(8,128)(2,1)} %get-tuple-element.64, bf16[1024,1536]{1,0:T(8,128)(2,1)} %copy-done.31, bf16[1024,1536]{1,0:T(8,128)(2,1)S(1)} %copy-done.14), kind=kOutput, calls=%fused_computation.2 | convolution fusion | flops 19344654336 | bytes 28311552 | tf_op jit(solution)/shard_map/dot_general | solution.py:525
  710.5 14.6 %fusion = f32[1024,1536]{1,0:T(8,128)S(1)} fusion(bf16[1536,6144]{1,0:T(8,128)(2,1)} %all-gather.6.cloned.1.call-done.wg_ref.wu_ref, bf16[2048,3072]{1,0:T(8,128)(2,1)} %get-tuple-element.65), kind=kOutput, calls=%fused_computation.14 | convolution fusion | flops 9663676416 | bytes 22020096 | tf_op jit(solution)/shard_map/dot_general | solution.py:517
  725.1 15.8 %add_convert_fusion.2 = bf16[1024,1536]{1,0:T(8,128)(2,1)} fusion(f32[1024,1536]{1,0:T(8,128)S(1)} %fusion, bf16[1536,6144]{1,0:T(8,128)(2,1)} %all-gather.6.cloned.1.call-done.wg_ref.wu_ref, bf16[2048,3072]{1,0:T(8,128)(2,1)} %get-tuple-element.64), kind=kOutput, calls=%fused_computation.44 | convolution fusion | flops 9666822144 | bytes 25165824 | tf_op jit(solution)/shard_map/dot_general | solution.py:517
  741.1 16.1 %fusion.2 = f32[1024,1536]{1,0:T(8,128)} fusion(bf16[1536,6144]{1,0:T(8,128)(2,1)} %all-gather.6.cloned.1.call-done.wg_ref.wu_ref, bf16[2048,3072]{1,0:T(8,128)(2,1)} %get-tuple-element.65), kind=kOutput, calls=%fused_computation.16 | convolution fusion | flops 9663676416 | bytes 22020096 | tf_op jit(solution)/shard_map/dot_general | solution.py:517
  757.2 21.8 %multiply_reduce_fusion.1 = (f32[1536]{0:T(1024)S(1)}, f32[1024]{0:T(1024)S(1)}, f32[1024]{0:T(1024)S(1)}, f32[1024,1536]{1,0:T(8,128)}) fusion(f32[1024,1536]{1,0:T(8,128)} %copy-done.1, f32[1024]{0:T(1024)S(1)} %copy-done.117, f32[1024]{0:T(1024)S(1)} %copy-done.102, f32[1536]{0:T(1024)S(1)} %copy-done.98, ...), kind=kOutput, calls=%fused_computation.30 | convolution fusion | flops 9680973824 | bytes 37777408 | tf_op jit(solution)/shard_map/dot_general | solution.py:517
  779.0 10.8 fusion.183
  795.7 10.2 fusion.40.g_ref
  805.9 18.3 %shard_map.458 = (bf16[2048,768]{1,0:T(8,128)(2,1)}, f32[128,768]{1,0:T(8,128)}, f32[128,768]{1,0:T(8,128)}) custom-call(bf16[2048,768]{1,0:T(8,128)(2,1)} %fusion.44.q_ref, bf16[2048,768]{1,0:T(8,128)(2,1)} %fusion.40.g_ref, bf16[128,1536]{1,0:T(8,128)(2,1)} %convolution_convert_fusion.7.k_ref.v_ref, ...), custom_call_target="tpu_custom_call" | custom-call | flops 6442450944 | bytes 25165824 | tf_op jit(solution)/shard_map/pallas_call | solution.py:529
  824.3 6.6 convolution_convert_fusion.3
  840.5 6.8 fusion.83
  849.3 7.4 fusion.41
  859.0 7.2 multiply_reduce_fusion.2
  871.4 25.6 %convolution_convert_fusion.1 = bf16[1536,3072]{1,0:T(8,128)(2,1)} fusion(bf16[2048,3072]{1,0:T(8,128)(2,1)} %get-tuple-element.65, bf16[1024,1536]{1,0:T(8,128)(2,1)} %copy-done.31, bf16[1024,1536]{1,0:T(8,128)(2,1)S(1)} %copy-done.15), kind=kOutput, calls=%fused_computation.1 | convolution fusion | flops 19344654336 | bytes 28311552 | tf_op jit(solution)/shard_map/dot_general | solution.py:525
  902.3 6.3 fusion.93.refs_15_
  912.2 7.4 fusion.43
  920.9 9.4 fusion.42.refs_1_
  934.2 76.4 %shard_map.459 = (bf16[2048,384]{1,0:T(8,128)(2,1)}, bf16[2048,384]{1,0:T(8,128)(2,1)}, bf16[2048,384]{1,0:T(8,128)(2,1)}, f32[16,384]{1,0:T(8,128)}, f32[16,384]{1,0:T(8,128)}) custom-call(bf16[2048,2304]{1,0:T(8,128)(2,1)} %shard_map.453.q_ref.k_ref.v_ref.refs_0_.refs_7_.refs_8_, bf16[2048,768]{1,0:T(8,128)(2,1)} %fusion.42.refs_1_, ...), custom_call_target="tpu_custom_call" | custom-call | flops 51539607552 | bytes 31457280 | tf_op jit(solution)/shard_map/pallas_call | solution.py:529
  1012.4 5.5 add_convert_fusion.6
  1025.2 8.3 fusion.59
  1033.5 8.4 fusion.61
  1043.2 10.1 fusion.8.refs_17_
  1059.1 76.3 %shard_map.460 = (bf16[2048,384]{1,0:T(8,128)(2,1)}, bf16[2048,384]{1,0:T(8,128)(2,1)}, bf16[2048,384]{1,0:T(8,128)(2,1)}, f32[16,384]{1,0:T(8,128)}, f32[16,384]{1,0:T(8,128)}) custom-call(bf16[2048,2304]{1,0:T(8,128)(2,1)} %shard_map.453.q_ref.k_ref.v_ref.refs_0_.refs_7_.refs_8_, bf16[2048,768]{1,0:T(8,128)(2,1)} %fusion.42.refs_1_, ...), custom_call_target="tpu_custom_call" | custom-call | flops 51539607552 | bytes 31457280 | tf_op jit(solution)/shard_map/pallas_call | solution.py:529
  1137.7 5.0 fusion.19
  1146.0 10.9 add_convert_fusion.1
  1157.0 10.0 fusion.9
  1182.0 13.6 multiply_reduce_fusion.3
  1215.8 124.0 %shard_map.461 = (f32[96,1152]{1,0:T(8,128)}, f32[96,1152]{1,0:T(8,128)}, f32[96,128]{1,0:T(8,128)}, f32[48,1536]{1,0:T(8,128)}, f32[96,768]{1,0:T(8,128)}, /*index=5*/f32[96,1536]{1,0:T(8,128)}) custom-call(bf16[2,2,4,96,1152]{4,3,2,1,0:T(8,128)(2,1)} %bitcast.213, bf16[2,2,4,96,1152]{4,3,2,1,0:T(8,128)(2,1)} %bitcast.214, ...), custom_call_target="tpu_custom_call" | custom-call | flops 99999997952 | bytes 10000000 | tf_op jit(solution)/shard_map/pallas_call | solution.py:1071
  (752 shorter events, 297.6 us)
Async XLA Ops:
  7.2 213.7 %all-gather.4.cloned.1.call-start = ((), (), s32[]{:S(2)}) async-start(), calls=%async_computation.3 | async-start | bytes 18382848 | tf_op jit(solution)/shard_map/all_gather | solution.py:1164
  9.5 9.2 collective-permute-start.9
  14.4 5.0 collective-permute-start.7
  20.5 420.3 %all-gather.6.cloned.1.call-start = ((), (), s32[]{:S(2)}) async-start(), calls=%async_computation.4 | async-start | bytes 20054016 | tf_op jit(solution)/shard_map/all_gather | solution.py:1169
  38.1 519.8 %all-gather.8.cloned.1.call-start = ((), (), s32[]{:S(2)}) async-start(), calls=%async_computation.5 | async-start | bytes 10027008 | tf_op jit(solution)/shard_map/all_gather | solution.py:1170
  38.6 5.6 collective-permute-start
  39.0 34.9 %collective-permute-start.3 = (bf16[2,512,64]{1,2,0:T(8,128)(2,1)S(1)}, bf16[2,512,64]{1,2,0:T(8,128)(2,1)S(1)}, u32[]{:S(2)}, u32[]{:S(2)}) collective-permute-start(bf16[2,512,64]{1,2,0:T(8,128)(2,1)S(1)} %get-tuple-element.303), channel_id=1, source_target_pairs={{0,8},{8,0},{16,24},{24,16},{1,9},{9,1},{17,25},{25,17},{2,10},{10... | collective-permute-start | bytes 393224 | tf_op jit(solution)/shard_map/ppermute | solution.py:1109
  41.8 32.2 %collective-permute-start.4 = (bf16[2,512,64]{1,2,0:T(8,128)(2,1)S(1)}, bf16[2,512,64]{1,2,0:T(8,128)(2,1)S(1)}, u32[]{:S(2)}, u32[]{:S(2)}) collective-permute-start(bf16[2,512,64]{1,2,0:T(8,128)(2,1)S(1)} %get-tuple-element.304), channel_id=1, source_target_pairs={{0,16},{8,24},{16,0},{24,8},{1,17},{9,25},{17,1},{25,9},{2,18},{10... | collective-permute-start | bytes 393224 | tf_op jit(solution)/shard_map/ppermute | solution.py:1109
  43.3 30.7 %collective-permute-start.5 = (bf16[2,512,64]{1,2,0:T(8,128)(2,1)S(1)}, bf16[2,512,64]{1,2,0:T(8,128)(2,1)S(1)}, u32[]{:S(2)}, u32[]{:S(2)}) collective-permute-start(bf16[2,512,64]{1,2,0:T(8,128)(2,1)S(1)} %get-tuple-element.305), channel_id=1, source_target_pairs={{0,24},{8,16},{16,8},{24,0},{1,25},{9,17},{17,9},{25,1},{2,26},{10... | collective-permute-start | bytes 393224 | tf_op jit(solution)/shard_map/ppermute | solution.py:1109
  44.3 5.8 collective-permute-start.1
  57.0 5.1 collective-permute-start.10
  74.8 5.1 collective-permute-start.6
  231.9 124.6 %collective-permute-start.15 = (bf16[768,768]{1,0:T(8,128)(2,1)S(1)}, bf16[768,768]{1,0:T(8,128)(2,1)}, u32[]{:S(2)}, u32[]{:S(2)}) collective-permute-start(bf16[768,768]{1,0:T(8,128)(2,1)S(1)} %get-tuple-element.282), channel_id=1, source_target_pairs={{0,1},{1,0},{2,3},{3,2},{4,5},{5,4},{6,7},{7,6},{8,9},{9,8},{10,11... | collective-permute-start | bytes 3538952 | tf_op jit(solution)/shard_map/ppermute | solution.py:1106
  361.4 5.7 collective-permute-start.16
  377.0 10.8 collective-permute-start.17
  378.7 801.6 %reduce-scatter.4.cloned.1.call-start = ((), (), s32[]{:S(2)}) async-start(), calls=%async_computation.6 | async-start | bytes 10027008 | tf_op jit(solution)/shard_map/reduce_scatter | solution.py:1332
  386.3 25.0 %collective-permute-start.19 = (bf16[768,768]{1,0:T(8,128)(2,1)}, bf16[768,768]{1,0:T(8,128)(2,1)}, u32[]{:S(2)}, u32[]{:S(2)}) collective-permute-start(bf16[768,768]{1,0:T(8,128)(2,1)} %get-tuple-element.278), channel_id=1, source_target_pairs={{0,1},{1,0},{2,3},{3,2},{4,5},{5,4},{6,7},{7,6},{8,9},{9,8},{10,11... | collective-permute-start | bytes 3538952 | tf_op jit(solution)/shard_map/ppermute | solution.py:1106
  416.2 5.7 collective-permute-start.20
  430.1 5.7 collective-permute-start.21
  573.8 6.0 collective-permute-start.23
  610.0 5.7 collective-permute-start.24
  710.4 492.4 %reduce-scatter.8.cloned.1.call-start = ((), (), s32[]{:S(2)}) async-start(), calls=%async_computation.8 | async-start | bytes 10027008 | tf_op jit(solution)/shard_map/reduce_scatter | solution.py:1332
  740.9 16.3 %collective-permute-start.25 = (bf16[1024,1536]{1,0:T(8,128)(2,1)}, bf16[1024,1536]{1,0:T(8,128)(2,1)S(1)}, u32[]{:S(2)}, u32[]{:S(2)}) collective-permute-start(bf16[1024,1536]{1,0:T(8,128)(2,1)} %add_convert_fusion.2), channel_id=1, source_target_pairs={{0,1},{1,0},{2,3},{3,2},{4,5},{5,4},{6,7},{7,6},{8,9},{9,8},{10,11... | collective-permute-start | bytes 9437192 | tf_op jit(solution)/shard_map/ppermute | solution.py:1106
  741.0 605.3 %reduce-scatter.6.cloned.1.call-start = ((), (), s32[]{:S(2)}) async-start(), calls=%async_computation.7 | async-start | bytes 10027008 | tf_op jit(solution)/shard_map/reduce_scatter | solution.py:1332
  789.9 5.9 collective-permute-start.26
  830.9 27.3 %collective-permute-start.27 = (bf16[1024,1536]{1,0:T(8,128)(2,1)}, bf16[1024,1536]{1,0:T(8,128)(2,1)}, u32[]{:S(2)}, u32[]{:S(2)}) collective-permute-start(bf16[1024,1536]{1,0:T(8,128)(2,1)} %convolution_convert_fusion.3), channel_id=1, source_target_pairs={{0,1},{1,0},{2,3},{3,2},{4,5},{5,4},{6,7},{7,6},{8,9},{9,8},{10,11... | collective-permute-start | bytes 9437192 | tf_op jit(solution)/shard_map/ppermute | solution.py:1106
  857.9 51.2 %collective-permute-start.30 = (bf16[768,768]{1,0:T(8,128)(2,1)}, bf16[768,768]{1,0:T(8,128)(2,1)}, u32[]{:S(2)}, u32[]{:S(2)}) collective-permute-start(bf16[768,768]{1,0:T(8,128)(2,1)} %get-tuple-element.274), channel_id=1, source_target_pairs={{0,1},{1,0},{2,3},{3,2},{4,5},{5,4},{6,7},{7,6},{8,9},{9,8},{10,11... | collective-permute-start | bytes 3538952 | tf_op jit(solution)/shard_map/ppermute | solution.py:1106
  871.1 41.0 %collective-permute-start.28 = (bf16[1024,1536]{1,0:T(8,128)(2,1)}, bf16[1024,1536]{1,0:T(8,128)(2,1)}, u32[]{:S(2)}, u32[]{:S(2)}) collective-permute-start(bf16[1024,1536]{1,0:T(8,128)(2,1)} %get-tuple-element.256), channel_id=1, source_target_pairs={{0,1},{1,0},{2,3},{3,2},{4,5},{5,4},{6,7},{7,6},{8,9},{9,8},{10,11... | collective-permute-start | bytes 9437192 | tf_op jit(solution)/shard_map/ppermute | solution.py:1106
  900.9 119.1 %collective-permute-start.31 = (bf16[384,1536]{1,0:T(8,128)(2,1)}, bf16[384,1536]{1,0:T(8,128)(2,1)}, u32[]{:S(2)}, u32[]{:S(2)}) collective-permute-start(bf16[384,1536]{1,0:T(8,128)(2,1)} %convolution_convert_fusion.6.refs_14_), channel_id=1, source_target_pairs={{0,8},{8,0},{16,24},{24,16},{1,9},{9,1},{17,25},{25,17},{2,10},{10... | collective-permute-start | bytes 3538952 | tf_op jit(solution)/shard_map/ppermute | solution.py:1109
  908.6 103.8 %collective-permute-start.32 = (bf16[768,768]{1,0:T(8,128)(2,1)}, bf16[768,768]{1,0:T(8,128)(2,1)}, u32[]{:S(2)}, u32[]{:S(2)}) collective-permute-start(bf16[768,768]{1,0:T(8,128)(2,1)} %fusion.93.refs_15_), channel_id=1, source_target_pairs={{0,8},{8,0},{16,24},{24,16},{1,9},{9,1},{17,25},{25,17},{2,10},{10... | collective-permute-start | bytes 3538952 | tf_op jit(solution)/shard_map/ppermute | solution.py:1109
  919.8 10.5 collective-permute-start.29
  933.1 120.2 %collective-permute-start.33 = (bf16[768,1536]{1,0:T(8,128)(2,1)}, bf16[768,1536]{1,0:T(8,128)(2,1)}, u32[]{:S(2)}, u32[]{:S(2)}) collective-permute-start(bf16[768,1536]{1,0:T(8,128)(2,1)} %fusion.67.refs_16_), channel_id=1, source_target_pairs={{0,16},{8,24},{16,0},{24,8},{1,17},{9,25},{17,1},{25,9},{2,18},{10... | collective-permute-start | bytes 7077896 | tf_op jit(solution)/shard_map/ppermute | solution.py:1109
  1018.9 152.2 %collective-permute-start.38 = (bf16[384,768]{1,0:T(8,128)(2,1)}, bf16[384,768]{1,0:T(8,128)(2,1)}, u32[]{:S(2)}, u32[]{:S(2)}) collective-permute-start(bf16[384,768]{1,0:T(8,128)(2,1)} %constant_dynamic-slice_fusion.7.refs_15_), channel_id=1, source_target_pairs={{0,16},{8,24},{16,0},{24,8},{1,17},{9,25},{17,1},{25,9},{2,18},{10... | collective-permute-start | bytes 1769480 | tf_op jit(solution)/shard_map/ppermute | solution.py:1109
  1022.8 146.1 %collective-permute-start.37 = (bf16[192,1536]{1,0:T(8,128)(2,1)}, bf16[192,1536]{1,0:T(8,128)(2,1)}, u32[]{:S(2)}, u32[]{:S(2)}) collective-permute-start(bf16[192,1536]{1,0:T(8,128)(2,1)} %constant_dynamic-slice_fusion.8.refs_14_), channel_id=1, source_target_pairs={{0,16},{8,24},{16,0},{24,8},{1,17},{9,25},{17,1},{25,9},{2,18},{10... | collective-permute-start | bytes 1769480 | tf_op jit(solution)/shard_map/ppermute | solution.py:1109
  1058.2 119.1 %collective-permute-start.39 = (bf16[384,1536]{1,0:T(8,128)(2,1)}, bf16[384,1536]{1,0:T(8,128)(2,1)}, u32[]{:S(2)}, u32[]{:S(2)}) collective-permute-start(bf16[384,1536]{1,0:T(8,128)(2,1)} %constant_dynamic-slice_fusion.6.refs_16_), channel_id=1, source_target_pairs={{0,8},{8,0},{16,24},{24,16},{1,9},{9,1},{17,25},{25,17},{2,10},{10... | collective-permute-start | bytes 3538952 | tf_op jit(solution)/shard_map/ppermute | solution.py:1109
  1143.2 29.9 %collective-permute-start.35 = (f32[1,1536]{1,0:T(1,128)S(1)}, f32[1,1536]{1,0:T(1,128)}, u32[]{:S(2)}, u32[]{:S(2)}) collective-permute-start(f32[1,1536]{1,0:T(1,128)S(1)} %copy.294), channel_id=1, source_target_pairs={{0,1},{1,0},{2,3},{3,2},{4,5},{5,4},{6,7},{7,6},{8,9},{9,8},{10,11... | collective-permute-start | bytes 18440 | tf_op jit(solution)/shard_map/ppermute | solution.py:1106
  1156.9 25.0 %collective-permute-start.34 = (bf16[1024,1536]{1,0:T(8,128)(2,1)}, bf16[1024,1536]{1,0:T(8,128)(2,1)}, u32[]{:S(2)}, u32[]{:S(2)}) collective-permute-start(bf16[1024,1536]{1,0:T(8,128)(2,1)} %add_convert_fusion.1), channel_id=1, source_target_pairs={{0,1},{1,0},{2,3},{3,2},{4,5},{5,4},{6,7},{7,6},{8,9},{9,8},{10,11... | collective-permute-start | bytes 9437192 | tf_op jit(solution)/shard_map/ppermute | solution.py:1106
  1201.5 12.1 collective-permute-start.36
  1202.8 6.2 collective-permute-start.55
  1342.2 20.5 %collective-permute-start.42 = (f32[1,1536]{1,0:T(1,128)S(1)}, f32[1,1536]{1,0:T(1,128)S(1)}, u32[]{:S(2)}, u32[]{:S(2)}) collective-permute-start(f32[1,1536]{1,0:T(1,128)S(1)} %copy.301), channel_id=1, source_target_pairs={{0,24},{8,16},{16,8},{24,0},{1,25},{9,17},{17,9},{25,1},{2,26},{10... | collective-permute-start | bytes 18440 | tf_op jit(solution)/shard_map/ppermute | solution.py:1109
  1344.5 18.2 %collective-permute-start.41 = (f32[1,1536]{1,0:T(1,128)S(1)}, f32[1,1536]{1,0:T(1,128)S(1)}, u32[]{:S(2)}, u32[]{:S(2)}) collective-permute-start(f32[1,1536]{1,0:T(1,128)S(1)} %copy.301), channel_id=1, source_target_pairs={{0,16},{8,24},{16,0},{24,8},{1,17},{9,25},{17,1},{25,9},{2,18},{10... | collective-permute-start | bytes 18440 | tf_op jit(solution)/shard_map/ppermute | solution.py:1109
  1345.1 17.6 %collective-permute-start.40 = (f32[1,1536]{1,0:T(1,128)S(1)}, f32[1,1536]{1,0:T(1,128)S(1)}, u32[]{:S(2)}, u32[]{:S(2)}) collective-permute-start(f32[1,1536]{1,0:T(1,128)S(1)} %copy.301), channel_id=1, source_target_pairs={{0,8},{8,0},{16,24},{24,16},{1,9},{9,1},{17,25},{25,17},{2,10},{10... | collective-permute-start | bytes 18440 | tf_op jit(solution)/shard_map/ppermute | solution.py:1109
  1354.3 11.0 collective-permute-start.51
  1354.5 42.0 %collective-permute-start.54 = (bf16[24,1536]{1,0:T(8,128)(2,1)S(1)}, bf16[24,1536]{1,0:T(8,128)(2,1)S(1)}, u32[]{:S(2)}, u32[]{:S(2)}) collective-permute-start(bf16[24,1536]{1,0:T(8,128)(2,1)S(1)} %dynamic-slice_convert_fusion.4), channel_id=1, source_target_pairs={{0,1},{1,0},{2,3},{3,2},{4,5},{5,4},{6,7},{7,6},{8,9},{9,8},{10,11... | collective-permute-start | bytes 221192 | tf_op jit(solution)/shard_map/ppermute | solution.py:1106
  1362.6 40.9 %collective-permute-start.56 = (bf16[48,3072]{1,0:T(8,128)(2,1)}, bf16[48,3072]{1,0:T(8,128)(2,1)}, u32[]{:S(2)}, u32[]{:S(2)}) collective-permute-start(bf16[48,3072]{1,0:T(8,128)(2,1)} %dynamic-slice_convert_fusion), channel_id=1, source_target_pairs={{0,1},{1,0},{2,3},{3,2},{4,5},{5,4},{6,7},{7,6},{8,9},{9,8},{10,11... | collective-permute-start | bytes 884744 | tf_op jit(solution)/shard_map/ppermute | solution.py:1106
  1362.8 5.8 collective-permute-start.45
  1368.5 29.4 %collective-permute-start.53 = (bf16[48,2304]{1,0:T(8,128)(2,1)}, bf16[48,2304]{1,0:T(8,128)(2,1)S(1)}, u32[]{:S(2)}, u32[]{:S(2)}) collective-permute-start(bf16[48,2304]{1,0:T(8,128)(2,1)} %dynamic-slice_convert_fusion.2), channel_id=1, source_target_pairs={{0,1},{1,0},{2,3},{3,2},{4,5},{5,4},{6,7},{7,6},{8,9},{9,8},{10,11... | collective-permute-start | bytes 663560 | tf_op jit(solution)/shard_map/ppermute | solution.py:1106
  1369.3 29.1 %collective-permute-start.52 = (bf16[48,2304]{1,0:T(8,128)(2,1)}, bf16[48,2304]{1,0:T(8,128)(2,1)}, u32[]{:S(2)}, u32[]{:S(2)}) collective-permute-start(bf16[48,2304]{1,0:T(8,128)(2,1)} %dynamic-slice_convert_fusion.3), channel_id=1, source_target_pairs={{0,1},{1,0},{2,3},{3,2},{4,5},{5,4},{6,7},{7,6},{8,9},{9,8},{10,11... | collective-permute-start | bytes 663560 | tf_op jit(solution)/shard_map/ppermute | solution.py:1106
  (187 other events, 2163.0 us)
Sparse Core Ops, SparseCore 0:
  20.6 200.1 all-gather.3
  224.2 209.6 all-gather.5
  437.2 120.6 all-gather.7
  710.5 169.6 reduce-scatter.3
  886.7 205.4 reduce-scatter.7
  1097.8 218.4 reduce-scatter.5

commit v5 on v4

--- a/solution.py
+++ b/solution.py
@@ -1331,9 +1331,9 @@
     def gathered_sum(g):
         return lax.psum_scatter(g, peers, scatter_dimension=0, tiled=True)
 
-    g_down = dot_tn(hidden, d_f).astype(bf16)
-    s_down = gathered_sum(g_down)
-    d_gate, d_up = down_back(d_f, down_w, gate, upper, g_down)
+    down_parts = [dot_tn(hidden, part).astype(bf16) for part in jnp.split(d_f, 2, 1)]
+    s_down = jnp.concatenate([gathered_sum(part) for part in down_parts], 1)
+    d_gate, d_up = down_back(d_f, down_w, gate, upper, down_parts[0])
     s_gate = gathered_sum(dot_tn(n3, d_gate).astype(bf16))
     s_upper = gathered_sum(dot_tn(n3, d_up).astype(bf16))
     d_n3 = shared_sum(

time: 1450 us -> 1470 us (1.014)
    dot_general x13 -> x14, matrix products: 131 us -> 138 us  [dot_tn(): lax.dot_general(a, b, (((0,), (0,)), ((), ())), preferred_element_type=f32)]
  transfers between devices with their start and end apart: 63 -> 64, of which waited for: 25 -> 25; matrix products, arithmetic and copies ran while one was open for 30% -> 33% of each run, Pallas kernels for 34% -> 37%
where the time goes in v5:
time: 1470 us; the launch traced here: 1460 us
  Pallas kernels  533 us (36%)
  matrix products  370 us (25%)
  waiting for transfers between devices  258 us (18%)
  other arithmetic  122 us (8%)
  local copies, waits for them, and re-layouts  97.7 us (7%)
  starting transfers between devices  43.5 us (3%)
  between operations  34.8 us (2%)
    pallas_call x9, Pallas kernels, call(): pl.pallas_call(kernel, grid=grid, in_specs=in_specs, out_specs=out_specs,...  398 us
    dot_general x14, matrix products, dot_nt(): lax.dot_general(a, b, (((1,), (1,)), ((), ())), preferred_element_type=f32)  153 us
    dot_general x14, matrix products, dot_tn(): lax.dot_general(a, b, (((0,), (0,)), ((), ())), preferred_element_type=f32)  138 us
    all_gather x1, waiting for transfers between devices, chip_body(): lax.all_gather(jnp.concatenate([first_mine, square_mine, cross_mine], 1),...  138 us
    pallas_call x1, Pallas kernels, chip_sums(): pl.pallas_call(functools.partial(chip_sum_kernel, inputs=len(arrays), job...  135 us
    dot_general x13, matrix products, dot_nn(): lax.dot_general(a, b, (((1,), (0,)), ((), ())), preferred_element_type=f32)  73.7 us
    all_gather x1, waiting for transfers between devices, chip_body(): down_w = lax.all_gather(down_weight.astype(bf16), peers, axis=0, tiled=True)  62.6 us
    ppermute x25, starting transfers between devices, across(): return lax.ppermute(x, axis, [(i, i ^ bit) for i in range(size)])  35.3 us
  transfers between devices with their start and end apart: 64, of which 25 were waited for; matrix products, arithmetic and copies ran while one was open for 33% of the time, Pallas kernels for 37%

profile of v5, /device:TPU:0, one launch (start us, length us, event | category | flops | bytes accessed | tf_op | source)
XLA Modules:
  0.0 1459.0 jit_solution(1711147012821780299)
XLA Ops:
  22.8 10.0 dynamic-slice_reduce_fusion.1
  82.5 138.3 %all-gather.4.cloned.1.call-done.w_ref = bf16[1536,5632]{1,0:T(8,128)(2,1)} async-done(((bf16[96,5632]{1,0:T(8,128)(2,1)}), bf16[1536,5632]{1,0:T(8,128)(2,1)}) %all-gather.4.cloned.1.call-update) | async-done | bytes 17301520 | tf_op jit(solution)/shard_map/all_gather | solution.py:1164
  226.0 5.8 fusion.192
  232.0 10.6 shard_map.452
  247.3 35.4 %shard_map.453.q_ref.k_ref.v_ref.refs_0_.refs_7_.refs_8_ = bf16[2048,2304]{1,0:T(8,128)(2,1)} custom-call(bf16[2048,1536]{1,0:T(8,128)(2,1)} %get-tuple-element.58.n_ref, bf16[1536,5632]{1,0:T(8,128)(2,1)} %all-gather.4.cloned.1.call-done.w_ref, f32[2048,128]{1,0:T(8,128)} %broadcast_select_fusion.1.cos_ref.refs_4_.refs_11_, ...), custom_call_target="tpu_custom_call" | custom-call | flops 14495514624 | bytes 25165824 | tf_op jit(solution)/shard_map/pallas_call | solution.py:529
  282.8 73.2 %shard_map.454 = (bf16[2048,768]{1,0:T(8,128)(2,1)}, f32[6,2,2048]{2,1,0:T(2,128)}) custom-call(bf16[2048,2304]{1,0:T(8,128)(2,1)} %shard_map.453.q_ref.k_ref.v_ref.refs_0_.refs_7_.refs_8_, bf16[2048,2304]{1,0:T(8,128)(2,1)} %shard_map.453.q_ref.k_ref.v_ref.refs_0_.refs_7_.refs_8_, bf16[2048,2304]{1,0:T(8,128)(2,1)} %shard_map.453.q_ref.k_ref.v_ref.refs_0_.refs_7_.refs_8_, ...), custom_call_target="tpu_custom_call" | custom-call | flops 51539607552 | bytes 31457280 | tf_op jit(solution)/shard_map/pallas_call | solution.py:529
  361.1 5.5 collective-permute-done.16
  366.6 6.4 fusion.200
  387.4 9.4 fusion.44.q_ref
  396.9 14.0 shard_map.455
  416.2 5.3 collective-permute-done.20
  430.2 5.3 collective-permute-done.21
  440.3 55.0 %shard_map.456 = (bf16[2048,3072]{1,0:T(8,128)(2,1)}, bf16[2048,3072]{1,0:T(8,128)(2,1)}, bf16[2048,3072]{1,0:T(8,128)(2,1)}) custom-call(bf16[2048,1536]{1,0:T(8,128)(2,1)} %pad_maximum_fusion.3.n_ref, bf16[1536,6144]{1,0:T(8,128)(2,1)} %all-gather.6.cloned.1.call-done.wg_ref.wu_ref, bf16[1536,6144]{1,0:T(8,128)(2,1)} %all-gather.6.cloned.1.call-done.wg_ref.wu_ref), custom_call_target="tpu_custom_call" | custom-call | flops 38654705664 | bytes 69206016 | tf_op jit(solution)/shard_map/pallas_call | solution.py:529
  495.3 62.6 %all-gather.8.cloned.1.call-done.w_ref = bf16[3072,1536]{1,0:T(8,128)(2,1)} async-done(((bf16[192,1536]{1,0:T(8,128)(2,1)}), bf16[3072,1536]{1,0:T(8,128)(2,1)}) %all-gather.8.cloned.1.call-update) | async-done | bytes 9437200 | tf_op jit(solution)/shard_map/all_gather | solution.py:1170
  557.9 15.9 %fusion.37 = bf16[1024,1536]{1,0:T(8,128)(2,1)} fusion(bf16[3072,1536]{1,0:T(8,128)(2,1)} %all-gather.8.cloned.1.call-done.w_ref, bf16[2048,3072]{1,0:T(8,128)(2,1)} %get-tuple-element.61), kind=kOutput, calls=%fused_computation.90 | convolution fusion | flops 9665249280 | bytes 18874368 | tf_op jit(solution)/shard_map/dot_general | solution.py:521
  579.8 17.2 %fusion.202 = (f32[1024]{0:T(1024)S(1)}, f32[1024,1536]{1,0:T(8,128)S(1)}) fusion(f32[1024,1536]{1,0:T(8,128)} %copy-done.1, bf16[1024,1536]{1,0:T(8,128)(2,1)} %collective-permute-done.23, bf16[3072,1536]{1,0:T(8,128)(2,1)} %all-gather.8.cloned.1.call-done.w_ref, bf16[2048,3072]{1,0:T(8,128)(2,1)} %get-tuple-element.61), kind=kOutput, calls=%fused_computation.481 | convolution fusion | flops 9669966848 | bytes 31461376 | tf_op jit(solution)/shard_map/dot_general | solution.py:521
  610.1 5.5 collective-permute-done.24
  617.3 14.5 convolution_convert_fusion.2
  631.8 15.1 %convolution_convert_fusion.3.after_ref = bf16[3072,768]{1,0:T(8,128)(2,1)} fusion(bf16[2048,3072]{1,0:T(8,128)(2,1)} %get-tuple-element.61, bf16[1024,1536]{1,0:T(8,128)(2,1)S(1)} %get-tuple-element.260, bf16[1024,1536]{1,0:T(8,128)(2,1)} %copy-done.33), kind=kOutput, calls=%fused_computation.84 | convolution fusion | flops 9672327168 | bytes 23592960 | tf_op jit(solution)/shard_map/dot_general | solution.py:525
  647.0 5.0 pad_maximum_fusion.1.d_ref
  652.0 38.9 %shard_map.457 = (bf16[2048,3072]{1,0:T(8,128)(2,1)}, bf16[2048,3072]{1,0:T(8,128)(2,1)}) custom-call(bf16[2048,1536]{1,0:T(8,128)(2,1)} %pad_maximum_fusion.1.d_ref, bf16[3072,1536]{1,0:T(8,128)(2,1)} %all-gather.8.cloned.1.call-done.w_ref, bf16[2048,3072]{1,0:T(8,128)(2,1)} %get-tuple-element.62.gate_ref, bf16[2048,3072]{1,0:T(8,128)(2,1)} %get-tuple-element.63.up_ref, ...), custom_call_target="tpu_custom_call" | custom-call | flops 19327352832 | bytes 72351744 | tf_op jit(solution)/shard_map/pallas_call | solution.py:529
  690.9 14.5 fusion
  705.4 15.8 %add_convert_fusion.2 = bf16[1024,1536]{1,0:T(8,128)(2,1)} fusion(f32[1024,1536]{1,0:T(8,128)S(1)} %fusion, bf16[1536,6144]{1,0:T(8,128)(2,1)} %all-gather.6.cloned.1.call-done.wg_ref.wu_ref, bf16[2048,3072]{1,0:T(8,128)(2,1)} %get-tuple-element.64), kind=kOutput, calls=%fused_computation.47 | convolution fusion | flops 9666822144 | bytes 25165824 | tf_op jit(solution)/shard_map/dot_general | solution.py:517
  721.8 24.4 %convolution_convert_fusion.1 = bf16[1536,3072]{1,0:T(8,128)(2,1)} fusion(bf16[2048,3072]{1,0:T(8,128)(2,1)} %get-tuple-element.64, bf16[1024,1536]{1,0:T(8,128)(2,1)S(1)} %copy-done.31, bf16[1024,1536]{1,0:T(8,128)(2,1)S(1)} %copy-done.14), kind=kOutput, calls=%fused_computation.1 | convolution fusion | flops 19344654336 | bytes 28311552 | tf_op jit(solution)/shard_map/dot_general | solution.py:525
  746.3 15.7 %fusion.2 = f32[1024,1536]{1,0:T(8,128)} fusion(bf16[1536,6144]{1,0:T(8,128)(2,1)} %all-gather.6.cloned.1.call-done.wg_ref.wu_ref, bf16[2048,3072]{1,0:T(8,128)(2,1)} %get-tuple-element.65), kind=kOutput, calls=%fused_computation.15 | convolution fusion | flops 9663676416 | bytes 22020096 | tf_op jit(solution)/shard_map/dot_general | solution.py:517
  762.0 21.9 %multiply_reduce_fusion.1 = (f32[1536]{0:T(1024)S(1)}, f32[1024]{0:T(1024)S(1)}, f32[1024]{0:T(1024)S(1)}, f32[1024,1536]{1,0:T(8,128)}) fusion(f32[1024,1536]{1,0:T(8,128)} %copy-done.1, f32[1024]{0:T(1024)S(1)} %copy-done.122, f32[1024]{0:T(1024)S(1)} %copy-done.108, f32[1536]{0:T(1024)S(1)} %copy-done.104, ...), kind=kOutput, calls=%fused_computation.33 | convolution fusion | flops 9680973824 | bytes 37777408 | tf_op jit(solution)/shard_map/dot_general | solution.py:517
  783.9 11.6 fusion.189
  801.6 11.2 fusion.40.g_ref
  812.8 18.4 %shard_map.458 = (bf16[2048,768]{1,0:T(8,128)(2,1)}, f32[128,768]{1,0:T(8,128)}, f32[128,768]{1,0:T(8,128)}) custom-call(bf16[2048,768]{1,0:T(8,128)(2,1)} %fusion.44.q_ref, bf16[2048,768]{1,0:T(8,128)(2,1)} %fusion.40.g_ref, bf16[128,1536]{1,0:T(8,128)(2,1)} %convolution_convert_fusion.8.k_ref.v_ref, ...), custom_call_target="tpu_custom_call" | custom-call | flops 6442450944 | bytes 25165824 | tf_op jit(solution)/shard_map/pallas_call | solution.py:529
  831.2 6.6 convolution_convert_fusion.4
  847.3 7.0 fusion.87
  856.3 8.4 fusion.41
  867.5 7.3 multiply_reduce_fusion.2
  879.8 25.3 %convolution_convert_fusion = bf16[1536,3072]{1,0:T(8,128)(2,1)} fusion(bf16[2048,3072]{1,0:T(8,128)(2,1)} %get-tuple-element.65, bf16[1024,1536]{1,0:T(8,128)(2,1)S(1)} %copy-done.32, bf16[1024,1536]{1,0:T(8,128)(2,1)S(1)} %copy-done.14), kind=kOutput, calls=%fused_computation | convolution fusion | flops 19344654336 | bytes 28311552 | tf_op jit(solution)/shard_map/dot_general | solution.py:525
  911.1 5.7 fusion.97.refs_15_
  924.3 8.6 fusion.43
  934.2 10.4 fusion.42.refs_1_
  948.8 76.2 %shard_map.459 = (bf16[2048,384]{1,0:T(8,128)(2,1)}, bf16[2048,384]{1,0:T(8,128)(2,1)}, bf16[2048,384]{1,0:T(8,128)(2,1)}, f32[16,384]{1,0:T(8,128)}, f32[16,384]{1,0:T(8,128)}) custom-call(bf16[2048,2304]{1,0:T(8,128)(2,1)} %shard_map.453.q_ref.k_ref.v_ref.refs_0_.refs_7_.refs_8_, bf16[2048,768]{1,0:T(8,128)(2,1)} %fusion.42.refs_1_, ...), custom_call_target="tpu_custom_call" | custom-call | flops 51539607552 | bytes 31457280 | tf_op jit(solution)/shard_map/pallas_call | solution.py:529
  1026.9 5.8 add_convert_fusion.6
  1040.1 8.3 fusion.63
  1048.4 8.2 fusion.65
  1056.7 10.1 fusion.8.refs_17_
  1072.3 76.6 %shard_map.460 = (bf16[2048,384]{1,0:T(8,128)(2,1)}, bf16[2048,384]{1,0:T(8,128)(2,1)}, bf16[2048,384]{1,0:T(8,128)(2,1)}, f32[16,384]{1,0:T(8,128)}, f32[16,384]{1,0:T(8,128)}) custom-call(bf16[2048,2304]{1,0:T(8,128)(2,1)} %shard_map.453.q_ref.k_ref.v_ref.refs_0_.refs_7_.refs_8_, bf16[2048,768]{1,0:T(8,128)(2,1)} %fusion.42.refs_1_, ...), custom_call_target="tpu_custom_call" | custom-call | flops 51539607552 | bytes 31457280 | tf_op jit(solution)/shard_map/pallas_call | solution.py:529
  1150.4 5.1 fusion.19
  1158.8 10.8 add_convert_fusion.1
  1170.0 10.0 fusion.9
  1194.6 13.3 multiply_reduce_fusion.3
  1224.6 135.0 %shard_map.461 = (f32[96,1152]{1,0:T(8,128)}, f32[96,1152]{1,0:T(8,128)}, f32[96,128]{1,0:T(8,128)}, f32[48,1536]{1,0:T(8,128)}, f32[96,768]{1,0:T(8,128)}, /*index=5*/f32[96,1536]{1,0:T(8,128)}) custom-call(bf16[2,2,4,96,1152]{4,3,2,1,0:T(8,128)(2,1)} %bitcast.214, bf16[2,2,4,96,1152]{4,3,2,1,0:T(8,128)(2,1)} %bitcast.215, ...), custom_call_target="tpu_custom_call" | custom-call | flops 99999997952 | bytes 10000000 | tf_op jit(solution)/shard_map/pallas_call | solution.py:1071
  (760 shorter events, 303.0 us)
Async XLA Ops:
  7.2 213.7 %all-gather.4.cloned.1.call-start = ((), (), s32[]{:S(2)}) async-start(), calls=%async_computation.4 | async-start | bytes 18382848 | tf_op jit(solution)/shard_map/all_gather | solution.py:1164
  9.5 9.2 collective-permute-start.9
  14.4 5.0 collective-permute-start.7
  20.5 419.8 %all-gather.6.cloned.1.call-start = ((), (), s32[]{:S(2)}) async-start(), calls=%async_computation.5 | async-start | bytes 20054016 | tf_op jit(solution)/shard_map/all_gather | solution.py:1169
  38.1 519.8 %all-gather.8.cloned.1.call-start = ((), (), s32[]{:S(2)}) async-start(), calls=%async_computation.6 | async-start | bytes 10027008 | tf_op jit(solution)/shard_map/all_gather | solution.py:1170
  38.6 5.6 collective-permute-start
  39.0 34.9 %collective-permute-start.3 = (bf16[2,512,64]{1,2,0:T(8,128)(2,1)S(1)}, bf16[2,512,64]{1,2,0:T(8,128)(2,1)S(1)}, u32[]{:S(2)}, u32[]{:S(2)}) collective-permute-start(bf16[2,512,64]{1,2,0:T(8,128)(2,1)S(1)} %get-tuple-element.303), channel_id=1, source_target_pairs={{0,8},{8,0},{16,24},{24,16},{1,9},{9,1},{17,25},{25,17},{2,10},{10... | collective-permute-start | bytes 393224 | tf_op jit(solution)/shard_map/ppermute | solution.py:1109
  41.7 32.2 %collective-permute-start.4 = (bf16[2,512,64]{1,2,0:T(8,128)(2,1)S(1)}, bf16[2,512,64]{1,2,0:T(8,128)(2,1)S(1)}, u32[]{:S(2)}, u32[]{:S(2)}) collective-permute-start(bf16[2,512,64]{1,2,0:T(8,128)(2,1)S(1)} %get-tuple-element.304), channel_id=1, source_target_pairs={{0,16},{8,24},{16,0},{24,8},{1,17},{9,25},{17,1},{25,9},{2,18},{10... | collective-permute-start | bytes 393224 | tf_op jit(solution)/shard_map/ppermute | solution.py:1109
  43.3 30.7 %collective-permute-start.5 = (bf16[2,512,64]{1,2,0:T(8,128)(2,1)S(1)}, bf16[2,512,64]{1,2,0:T(8,128)(2,1)S(1)}, u32[]{:S(2)}, u32[]{:S(2)}) collective-permute-start(bf16[2,512,64]{1,2,0:T(8,128)(2,1)S(1)} %get-tuple-element.305), channel_id=1, source_target_pairs={{0,24},{8,16},{16,8},{24,0},{1,25},{9,17},{17,9},{25,1},{2,26},{10... | collective-permute-start | bytes 393224 | tf_op jit(solution)/shard_map/ppermute | solution.py:1109
  44.3 5.8 collective-permute-start.1
  57.0 5.1 collective-permute-start.10
  74.8 5.1 collective-permute-start.6
  232.0 124.0 %collective-permute-start.15 = (bf16[768,768]{1,0:T(8,128)(2,1)S(1)}, bf16[768,768]{1,0:T(8,128)(2,1)}, u32[]{:S(2)}, u32[]{:S(2)}) collective-permute-start(bf16[768,768]{1,0:T(8,128)(2,1)S(1)} %get-tuple-element.282), channel_id=1, source_target_pairs={{0,1},{1,0},{2,3},{3,2},{4,5},{5,4},{6,7},{7,6},{8,9},{9,8},{10,11... | collective-permute-start | bytes 3538952 | tf_op jit(solution)/shard_map/ppermute | solution.py:1106
  360.9 5.7 collective-permute-start.16
  376.6 10.9 collective-permute-start.17
  378.2 541.3 %reduce-scatter.11.cloned.1.call-start = ((), (), s32[]{:S(2)}) async-start(), calls=%async_computation.10 | async-start | bytes 5013504 | tf_op jit(solution)/shard_map/reduce_scatter | solution.py:1332
  385.9 25.0 %collective-permute-start.19 = (bf16[768,768]{1,0:T(8,128)(2,1)}, bf16[768,768]{1,0:T(8,128)(2,1)}, u32[]{:S(2)}, u32[]{:S(2)}) collective-permute-start(bf16[768,768]{1,0:T(8,128)(2,1)} %get-tuple-element.278), channel_id=1, source_target_pairs={{0,1},{1,0},{2,3},{3,2},{4,5},{5,4},{6,7},{7,6},{8,9},{9,8},{10,11... | collective-permute-start | bytes 3538952 | tf_op jit(solution)/shard_map/ppermute | solution.py:1106
  415.8 5.7 collective-permute-start.20
  429.7 5.7 collective-permute-start.21
  573.8 6.0 collective-permute-start.23
  609.9 5.7 collective-permute-start.24
  631.8 287.7 %reduce-scatter.9.cloned.1.call-start = ((), (), s32[]{:S(2)}) async-start(), calls=%async_computation.9 | async-start | bytes 5013504 | tf_op jit(solution)/shard_map/reduce_scatter | solution.py:1332
  646.9 546.4 %reduce-scatter.5.cloned.1.call-start = ((), (), s32[]{:S(2)}) async-start(), calls=%async_computation.7 | async-start | bytes 10027008 | tf_op jit(solution)/shard_map/reduce_scatter | solution.py:1332
  721.2 40.8 %collective-permute-start.25 = (bf16[1024,1536]{1,0:T(8,128)(2,1)}, bf16[1024,1536]{1,0:T(8,128)(2,1)}, u32[]{:S(2)}, u32[]{:S(2)}) collective-permute-start(bf16[1024,1536]{1,0:T(8,128)(2,1)} %add_convert_fusion.2), channel_id=1, source_target_pairs={{0,1},{1,0},{2,3},{3,2},{4,5},{5,4},{6,7},{7,6},{8,9},{9,8},{10,11... | collective-permute-start | bytes 9437192 | tf_op jit(solution)/shard_map/ppermute | solution.py:1106
  746.3 619.8 %reduce-scatter.7.cloned.1.call-start = ((), (), s32[]{:S(2)}) async-start(), calls=%async_computation.8 | async-start | bytes 10027008 | tf_op jit(solution)/shard_map/reduce_scatter | solution.py:1332
  795.5 6.1 collective-permute-start.26
  837.8 28.8 %collective-permute-start.27 = (bf16[1024,1536]{1,0:T(8,128)(2,1)}, bf16[1024,1536]{1,0:T(8,128)(2,1)}, u32[]{:S(2)}, u32[]{:S(2)}) collective-permute-start(bf16[1024,1536]{1,0:T(8,128)(2,1)} %convolution_convert_fusion.4), channel_id=1, source_target_pairs={{0,1},{1,0},{2,3},{3,2},{4,5},{5,4},{6,7},{7,6},{8,9},{9,8},{10,11... | collective-permute-start | bytes 9437192 | tf_op jit(solution)/shard_map/ppermute | solution.py:1106
  866.3 51.1 %collective-permute-start.30 = (bf16[768,768]{1,0:T(8,128)(2,1)}, bf16[768,768]{1,0:T(8,128)(2,1)}, u32[]{:S(2)}, u32[]{:S(2)}) collective-permute-start(bf16[768,768]{1,0:T(8,128)(2,1)} %get-tuple-element.274), channel_id=1, source_target_pairs={{0,1},{1,0},{2,3},{3,2},{4,5},{5,4},{6,7},{7,6},{8,9},{9,8},{10,11... | collective-permute-start | bytes 3538952 | tf_op jit(solution)/shard_map/ppermute | solution.py:1106
  879.5 44.7 %collective-permute-start.28 = (bf16[1024,1536]{1,0:T(8,128)(2,1)}, bf16[1024,1536]{1,0:T(8,128)(2,1)}, u32[]{:S(2)}, u32[]{:S(2)}) collective-permute-start(bf16[1024,1536]{1,0:T(8,128)(2,1)} %get-tuple-element.256), channel_id=1, source_target_pairs={{0,1},{1,0},{2,3},{3,2},{4,5},{5,4},{6,7},{7,6},{8,9},{9,8},{10,11... | collective-permute-start | bytes 9437192 | tf_op jit(solution)/shard_map/ppermute | solution.py:1106
  909.7 124.8 %collective-permute-start.31 = (bf16[384,1536]{1,0:T(8,128)(2,1)}, bf16[384,1536]{1,0:T(8,128)(2,1)}, u32[]{:S(2)}, u32[]{:S(2)}) collective-permute-start(bf16[384,1536]{1,0:T(8,128)(2,1)} %convolution_convert_fusion.7.refs_14_), channel_id=1, source_target_pairs={{0,8},{8,0},{16,24},{24,16},{1,9},{9,1},{17,25},{25,17},{2,10},{10... | collective-permute-start | bytes 3538952 | tf_op jit(solution)/shard_map/ppermute | solution.py:1109
  916.8 110.1 %collective-permute-start.32 = (bf16[768,768]{1,0:T(8,128)(2,1)}, bf16[768,768]{1,0:T(8,128)(2,1)S(1)}, u32[]{:S(2)}, u32[]{:S(2)}) collective-permute-start(bf16[768,768]{1,0:T(8,128)(2,1)} %fusion.97.refs_15_), channel_id=1, source_target_pairs={{0,8},{8,0},{16,24},{24,16},{1,9},{9,1},{17,25},{25,17},{2,10},{10... | collective-permute-start | bytes 3538952 | tf_op jit(solution)/shard_map/ppermute | solution.py:1109
  933.1 11.5 collective-permute-start.29
  947.4 119.4 %collective-permute-start.33 = (bf16[768,1536]{1,0:T(8,128)(2,1)}, bf16[768,1536]{1,0:T(8,128)(2,1)}, u32[]{:S(2)}, u32[]{:S(2)}) collective-permute-start(bf16[768,1536]{1,0:T(8,128)(2,1)} %fusion.71.refs_16_), channel_id=1, source_target_pairs={{0,16},{8,24},{16,0},{24,8},{1,17},{9,25},{17,1},{25,9},{2,18},{10... | collective-permute-start | bytes 7077896 | tf_op jit(solution)/shard_map/ppermute | solution.py:1109
  1033.7 150.4 %collective-permute-start.38 = (bf16[384,768]{1,0:T(8,128)(2,1)}, bf16[384,768]{1,0:T(8,128)(2,1)}, u32[]{:S(2)}, u32[]{:S(2)}) collective-permute-start(bf16[384,768]{1,0:T(8,128)(2,1)} %constant_dynamic-slice_fusion.7.refs_15_), channel_id=1, source_target_pairs={{0,16},{8,24},{16,0},{24,8},{1,17},{9,25},{17,1},{25,9},{2,18},{10... | collective-permute-start | bytes 1769480 | tf_op jit(solution)/shard_map/ppermute | solution.py:1109
  1037.4 144.6 %collective-permute-start.37 = (bf16[192,1536]{1,0:T(8,128)(2,1)}, bf16[192,1536]{1,0:T(8,128)(2,1)}, u32[]{:S(2)}, u32[]{:S(2)}) collective-permute-start(bf16[192,1536]{1,0:T(8,128)(2,1)} %constant_dynamic-slice_fusion.8.refs_14_), channel_id=1, source_target_pairs={{0,16},{8,24},{16,0},{24,8},{1,17},{9,25},{17,1},{25,9},{2,18},{10... | collective-permute-start | bytes 1769480 | tf_op jit(solution)/shard_map/ppermute | solution.py:1109
  1071.7 118.5 %collective-permute-start.39 = (bf16[384,1536]{1,0:T(8,128)(2,1)}, bf16[384,1536]{1,0:T(8,128)(2,1)}, u32[]{:S(2)}, u32[]{:S(2)}) collective-permute-start(bf16[384,1536]{1,0:T(8,128)(2,1)} %constant_dynamic-slice_fusion.6.refs_16_), channel_id=1, source_target_pairs={{0,8},{8,0},{16,24},{24,16},{1,9},{9,1},{17,25},{25,17},{2,10},{10... | collective-permute-start | bytes 3538952 | tf_op jit(solution)/shard_map/ppermute | solution.py:1109
  1156.0 30.2 %collective-permute-start.35 = (f32[1,1536]{1,0:T(1,128)S(1)}, f32[1,1536]{1,0:T(1,128)}, u32[]{:S(2)}, u32[]{:S(2)}) collective-permute-start(f32[1,1536]{1,0:T(1,128)S(1)} %copy.294), channel_id=1, source_target_pairs={{0,1},{1,0},{2,3},{3,2},{4,5},{5,4},{6,7},{7,6},{8,9},{9,8},{10,11... | collective-permute-start | bytes 18440 | tf_op jit(solution)/shard_map/ppermute | solution.py:1106
  1169.6 24.9 %collective-permute-start.34 = (bf16[1024,1536]{1,0:T(8,128)(2,1)}, bf16[1024,1536]{1,0:T(8,128)(2,1)}, u32[]{:S(2)}, u32[]{:S(2)}) collective-permute-start(bf16[1024,1536]{1,0:T(8,128)(2,1)} %add_convert_fusion.1), channel_id=1, source_target_pairs={{0,1},{1,0},{2,3},{3,2},{4,5},{5,4},{6,7},{7,6},{8,9},{9,8},{10,11... | collective-permute-start | bytes 9437192 | tf_op jit(solution)/shard_map/ppermute | solution.py:1106
  1213.7 8.6 collective-permute-start.36
  1362.0 20.4 %collective-permute-start.42 = (f32[1,1536]{1,0:T(1,128)S(1)}, f32[1,1536]{1,0:T(1,128)S(1)}, u32[]{:S(2)}, u32[]{:S(2)}) collective-permute-start(f32[1,1536]{1,0:T(1,128)S(1)} %copy.301), channel_id=1, source_target_pairs={{0,24},{8,16},{16,8},{24,0},{1,25},{9,17},{17,9},{25,1},{2,26},{10... | collective-permute-start | bytes 18440 | tf_op jit(solution)/shard_map/ppermute | solution.py:1109
  1363.4 19.0 %collective-permute-start.41 = (f32[1,1536]{1,0:T(1,128)S(1)}, f32[1,1536]{1,0:T(1,128)S(1)}, u32[]{:S(2)}, u32[]{:S(2)}) collective-permute-start(f32[1,1536]{1,0:T(1,128)S(1)} %copy.301), channel_id=1, source_target_pairs={{0,16},{8,24},{16,0},{24,8},{1,17},{9,25},{17,1},{25,9},{2,18},{10... | collective-permute-start | bytes 18440 | tf_op jit(solution)/shard_map/ppermute | solution.py:1109
  1364.6 17.8 %collective-permute-start.40 = (f32[1,1536]{1,0:T(1,128)S(1)}, f32[1,1536]{1,0:T(1,128)S(1)}, u32[]{:S(2)}, u32[]{:S(2)}) collective-permute-start(f32[1,1536]{1,0:T(1,128)S(1)} %copy.301), channel_id=1, source_target_pairs={{0,8},{8,0},{16,24},{24,16},{1,9},{9,1},{17,25},{25,17},{2,10},{10... | collective-permute-start | bytes 18440 | tf_op jit(solution)/shard_map/ppermute | solution.py:1109
  1374.1 10.7 collective-permute-start.51
  1374.3 42.2 %collective-permute-start.54 = (bf16[24,1536]{1,0:T(8,128)(2,1)S(1)}, bf16[24,1536]{1,0:T(8,128)(2,1)S(1)}, u32[]{:S(2)}, u32[]{:S(2)}) collective-permute-start(bf16[24,1536]{1,0:T(8,128)(2,1)S(1)} %dynamic-slice_convert_fusion.4), channel_id=1, source_target_pairs={{0,1},{1,0},{2,3},{3,2},{4,5},{5,4},{6,7},{7,6},{8,9},{9,8},{10,11... | collective-permute-start | bytes 221192 | tf_op jit(solution)/shard_map/ppermute | solution.py:1106
  1382.3 41.1 %collective-permute-start.56 = (bf16[48,3072]{1,0:T(8,128)(2,1)}, bf16[48,3072]{1,0:T(8,128)(2,1)}, u32[]{:S(2)}, u32[]{:S(2)}) collective-permute-start(bf16[48,3072]{1,0:T(8,128)(2,1)} %dynamic-slice_convert_fusion), channel_id=1, source_target_pairs={{0,1},{1,0},{2,3},{3,2},{4,5},{5,4},{6,7},{7,6},{8,9},{9,8},{10,11... | collective-permute-start | bytes 884744 | tf_op jit(solution)/shard_map/ppermute | solution.py:1106
  1382.5 5.8 collective-permute-start.45
  1388.2 29.7 %collective-permute-start.53 = (bf16[48,2304]{1,0:T(8,128)(2,1)}, bf16[48,2304]{1,0:T(8,128)(2,1)S(1)}, u32[]{:S(2)}, u32[]{:S(2)}) collective-permute-start(bf16[48,2304]{1,0:T(8,128)(2,1)} %dynamic-slice_convert_fusion.2), channel_id=1, source_target_pairs={{0,1},{1,0},{2,3},{3,2},{4,5},{5,4},{6,7},{7,6},{8,9},{9,8},{10,11... | collective-permute-start | bytes 663560 | tf_op jit(solution)/shard_map/ppermute | solution.py:1106
  1389.3 29.1 %collective-permute-start.52 = (bf16[48,2304]{1,0:T(8,128)(2,1)}, bf16[48,2304]{1,0:T(8,128)(2,1)}, u32[]{:S(2)}, u32[]{:S(2)}) collective-permute-start(bf16[48,2304]{1,0:T(8,128)(2,1)} %dynamic-slice_convert_fusion.3), channel_id=1, source_target_pairs={{0,1},{1,0},{2,3},{3,2},{4,5},{5,4},{6,7},{7,6},{8,9},{9,8},{10,11... | collective-permute-start | bytes 663560 | tf_op jit(solution)/shard_map/ppermute | solution.py:1106
  (190 other events, 2018.6 us)
Sparse Core Ops, SparseCore 0:
  20.6 200.1 all-gather.3
  224.2 209.6 all-gather.5
  437.2 120.6 all-gather.7
  631.9 135.9 reduce-scatter.10
  773.7 136.3 reduce-scatter.8
  915.6 196.3 reduce-scatter.4
  1118.7 223.5 reduce-scatter.6
